TPU v7x, 32 devices: a whole 2x2x4 slice. The times are simulated.
32 devices in a mesh: dp: 8 (over y, x, core), mp: 4 (over z).
Axes of the slice: x: 2, y: 2, z: 4, core: 2. Of those that a mesh axis runs over, the one named last changes fastest.
Arguments:
- tokens: bfloat16 [32768, 768], P('dp'), may hold values from -18 to 18, as said below
- cotangent: bfloat16 [32768, 768], P('dp'), may hold values from -20 to 20, as said below
- counts: int32 [8, 32], P('dp'), may hold values from 0 to 128, as said below
- attend_in: float32 [3, 2, 768, 2304], P(None, None, 'dp', 'mp'), as said below
- attend_out: float32 [3, 2, 768, 768], P(None, None, ('mp', 'dp')), as said below
- expand_in: float32 [3, 2, 768, 3072], P(None, None, 'dp', 'mp'), as said below
- expand_bias: float32 [3, 2, 3072], P(None, None, ('mp', 'dp')), as said below
- expand_out: float32 [3, 2, 3072, 768], P(None, None, ('mp', 'dp')), as said below
- affine_state: float32 [3, 2, 6, 768], P(None, None, None, 'dp'), as said below
- position_state: float32 [3, 32, 768], P(None, None, 'dp'), as said below
Outputs:
- out_tokens: bfloat16 [32768, 768], P('dp')
- input_grad: float32 [32768, 768], P('dp')
- grad_norm: float32 [], replicated
- new_attend_in: float32 [2, 768, 2304], P(None, 'dp', 'mp')
- new_attend_out: float32 [2, 768, 768], P(None, ('mp', 'dp'))
- new_expand_in: float32 [2, 768, 3072], P(None, 'dp', 'mp')
- new_expand_bias: float32 [2, 3072], P(None, ('mp', 'dp'))
- new_expand_out: float32 [2, 3072, 768], P(None, ('mp', 'dp'))
- new_affine_state: float32 [2, 6, 768], P(None, None, 'dp')
- new_position_state: float32 [32, 768], P(None, 'dp')
- first_attend_in: float32 [2, 768, 2304], P(None, 'dp', 'mp')
- first_attend_out: float32 [2, 768, 768], P(None, ('mp', 'dp'))
- first_expand_in: float32 [2, 768, 3072], P(None, 'dp', 'mp')
- first_expand_bias: float32 [2, 3072], P(None, ('mp', 'dp'))
- first_expand_out: float32 [2, 3072, 768], P(None, ('mp', 'dp'))
- first_affine_state: float32 [2, 6, 768], P(None, None, 'dp')
- first_position_state: float32 [32, 768], P(None, 'dp')
- second_attend_in: float32 [2, 768, 2304], P(None, 'dp', 'mp')
- second_attend_out: float32 [2, 768, 768], P(None, ('mp', 'dp'))
- second_expand_in: float32 [2, 768, 3072], P(None, 'dp', 'mp')
- second_expand_bias: float32 [2, 3072], P(None, ('mp', 'dp'))
- second_expand_out: float32 [2, 3072, 768], P(None, ('mp', 'dp'))
- second_affine_state: float32 [2, 6, 768], P(None, None, 'dp')
- second_position_state: float32 [32, 768], P(None, 'dp')
Inputs may be any that keep to these rules, and one draw needn't show every extreme that they name: counts[d, s] = min(128, max(0, L - 128 * s)) for a document length L of 512 tokens or more; in every draw some document is full and some has an empty last segment. `tokens`: real values. `cotangent`: real values. `attend_in`: along the first dimension: master weight, first moment, second moment; second moments are positive. `attend_out`: along the first dimension: master weight, first moment, second moment; second moments are positive. `expand_in`: along the first dimension: master weight, first moment, second moment; second moments are positive. `expand_bias`: along the first dimension: master weight, first moment, second moment; second moments are positive. `expand_out`: along the first dimension: master weight, first moment, second moment; second moments are positive. `affine_state`: along the first dimension: master, first moment, second moment; second moments are positive. `position_state`: along the first dimension: master, first moment, second moment; second moments are positive.
All inputs are finite; a program needn't handle non-finite values.
Results may differ from a plain program's by a relative error of at most 0.024.
Values may be sent and summed in bfloat16 or wider, within the bound.
No kernel may reach another device: no remote copies, remote signals or barrier semaphores. Data moves between devices by JAX's collectives and lax.ppermute only.
A program may use at most 320 MiB of HBM per device.

v0:
```python
import jax
import jax.numpy as jnp
from jax import lax
from jax.sharding import PartitionSpec as P

HEAD_DIM = 64
SEG = 128
NSEG = 32


norm_eps = 1e-05
clip_level = 1.0
rate = 0.02
decay = 0.01
beta_one = 0.9
beta_two = 0.999
adam_eps = 1e-08
adam_step = 10


def layer_norm(values, gain, shift):
    mean = jnp.mean(values, axis=-1, keepdims=True)
    centred = values - mean
    spread = jnp.mean(centred * centred, axis=-1, keepdims=True)
    return centred * lax.rsqrt(spread + norm_eps) * gain + shift


def matmul(left, right):
    return jnp.dot(left, right, preferred_element_type=jnp.float32)


def matmul_tn(left, right):
    return lax.dot_general(
        left, right, (((0,), (0,)), ((), ())), preferred_element_type=jnp.float32
    )


def matmul_nt(left, right):
    return lax.dot_general(
        left, right, (((1,), (1,)), ((), ())), preferred_element_type=jnp.float32
    )


def split_heads(triple, span):
    rows = triple.shape[0]
    heads = triple.shape[1] // (3 * HEAD_DIM)
    parts = triple.reshape(rows // span, span, heads, 3, HEAD_DIM)
    return (parts[:, :, :, 0], parts[:, :, :, 1], parts[:, :, :, 2])


def scores_of(query, key, keep, span):
    raw = jnp.einsum(
        "bqhe,bkhe->bhqk", query, key, preferred_element_type=jnp.float32
    ) * HEAD_DIM ** (-0.5)
    live = keep.reshape(-1, 1, 1, span) > 0.5
    return jnp.where(live, raw, -1e30)


def attend(triple, keep, span):
    query, key, value = split_heads(triple, span)
    scores = scores_of(query, key, keep, span)
    top = jnp.max(scores, axis=-1, keepdims=True)
    weights = jnp.exp(scores - top)
    total = jnp.sum(weights, axis=-1, keepdims=True)
    probs = (weights / total).astype(jnp.bfloat16)
    context = jnp.einsum("bhqk,bkhe->bqhe", probs, value, preferred_element_type=jnp.float32)
    return (context.reshape(triple.shape[0], -1).astype(jnp.bfloat16), top, total)


def attend_back(triple, keep, span, top, total, grad_context):
    query, key, value = split_heads(triple, span)
    scores = scores_of(query, key, keep, span)
    probs = jnp.exp(scores - top) / total
    grad_ctx = grad_context.reshape(query.shape)
    grad_probs = jnp.einsum("bqhe,bkhe->bhqk", grad_ctx, value, preferred_element_type=jnp.float32)
    inner = jnp.sum(probs * grad_probs, axis=-1, keepdims=True)
    grad_scores = (probs * (grad_probs - inner)).astype(jnp.bfloat16)
    scale = HEAD_DIM ** (-0.5)
    grad_query = (
        jnp.einsum("bhqk,bkhe->bqhe", grad_scores, key, preferred_element_type=jnp.float32) * scale
    )
    grad_key = (
        jnp.einsum("bhqk,bqhe->bkhe", grad_scores, query, preferred_element_type=jnp.float32)
        * scale
    )
    grad_value = jnp.einsum(
        "bhqk,bqhe->bkhe", probs.astype(jnp.bfloat16), grad_ctx, preferred_element_type=jnp.float32
    )
    stacked = jnp.stack([grad_query, grad_key, grad_value], axis=3)
    return stacked.reshape(triple.shape).astype(jnp.bfloat16)


def forward(inputs, keep, span, weights):
    w_in, w_out, w_up, b_up, w_down, affine = weights
    affine = affine.astype(jnp.float32)
    unit = inputs.astype(jnp.bfloat16)
    triple = matmul(unit, w_in).astype(jnp.bfloat16)
    context, top, total = attend(triple, keep, span)
    mixed = lax.psum(matmul(context, w_out).astype(jnp.bfloat16), "mp").astype(jnp.float32)
    resid = inputs + mixed + affine[4]
    hidden = layer_norm(resid, affine[0], affine[1])
    hid_low = hidden.astype(jnp.bfloat16)
    expanded = matmul(hid_low, w_up) + b_up.astype(jnp.float32)
    activated = jax.nn.gelu(expanded).astype(jnp.bfloat16)
    returned = lax.psum(matmul(activated, w_down).astype(jnp.bfloat16), "mp").astype(jnp.float32)
    resid_two = hidden + returned + affine[5]
    output = layer_norm(resid_two, affine[2], affine[3])
    cache = (unit, triple, top, total, context, resid, hid_low, expanded, activated, resid_two)
    return (output, cache)


def backward(grad_out, cache, keep, span, weights):
    w_in, w_out, w_up, b_up, w_down, affine = weights
    affine = affine.astype(jnp.float32)
    unit, triple, top, total, context, resid, hid_low, expanded, activated, resid_two = cache
    pull_two = jax.vjp(layer_norm, resid_two, affine[2], affine[3])[1]
    grad_resid_two, grad_gain_two, grad_shift_two = pull_two(grad_out)
    grad_returned = grad_resid_two.astype(jnp.bfloat16)
    grad_down = matmul_tn(activated, grad_returned)
    grad_act = matmul_nt(grad_returned, w_down)
    pull_act = jax.vjp(jax.nn.gelu, expanded)[1]
    grad_expanded = pull_act(grad_act)[0]
    grad_exp_low = grad_expanded.astype(jnp.bfloat16)
    grad_up = matmul_tn(hid_low, grad_exp_low)
    grad_hidden = grad_resid_two + lax.psum(
        matmul_nt(grad_exp_low, w_up).astype(jnp.bfloat16), "mp"
    ).astype(jnp.float32)
    pull_one = jax.vjp(layer_norm, resid, affine[0], affine[1])[1]
    grad_resid, grad_gain_one, grad_shift_one = pull_one(grad_hidden)
    grad_mixed = grad_resid.astype(jnp.bfloat16)
    grad_wout = matmul_tn(context, grad_mixed)
    grad_context = matmul_nt(grad_mixed, w_out).astype(jnp.bfloat16)
    grad_triple = attend_back(triple, keep, span, top, total, grad_context)
    grad_win = matmul_tn(unit, grad_triple)
    grad_inputs = grad_resid + lax.psum(
        matmul_nt(grad_triple, w_in).astype(jnp.bfloat16), "mp"
    ).astype(jnp.float32)
    grad_affine = jnp.stack(
        [
            grad_gain_one,
            grad_shift_one,
            grad_gain_two,
            grad_shift_two,
            jnp.sum(grad_resid, axis=0),
            jnp.sum(grad_resid_two, axis=0),
        ]
    )
    return (
        grad_inputs,
        (grad_win, grad_wout, grad_up, jnp.sum(grad_expanded, axis=0), grad_down, grad_affine),
    )


def adam(state, grad, factor):
    clipped = grad * factor
    first = beta_one * state[1] + (1.0 - beta_one) * clipped
    second = beta_two * state[2] + (1.0 - beta_two) * clipped * clipped
    fixed_first = first / (1.0 - beta_one**adam_step)
    fixed_second = second / (1.0 - beta_two**adam_step)
    master = state[0] - rate * (
        fixed_first / (jnp.sqrt(fixed_second) + adam_eps) + decay * state[0]
    )
    return (master, first, second)


def shards(
    tokens,
    cotangent,
    counts,
    attend_in,
    attend_out,
    expand_in,
    expand_bias,
    expand_out,
    affine_state,
    position_state,
):
    working = (
        lax.all_gather(attend_in[0].astype(jnp.bfloat16), "dp", axis=1, tiled=True),
        lax.all_gather(attend_out[0].astype(jnp.bfloat16), "dp", axis=1, tiled=True),
        lax.all_gather(expand_in[0].astype(jnp.bfloat16), "dp", axis=1, tiled=True),
        lax.all_gather(expand_bias[0].astype(jnp.bfloat16), "dp", axis=1, tiled=True),
        lax.all_gather(expand_out[0].astype(jnp.bfloat16), "dp", axis=1, tiled=True),
        lax.all_gather(affine_state[0].astype(jnp.bfloat16), "dp", axis=2, tiled=True),
        lax.all_gather(position_state[0].astype(jnp.bfloat16), "dp", axis=1, tiled=True),
    )
    layer_one = tuple((member[0] for member in working[:6]))
    layer_two = tuple((member[1] for member in working[:6]))
    position = working[6].astype(jnp.float32)
    docs_here = counts.shape[0]
    spot = lax.broadcasted_iota(jnp.int32, (docs_here, NSEG, SEG), 2)
    keep_tokens = (spot < counts[:, :, None]).astype(jnp.float32).reshape(-1)
    keep_heads = (counts > 0).astype(jnp.float32).reshape(-1)
    inputs = tokens.astype(jnp.float32)
    first, cache_one = forward(inputs, keep_tokens, SEG, layer_one)
    grid = first.reshape(docs_here, NSEG, SEG, -1)
    heads_in = (grid[:, :, 0] + position[None]).reshape(docs_here * NSEG, -1)
    second, cache_two = forward(heads_in, keep_heads, NSEG, layer_two)
    merged = (
        grid.at[:, :, 0].set(second.reshape(docs_here, NSEG, -1)).reshape(first.shape)
        * keep_tokens[:, None]
    )
    grad_out = cotangent.astype(jnp.float32) * keep_tokens[:, None]
    grad_grid = grad_out.reshape(docs_here, NSEG, SEG, -1)
    grad_heads, grads_two = backward(
        grad_grid[:, :, 0].reshape(docs_here * NSEG, -1), cache_two, keep_heads, NSEG, layer_two
    )
    grad_position = jnp.sum(grad_heads.reshape(docs_here, NSEG, -1), axis=0)
    grad_first = (
        grad_grid.at[:, :, 0].set(grad_heads.reshape(docs_here, NSEG, -1)).reshape(grad_out.shape)
    )
    again_inputs = lax.optimization_barrier((inputs, grad_first))[0]
    cache_one = forward(again_inputs, keep_tokens, SEG, layer_one)[1]
    grad_inputs, grads_one = backward(grad_first, cache_one, keep_tokens, SEG, layer_one)
    shares = (
        lax.psum_scatter(
            jnp.stack([grads_one[0], grads_two[0]]).astype(jnp.bfloat16),
            "dp",
            scatter_dimension=1,
            tiled=True,
        ).astype(jnp.float32),
        lax.psum_scatter(
            jnp.stack([grads_one[1], grads_two[1]]).astype(jnp.bfloat16),
            "dp",
            scatter_dimension=1,
            tiled=True,
        ).astype(jnp.float32),
        lax.psum_scatter(
            jnp.stack([grads_one[2], grads_two[2]]).astype(jnp.bfloat16),
            "dp",
            scatter_dimension=1,
            tiled=True,
        ).astype(jnp.float32),
        lax.psum_scatter(
            jnp.stack([grads_one[3], grads_two[3]]).astype(jnp.bfloat16),
            "dp",
            scatter_dimension=1,
            tiled=True,
        ).astype(jnp.float32),
        lax.psum_scatter(
            jnp.stack([grads_one[4], grads_two[4]]).astype(jnp.bfloat16),
            "dp",
            scatter_dimension=1,
            tiled=True,
        ).astype(jnp.float32),
        lax.psum_scatter(
            jnp.stack([grads_one[5], grads_two[5]]).astype(jnp.bfloat16),
            "dp",
            scatter_dimension=2,
            tiled=True,
        ).astype(jnp.float32),
        lax.psum_scatter(
            grad_position.astype(jnp.bfloat16), "dp", scatter_dimension=1, tiled=True
        ).astype(jnp.float32),
    )
    matrix_squares = jnp.sum(shares[0] * shares[0])
    for member in shares[1:5]:
        matrix_squares = matrix_squares + jnp.sum(member * member)
    small_squares = jnp.sum(shares[5] * shares[5]) + jnp.sum(shares[6] * shares[6])
    leader = (lax.axis_index("mp") == 0).astype(jnp.float32)
    total_squares = lax.psum(matrix_squares + leader * small_squares, ("dp", "mp"))
    grad_norm = jnp.sqrt(total_squares)
    factor = jnp.minimum(1.0, clip_level / grad_norm)
    states = (
        attend_in,
        attend_out,
        expand_in,
        expand_bias,
        expand_out,
        affine_state,
        position_state,
    )
    updated = [adam(state, share, factor) for state, share in zip(states, shares)]
    masters = [item[0] for item in updated]
    firsts = [item[1] for item in updated]
    seconds = [item[2] for item in updated]
    head = [merged.astype(jnp.bfloat16), grad_inputs * keep_tokens[:, None], grad_norm]
    return tuple(head + masters + firsts + seconds)


def solution(mesh):
    in_specs = (
        P("dp", None),
        P("dp", None),
        P("dp", None),
        P(None, None, "dp", "mp"),
        P(None, None, ("mp", "dp"), None),
        P(None, None, "dp", "mp"),
        P(None, None, ("mp", "dp")),
        P(None, None, ("mp", "dp"), None),
        P(None, None, None, "dp"),
        P(None, None, "dp"),
    )
    out_specs = (
        P("dp", None),
        P("dp", None),
        P(),
        P(None, "dp", "mp"),
        P(None, ("mp", "dp"), None),
        P(None, "dp", "mp"),
        P(None, ("mp", "dp")),
        P(None, ("mp", "dp"), None),
        P(None, None, "dp"),
        P(None, "dp"),
        P(None, "dp", "mp"),
        P(None, ("mp", "dp"), None),
        P(None, "dp", "mp"),
        P(None, ("mp", "dp")),
        P(None, ("mp", "dp"), None),
        P(None, None, "dp"),
        P(None, "dp"),
        P(None, "dp", "mp"),
        P(None, ("mp", "dp"), None),
        P(None, "dp", "mp"),
        P(None, ("mp", "dp")),
        P(None, ("mp", "dp"), None),
        P(None, None, "dp"),
        P(None, "dp"),
    )
    return jax.shard_map(shards, mesh=mesh, in_specs=in_specs, out_specs=out_specs, check_vma=False)
```

profile of v0, /device:TPU:0, one launch (start us, length us, event | category | flops | bytes accessed | tf_op | source)
XLA Modules:
  0.0 2037.6 jit_solution(3129820084597151620)
XLA Ops:
  125.2 13.1 slice_reduce_fusion.7
  138.3 390.5 %all-reduce.17.cloned.1.call-done = (bf16[4096,768]{1,0:T(8,128)(2,1)}, bf16[4096,768]{1,0:T(8,128)(2,1)}) async-done(((bf16[4096,768]{1,0:T(8,128)(2,1)}, bf16[4096,768]{1,0:T(8,128)(2,1)}), (bf16[4096,768]{1,0:T(8,128)(2,1)}, bf16[4096,768]{1,0:T(8,128)(2,1)})) %all-reduce.17.cloned.1.call-update) | async-done | bytes 12582928 | tf_op jit(solution)/shard_map/psum | solution.py:99
  569.7 21.0 %all-gather.10.cloned.1.call-done = bf16[2,768,768]{2,1,0:T(8,128)(2,1)} async-done(((bf16[2,96,768]{2,1,0:T(8,128)(2,1)}), bf16[2,768,768]{2,1,0:T(8,128)(2,1)}) %all-gather.10.cloned.1.call-update) | async-done | bytes 2359312 | tf_op jit(solution)/shard_map/all_gather | solution.py:183
  590.7 19.5 convolution_convert_fusion.5
  610.2 12.9 convolution_convert_fusion.4
  642.3 13.3 slice_reduce_fusion.1
  659.3 390.8 %all-reduce.15.cloned.1.call-done = (bf16[4096,768]{1,0:T(8,128)(2,1)}, bf16[4096,768]{1,0:T(8,128)(2,1)}) async-done(((bf16[4096,768]{1,0:T(8,128)(2,1)}, bf16[4096,768]{1,0:T(8,128)(2,1)}), (bf16[4096,768]{1,0:T(8,128)(2,1)}, bf16[4096,768]{1,0:T(8,128)(2,1)})) %all-reduce.15.cloned.1.call-update) | async-done | bytes 12582928 | tf_op jit(solution)/shard_map/psum | solution.py:105
  1050.1 18.5 fusion.217
  1078.7 17.1 psum.79
  1099.3 17.1 psum.80
  1122.0 17.1 psum.81
  1147.9 16.9 psum.82
  1191.4 19.2 fusion.211
  1221.8 17.6 fusion.82
  1255.7 186.6 %all-reduce.9.cloned.1.call-done = bf16[4096,768]{1,0:T(8,128)(2,1)} async-done(((bf16[4096,768]{1,0:T(8,128)(2,1)}), bf16[4096,768]{1,0:T(8,128)(2,1)}) %all-reduce.9.cloned.1.call-update) | async-done | bytes 6291472 | tf_op jit(solution)/shard_map/psum | solution.py:125
  1442.2 12.7 multiply_reduce_fusion.1
  1521.0 40.7 %reduce-scatter.17.cloned.1.call-done = bf16[2,96,768]{2,1,0:T(8,128)(2,1)} async-done(((bf16[2,768,768]{2,1,0:T(8,128)(2,1)}), bf16[2,96,768]{2,1,0:T(8,128)(2,1)}) %reduce-scatter.17.cloned.1.call-update) | async-done | bytes 294928 | tf_op jit(solution)/shard_map/reduce_scatter | solution.py:240
  1563.4 44.4 %reduce-scatter.15.cloned.1.call-done = bf16[2,96,768]{2,1,0:T(8,128)(2,1)} async-done(((bf16[2,768,768]{2,1,0:T(8,128)(2,1)}), bf16[2,96,768]{2,1,0:T(8,128)(2,1)}) %reduce-scatter.15.cloned.1.call-update) | async-done | bytes 294928 | tf_op jit(solution)/shard_map/reduce_scatter | solution.py:228
  1626.2 19.7 reduce-scatter.19.cloned.1.call-done
  1648.1 223.5 %all-reduce.11.cloned.1.call-done = bf16[4096,768]{1,0:T(8,128)(2,1)} async-done(((bf16[4096,768]{1,0:T(8,128)(2,1)}), bf16[4096,768]{1,0:T(8,128)(2,1)}) %all-reduce.11.cloned.1.call-update) | async-done | bytes 6291472 | tf_op jit(solution)/shard_map/psum | solution.py:135
  1871.5 18.6 add_reduce_fusion
  1897.2 37.4 %all-reduce.13.cloned.1.call-done = bf16[2,768,576]{2,0,1:T(2,128)(2,1)} async-done(((bf16[2,768,576]{2,0,1:T(2,128)(2,1)}), bf16[2,768,576]{2,0,1:T(2,128)(2,1)}) %all-reduce.13.cloned.1.call-update) | async-done | bytes 1769488
  1939.9 30.9 %reduce-scatter.23.cloned.1.call-done = bf16[96,12]{1,0:T(8,128)(2,1)} async-done(((bf16[768,12]{1,0:T(8,128)(2,1)}), bf16[96,12]{1,0:T(8,128)(2,1)}) %reduce-scatter.23.cloned.1.call-update) | async-done | bytes 2320
  1975.1 39.5 %psum.87 = f32[]{:T(128)} all-reduce(f32[]{:T(128)S(6)} %add.468), channel_id=1, replica_groups=mesh['dp'=8,'mp'=4] {'dp','mp'}, use_global_device_ids=true, to_apply=%region_66.67 | all-reduce | flops 1 | bytes 8 | tf_op jit(solution)/shard_map/psum | solution.py:261
  (334 shorter events, 376.7 us)
Async XLA Ops:
  7.2 34.7 %all-gather.6.cloned.1.call-start = ((), (), s32[]{:S(2)}) async-start(), calls=%async_computation.6 | async-start | bytes 2211840 | tf_op jit(solution)/shard_map/all_gather | solution.py:179
  11.5 21.4 %copy-start.48 = (s32[1,32]{1,0:T(1,128)S(1)}, s32[1,32]{1,0:T(1,128)}, u32[]{:S(2)}) copy-start(s32[1,32]{1,0:T(1,128)} %param.16) | copy-start | bytes 388
  11.5 517.3 %all-reduce.17.cloned.1.call-start = ((), (), s32[]{:S(2)}) async-start(), calls=%async_computation.19 | async-start | bytes 25165824 | tf_op jit(solution)/shard_map/psum | solution.py:99
  101.9 457.4 %all-gather.8.cloned.1.call-start = ((), (), s32[]{:S(2)}) async-start(), calls=%async_computation.7 | async-start | bytes 2654208 | tf_op jit(solution)/shard_map/all_gather | solution.py:181
  103.8 486.9 %all-gather.10.cloned.1.call-start = ((), (), s32[]{:S(2)}) async-start(), calls=%async_computation.8 | async-start | bytes 2654208 | tf_op jit(solution)/shard_map/all_gather | solution.py:183
  105.6 944.5 %all-reduce.15.cloned.1.call-start = ((), (), s32[]{:S(2)}) async-start(), calls=%async_computation.18 | async-start | bytes 25165824 | tf_op jit(solution)/shard_map/psum | solution.py:105
  623.1 819.1 %all-reduce.9.cloned.1.call-start = ((), (), s32[]{:S(2)}) async-start(), calls=%async_computation.9 | async-start | bytes 12582912 | tf_op jit(solution)/shard_map/psum | solution.py:125
  1191.4 19.2 copy-start.50
  1220.4 297.7 %reduce-scatter.21.cloned.1.call-start = ((), (), s32[]{:S(2)}) async-start(), calls=%async_computation.14 | async-start | bytes 221184
  1239.3 280.2 %reduce-scatter.25.cloned.1.call-start = ((), (), s32[]{:S(2)}) async-start(), calls=%async_computation.16 | async-start | bytes 221184
  1240.8 320.9 %reduce-scatter.17.cloned.1.call-start = ((), (), s32[]{:S(2)}) async-start(), calls=%async_computation.12 | async-start | bytes 2654208 | tf_op jit(solution)/shard_map/reduce_scatter | solution.py:240
  1243.7 364.0 %reduce-scatter.15.cloned.1.call-start = ((), (), s32[]{:S(2)}) async-start(), calls=%async_computation.11 | async-start | bytes 2654208 | tf_op jit(solution)/shard_map/reduce_scatter | solution.py:228
  1255.4 199.5 %copy-start.35 = (f32[4096]{0:T(1024)S(1)}, f32[4096]{0:T(1024)}, u32[]{:S(2)}) copy-start(f32[4096]{0:T(1024)} %copy-done.34) | copy-start | bytes 49156
  1255.5 390.4 %reduce-scatter.19.cloned.1.call-start = ((), (), s32[]{:S(2)}) async-start(), calls=%async_computation.13 | async-start | bytes 663552
  1488.0 383.6 %all-reduce.11.cloned.1.call-start = ((), (), s32[]{:S(2)}) async-start(), calls=%async_computation.10 | async-start | bytes 12582912 | tf_op jit(solution)/shard_map/psum | solution.py:135
  1506.0 428.6 %all-reduce.13.cloned.1.call-start = ((), (), s32[]{:S(2)}) async-start(), calls=%async_computation.17 | async-start | bytes 3932160
  1518.9 92.3 %copy-start.47 = (bf16[2,96]{1,0:T(2,128)(2,1)}, bf16[2,96]{1,0:T(2,128)(2,1)S(1)}, u32[]{:S(2)}) copy-start(bf16[2,96]{1,0:T(2,128)(2,1)S(1)} %copy.261) | copy-start | bytes 1156
  1621.4 250.1 %copy-start.37 = (f32[4096]{0:T(1024)S(1)}, f32[4096]{0:T(1024)}, u32[]{:S(2)}) copy-start(f32[4096]{0:T(1024)} %copy-done.36) | copy-start | bytes 49156
  1626.2 344.7 %reduce-scatter.23.cloned.1.call-start = ((), (), s32[]{:S(2)}) async-start(), calls=%async_computation.15 | async-start | bytes 221184
  1648.0 373.4 %copy-start.15 = (f32[1,2,96,576]{3,2,1,0:T(8,128)S(1)}, f32[1,2,96,576]{3,2,1,0:T(8,128)}, u32[]{:S(2)}) copy-start(f32[1,2,96,576]{3,2,1,0:T(8,128)} %copy-done.14) | copy-start | bytes 1327108
  1648.0 373.4 %copy-start.18 = (f32[1,2,96,576]{3,2,1,0:T(8,128)S(1)}, f32[1,2,96,576]{3,2,1,0:T(8,128)}, u32[]{:S(2)}) copy-start(f32[1,2,96,576]{3,2,1,0:T(8,128)} %get-tuple-element.253) | copy-start | bytes 1327108
  1648.1 373.4 %copy-start.19 = (f32[1,2,96,576]{3,2,1,0:T(8,128)S(1)}, f32[1,2,96,576]{3,2,1,0:T(8,128)}, u32[]{:S(2)}) copy-start(f32[1,2,96,576]{3,2,1,0:T(8,128)} %get-tuple-element.254) | copy-start | bytes 1327108
  1890.1 136.6 %copy-start.16 = (f32[3,2,96,768]{3,2,1,0:T(8,128)S(1)}, f32[3,2,96,768]{3,2,1,0:T(8,128)}, u32[]{:S(2)}) copy-start(f32[3,2,96,768]{3,2,1,0:T(8,128)} %param.21) | copy-start | bytes 5308420
  1890.1 136.6 %copy-start.24 = (bf16[2,96,768]{2,1,0:T(8,128)(2,1)S(1)}, bf16[2,96,768]{2,1,0:T(8,128)(2,1)}, u32[]{:S(2)}) copy-start(bf16[2,96,768]{2,1,0:T(8,128)(2,1)} %reduce-scatter.17.cloned.1.call-done) | copy-start | bytes 884740
  (48 other events, 251.0 us)
Sparse Core Ops, SparseCore 0:
  11.6 30.2 all-gather.5
  102.0 426.8 all-reduce.16
  531.3 27.9 all-gather.7
  561.7 29.0 all-gather.9
  623.3 426.8 all-reduce.14
  1220.5 221.6 all-reduce.8
  1445.8 32.4 reduce-scatter.20
  1482.2 33.5 reduce-scatter.24
  1519.1 42.5 reduce-scatter.16
  1565.2 42.4 reduce-scatter.14
  1611.5 34.3 reduce-scatter.18
  1648.7 222.8 all-reduce.10
  1874.8 59.7 all-reduce.12
  1938.1 32.6 reduce-scatter.22
where the time goes:
time: 2040 us
  waiting for transfers between devices  1400 us (69%)
  other arithmetic  180 us (9%)
  matrix products  176 us (9%)
  blocking collectives  146 us (7%)
  local copies, waits for them, and re-layouts  114 us (6%)
  between operations  22.5 us (1%)
    psum x1, waiting for transfers between devices, forward(): lax.psum(matmul(activated, w_down).astype(jnp.bfloat16), 'mp')  391 us
    psum x1, waiting for transfers between devices, forward(): lax.psum(matmul(context, w_out).astype(jnp.bfloat16), 'mp')  391 us
    psum x1, waiting for transfers between devices, backward(): lax.psum(matmul_nt(grad_triple, w_in).astype(jnp.bfloat16), 'mp')  223 us
    psum x1, waiting for transfers between devices, backward(): lax.psum(matmul_nt(grad_exp_low, w_up).astype(jnp.bfloat16), 'mp')  187 us
    unnamed x19, waiting for transfers between devices  88.2 us
    dot_general x11, matrix products, matmul(): return jnp.dot(left, right, preferred_element_type=jnp.float32)  68.4 us
    unnamed x139, local copies, waits for them, and re-layouts  51.1 us
    dot_general x8, matrix products, matmul_nt(): lax.dot_general(left, right, (((1,), (1,)), ((), ())), preferred_element_...  46.3 us
  transfers between devices with their start and end apart: 14, of which 12 were waited for; matrix products, arithmetic and copies ran while one was open for 12% of the time, Pallas kernels for 0%

commit v1 on v0

--- a/solution.py
+++ b/solution.py
@@ -90,26 +90,32 @@
     return stacked.reshape(triple.shape).astype(jnp.bfloat16)
 
 
-def forward(inputs, keep, span, weights):
+def share_sum(value, axis):
+    if axis is None:
+        return value
+    return lax.psum(value.astype(jnp.bfloat16), axis).astype(jnp.float32)
+
+
+def forward(inputs, keep, span, weights, axis):
     w_in, w_out, w_up, b_up, w_down, affine = weights
     affine = affine.astype(jnp.float32)
     unit = inputs.astype(jnp.bfloat16)
     triple = matmul(unit, w_in).astype(jnp.bfloat16)
     context, top, total = attend(triple, keep, span)
-    mixed = lax.psum(matmul(context, w_out).astype(jnp.bfloat16), "mp").astype(jnp.float32)
+    mixed = share_sum(matmul(context, w_out), axis)
     resid = inputs + mixed + affine[4]
     hidden = layer_norm(resid, affine[0], affine[1])
     hid_low = hidden.astype(jnp.bfloat16)
     expanded = matmul(hid_low, w_up) + b_up.astype(jnp.float32)
     activated = jax.nn.gelu(expanded).astype(jnp.bfloat16)
-    returned = lax.psum(matmul(activated, w_down).astype(jnp.bfloat16), "mp").astype(jnp.float32)
+    returned = share_sum(matmul(activated, w_down), axis)
     resid_two = hidden + returned + affine[5]
     output = layer_norm(resid_two, affine[2], affine[3])
     cache = (unit, triple, top, total, context, resid, hid_low, expanded, activated, resid_two)
     return (output, cache)
 
 
-def backward(grad_out, cache, keep, span, weights):
+def backward(grad_out, cache, keep, span, weights, axis):
     w_in, w_out, w_up, b_up, w_down, affine = weights
     affine = affine.astype(jnp.float32)
     unit, triple, top, total, context, resid, hid_low, expanded, activated, resid_two = cache
@@ -122,9 +128,7 @@
     grad_expanded = pull_act(grad_act)[0]
     grad_exp_low = grad_expanded.astype(jnp.bfloat16)
     grad_up = matmul_tn(hid_low, grad_exp_low)
-    grad_hidden = grad_resid_two + lax.psum(
-        matmul_nt(grad_exp_low, w_up).astype(jnp.bfloat16), "mp"
-    ).astype(jnp.float32)
+    grad_hidden = grad_resid_two + share_sum(matmul_nt(grad_exp_low, w_up), axis)
     pull_one = jax.vjp(layer_norm, resid, affine[0], affine[1])[1]
     grad_resid, grad_gain_one, grad_shift_one = pull_one(grad_hidden)
     grad_mixed = grad_resid.astype(jnp.bfloat16)
@@ -132,9 +136,7 @@
     grad_context = matmul_nt(grad_mixed, w_out).astype(jnp.bfloat16)
     grad_triple = attend_back(triple, keep, span, top, total, grad_context)
     grad_win = matmul_tn(unit, grad_triple)
-    grad_inputs = grad_resid + lax.psum(
-        matmul_nt(grad_triple, w_in).astype(jnp.bfloat16), "mp"
-    ).astype(jnp.float32)
+    grad_inputs = grad_resid + share_sum(matmul_nt(grad_triple, w_in), axis)
     grad_affine = jnp.stack(
         [
             grad_gain_one,
@@ -175,84 +177,84 @@
     affine_state,
     position_state,
 ):
-    working = (
-        lax.all_gather(attend_in[0].astype(jnp.bfloat16), "dp", axis=1, tiled=True),
-        lax.all_gather(attend_out[0].astype(jnp.bfloat16), "dp", axis=1, tiled=True),
-        lax.all_gather(expand_in[0].astype(jnp.bfloat16), "dp", axis=1, tiled=True),
-        lax.all_gather(expand_bias[0].astype(jnp.bfloat16), "dp", axis=1, tiled=True),
-        lax.all_gather(expand_out[0].astype(jnp.bfloat16), "dp", axis=1, tiled=True),
-        lax.all_gather(affine_state[0].astype(jnp.bfloat16), "dp", axis=2, tiled=True),
-        lax.all_gather(position_state[0].astype(jnp.bfloat16), "dp", axis=1, tiled=True),
-    )
-    layer_one = tuple((member[0] for member in working[:6]))
-    layer_two = tuple((member[1] for member in working[:6]))
-    position = working[6].astype(jnp.float32)
+    low = jnp.bfloat16
+    groups = lax.axis_size("mp")
+    mine = lax.axis_index("mp")
+
+    def spread(state, layer, axes, dim):
+        value = state[0, layer].astype(low)
+        for axis in axes:
+            value = lax.all_gather(value, axis, axis=dim[axis], tiled=True)
+        return value
+
+    cols = {"dp": 0, "mp": 1}
+    rows = {"dp": 0, "mp": 0}
+    affine = lax.all_gather(affine_state[0].astype(low), "dp", axis=2, tiled=True)
+    position = lax.all_gather(position_state[0].astype(low), "dp", axis=1, tiled=True)
+    position = position.astype(jnp.float32)
+    layers = []
+    for layer, axes in enumerate([("dp", "mp"), ("dp",)]):
+        layers.append(
+            (
+                spread(attend_in, layer, axes, cols),
+                spread(attend_out, layer, axes, rows),
+                spread(expand_in, layer, axes, cols),
+                spread(expand_bias, layer, axes, rows),
+                spread(expand_out, layer, axes, rows),
+                affine[layer],
+            )
+        )
+    layer_one, layer_two = layers
     docs_here = counts.shape[0]
+    segments = docs_here * NSEG
+    here = segments // groups
     spot = lax.broadcasted_iota(jnp.int32, (docs_here, NSEG, SEG), 2)
     keep_tokens = (spot < counts[:, :, None]).astype(jnp.float32).reshape(-1)
     keep_heads = (counts > 0).astype(jnp.float32).reshape(-1)
-    inputs = tokens.astype(jnp.float32)
-    first, cache_one = forward(inputs, keep_tokens, SEG, layer_one)
-    grid = first.reshape(docs_here, NSEG, SEG, -1)
-    heads_in = (grid[:, :, 0] + position[None]).reshape(docs_here * NSEG, -1)
-    second, cache_two = forward(heads_in, keep_heads, NSEG, layer_two)
-    merged = (
-        grid.at[:, :, 0].set(second.reshape(docs_here, NSEG, -1)).reshape(first.shape)
-        * keep_tokens[:, None]
-    )
-    grad_out = cotangent.astype(jnp.float32) * keep_tokens[:, None]
-    grad_grid = grad_out.reshape(docs_here, NSEG, SEG, -1)
-    grad_heads, grads_two = backward(
-        grad_grid[:, :, 0].reshape(docs_here * NSEG, -1), cache_two, keep_heads, NSEG, layer_two
-    )
+
+    def part(value):
+        size = value.shape[0] // groups
+        return lax.dynamic_slice_in_dim(value, mine * size, size)
+
+    keep_part = part(keep_tokens)
+    inputs = part(tokens).astype(jnp.float32)
+    first, cache_one = forward(inputs, keep_part, SEG, layer_one, None)
+    grid = first.reshape(here, SEG, -1)
+    heads = lax.all_gather(grid[:, 0], "mp", axis=0, tiled=True)
+    heads_in = (heads.reshape(docs_here, NSEG, -1) + position[None]).reshape(segments, -1)
+    second, cache_two = forward(heads_in, keep_heads, NSEG, layer_two, "mp")
+    merged = grid.at[:, 0].set(part(second)).reshape(first.shape) * keep_part[:, None]
+    merged = lax.all_gather(merged.astype(low), "mp", axis=0, tiled=True)
+    grad_out = part(cotangent).astype(jnp.float32) * keep_part[:, None]
+    top_grad = cotangent.reshape(segments, SEG, -1)[:, 0].astype(jnp.float32) * keep_heads[:, None]
+    grad_heads, grads_two = backward(top_grad, cache_two, keep_heads, NSEG, layer_two, "mp")
     grad_position = jnp.sum(grad_heads.reshape(docs_here, NSEG, -1), axis=0)
-    grad_first = (
-        grad_grid.at[:, :, 0].set(grad_heads.reshape(docs_here, NSEG, -1)).reshape(grad_out.shape)
-    )
-    again_inputs = lax.optimization_barrier((inputs, grad_first))[0]
-    cache_one = forward(again_inputs, keep_tokens, SEG, layer_one)[1]
-    grad_inputs, grads_one = backward(grad_first, cache_one, keep_tokens, SEG, layer_one)
-    shares = (
-        lax.psum_scatter(
-            jnp.stack([grads_one[0], grads_two[0]]).astype(jnp.bfloat16),
-            "dp",
-            scatter_dimension=1,
-            tiled=True,
-        ).astype(jnp.float32),
-        lax.psum_scatter(
-            jnp.stack([grads_one[1], grads_two[1]]).astype(jnp.bfloat16),
-            "dp",
-            scatter_dimension=1,
-            tiled=True,
-        ).astype(jnp.float32),
-        lax.psum_scatter(
-            jnp.stack([grads_one[2], grads_two[2]]).astype(jnp.bfloat16),
-            "dp",
-            scatter_dimension=1,
-            tiled=True,
-        ).astype(jnp.float32),
-        lax.psum_scatter(
-            jnp.stack([grads_one[3], grads_two[3]]).astype(jnp.bfloat16),
-            "dp",
-            scatter_dimension=1,
-            tiled=True,
-        ).astype(jnp.float32),
-        lax.psum_scatter(
-            jnp.stack([grads_one[4], grads_two[4]]).astype(jnp.bfloat16),
-            "dp",
-            scatter_dimension=1,
-            tiled=True,
-        ).astype(jnp.float32),
-        lax.psum_scatter(
-            jnp.stack([grads_one[5], grads_two[5]]).astype(jnp.bfloat16),
-            "dp",
-            scatter_dimension=2,
-            tiled=True,
-        ).astype(jnp.float32),
-        lax.psum_scatter(
-            grad_position.astype(jnp.bfloat16), "dp", scatter_dimension=1, tiled=True
-        ).astype(jnp.float32),
-    )
+    grad_grid = grad_out.reshape(here, SEG, -1)
+    grad_first = grad_grid.at[:, 0].set(part(grad_heads)).reshape(grad_out.shape)
+    grad_inputs, grads_one = backward(grad_first, cache_one, keep_part, SEG, layer_one, None)
+    grad_inputs = lax.all_gather(
+        (grad_inputs * keep_part[:, None]).astype(low), "mp", axis=0, tiled=True
+    ).astype(jnp.float32)
+
+    def collect(value, axes, dim):
+        value = value.astype(low)
+        for axis in axes:
+            value = lax.psum_scatter(value, axis, scatter_dimension=dim[axis], tiled=True)
+        return value.astype(jnp.float32)
+
+    shares = []
+    for which, dim in enumerate([cols, rows, cols, rows, rows]):
+        shares.append(
+            jnp.stack(
+                [
+                    collect(grads_one[which], ("mp", "dp"), dim),
+                    collect(grads_two[which], ("dp",), dim),
+                ]
+            )
+        )
+    grad_affine = jnp.stack([lax.psum(grads_one[5], "mp"), grads_two[5]])
+    shares.append(collect(grad_affine, ("dp",), {"dp": 2}))
+    shares.append(collect(grad_position, ("dp",), {"dp": 1}))
     matrix_squares = jnp.sum(shares[0] * shares[0])
     for member in shares[1:5]:
         matrix_squares = matrix_squares + jnp.sum(member * member)
@@ -274,7 +276,7 @@
     masters = [item[0] for item in updated]
     firsts = [item[1] for item in updated]
     seconds = [item[2] for item in updated]
-    head = [merged.astype(jnp.bfloat16), grad_inputs * keep_tokens[:, None], grad_norm]
+    head = [merged, grad_inputs, grad_norm]
     return tuple(head + masters + firsts + seconds)
 
 

time: 2040 us -> 1520 us (0.75)
  waiting for transfers between devices: 1400 us -> 901 us
  other arithmetic: 180 us -> 70.8 us
  blocking collectives: 146 us -> 254 us
  matrix products: 176 us -> 147 us
    psum x4 -> x0, waiting for transfers between devices: 1190 us -> none  [the longest x1 391 us: forward(): lax.psum(matmul(activated, w_down).astype(jnp.bfloat16), 'mp')]
    all_gather x3 -> x10, waiting for transfers between devices: 33 us -> 390 us  [the longest x8 162 us: spread(): value = lax.all_gather(value, axis, axis=dim[axis], tiled=True)]
    reduce_scatter x2 -> x10, waiting for transfers between devices: 85.1 us -> 390 us  [collect(): lax.psum_scatter(value, axis, scatter_dimension=dim[axis], tiled=True)]
    all_gather x4 -> x8, blocking collectives: 38.3 us -> 88.6 us  [the longest x5 57.3 us: spread(): value = lax.all_gather(value, axis, axis=dim[axis], tiled=True)]
    unnamed x0 -> x3, blocking collectives: none -> 37.1 us
    reduce_sum x5 -> x2, other arithmetic: 37.4 us -> 2.1 us  [layer_norm(): mean = jnp.mean(values, axis=-1, keepdims=True)]
    unnamed x19 -> x28, waiting for transfers between devices: 88.2 us -> 120 us
    dot_general x11 -> x8, matrix products: 68.4 us -> 41.8 us  [matmul(): return jnp.dot(left, right, preferred_element_type=jnp.float32)]
  transfers between devices with their start and end apart: 14 -> 24, of which waited for: 12 -> 19; matrix products, arithmetic and copies ran while one was open for 12% -> 14% of each run, Pallas kernels for 0% -> 0%
where the time goes in v1:
time: 1520 us; the launch traced here: 1500 us
  waiting for transfers between devices  901 us (59%)
  blocking collectives  254 us (17%)
  matrix products  147 us (10%)
  local copies, waits for them, and re-layouts  107 us (7%)
  other arithmetic  70.8 us (5%)
  between operations  24.5 us (2%)
    reduce_scatter x10, waiting for transfers between devices, collect(): lax.psum_scatter(value, axis, scatter_dimension=dim[axis], tiled=True)  390 us
    all_gather x8, waiting for transfers between devices, spread(): value = lax.all_gather(value, axis, axis=dim[axis], tiled=True)  162 us
    unnamed x28, waiting for transfers between devices  120 us
    all_gather x1, waiting for transfers between devices, shards(): merged = lax.all_gather(merged.astype(low), 'mp', axis=0, tiled=True)  114 us
    all_gather x1, waiting for transfers between devices, shards(): lax.all_gather((grad_inputs * keep_part[:, None]).astype(low), 'mp', axis...  114 us
    psum x4, blocking collectives, share_sum(): return lax.psum(value.astype(jnp.bfloat16), axis).astype(jnp.float32)  71.1 us
    all_gather x5, blocking collectives, spread(): value = lax.all_gather(value, axis, axis=dim[axis], tiled=True)  57.3 us
    dot_general x8, matrix products, matmul_nt(): lax.dot_general(left, right, (((1,), (1,)), ((), ())), preferred_element_...  46.5 us
  transfers between devices with their start and end apart: 24, of which 19 were waited for; matrix products, arithmetic and copies ran while one was open for 14% of the time, Pallas kernels for 0%

profile of v1, /device:TPU:0, one launch (start us, length us, event | category | flops | bytes accessed | tf_op | source)
XLA Modules:
  0.0 1504.8 jit_solution(1652139954793461995)
XLA Ops:
  37.8 26.5 %all-gather.40.cloned.1.call-done = bf16[1,1,768,768]{3,2,1,0:T(8,128)(2,1)} async-done(((bf16[1,1,96,768]{3,2,1,0:T(8,128)(2,1)}), bf16[1,1,768,768]{3,2,1,0:T(8,128)(2,1)}) %all-gather.40.cloned.1.call-update) | async-done | bytes 1179664 | tf_op jit(solution)/shard_map/all_gather | solution.py:187
  93.0 14.0 all-reduce.6
  202.5 54.5 %all-gather.38.cloned.1.call-done = bf16[1,1,768,3072]{3,2,1,0:T(8,128)(2,1)} async-done(((bf16[1,1,768,768]{3,2,1,0:T(8,128)(2,1)}), bf16[1,1,768,3072]{3,2,1,0:T(8,128)(2,1)}) %all-gather.38.cloned.1.call-update) | async-done | bytes 4718608 | tf_op jit(solution)/shard_map/all_gather | solution.py:187
  268.0 78.4 %all-gather.42.cloned.1.call-done = bf16[1,1,3072,768]{3,2,1,0:T(8,128)(2,1)} async-done(((bf16[1,1,768,768]{3,2,1,0:T(8,128)(2,1)}), bf16[1,1,3072,768]{3,2,1,0:T(8,128)(2,1)}) %all-gather.42.cloned.1.call-update) | async-done | bytes 4718608 | tf_op jit(solution)/shard_map/all_gather | solution.py:187
  382.0 17.4 %psum.42 = bf16[32,768]{1,0:T(8,128)(2,1)} all-reduce(bf16[32,768]{1,0:T(8,128)(2,1)S(1)} %convolution_convert_fusion.12), channel_id=1, replica_groups=mesh['dp'=8,'mp'=4] {'mp'}, use_global_device_ids=true, to_apply=%region_8.9 | all-reduce | flops 24576 | bytes 98304 | tf_op jit(solution)/shard_map/psum | solution.py:96
  406.9 18.5 %psum.43 = bf16[32,768]{1,0:T(8,128)(2,1)} all-reduce(bf16[32,768]{1,0:T(8,128)(2,1)} %fusion.84), channel_id=1, replica_groups=mesh['dp'=8,'mp'=4] {'mp'}, use_global_device_ids=true, to_apply=%region_11.12 | all-reduce | flops 24576 | bytes 98304 | tf_op jit(solution)/shard_map/psum | solution.py:96
  436.0 17.7 %psum.44 = bf16[32,768]{1,0:T(8,128)(2,1)} all-reduce(bf16[32,768]{1,0:T(8,128)(2,1)} %fusion.81), channel_id=1, replica_groups=mesh['dp'=8,'mp'=4] {'mp'}, use_global_device_ids=true, to_apply=%region_16.17 | all-reduce | flops 24576 | bytes 98304 | tf_op jit(solution)/shard_map/psum | solution.py:96
  465.9 17.4 %psum.45 = bf16[32,768]{1,0:T(8,128)(2,1)S(1)} all-reduce(bf16[32,768]{1,0:T(8,128)(2,1)S(1)} %convolution_convert_fusion.11), channel_id=1, replica_groups=mesh['dp'=8,'mp'=4] {'mp'}, use_global_device_ids=true, to_apply=%region_20.21 | all-reduce | flops 24576 | bytes 98304 | tf_op jit(solution)/shard_map/psum | solution.py:96
  498.9 16.4 %fusion.218 = (bf16[3072]{0:T(1024)(128)(2,1)}, bf16[1024,3072]{1,0:T(8,128)(2,1)}) fusion(f32[1024,3072]{1,0:T(8,128)} %fusion.18, f32[3072]{0:T(1024)S(1)} %bitcast.415, bf16[1,1,3072,768]{3,2,1,0:T(8,128)(2,1)S(1)} %bitcast.419, f32[1024,768]{1,0:T(8,128)S(1)} %get-tuple-element.248, f32[1024]{0:T(1024)S(1)} %negate_multiply_fusion.1), kind=kOutput, calls=%fused_computation.342 | convolution fusion | flops 4902614016 | bytes 26761216 | tf_op jit(solution)/shard_map/dot_general | solution.py:39
  608.8 18.8 %psum.46 = bf16[6,768]{1,0:T(8,128)(2,1)S(1)} all-reduce(f32[6,768]{1,0:T(8,128)S(1)} %stack.177), channel_id=1, replica_groups=mesh['dp'=8,'mp'=4] {'mp'}, use_global_device_ids=true, to_apply=%region_54.55 | all-reduce | flops 4608 | bytes 27648 | tf_op jit(solution)/shard_map/psum | solution.py:255
  656.2 74.9 %reduce-scatter.31.cloned.1.call-done = bf16[768,768]{1,0:T(8,128)(2,1)} async-done(((bf16[768,3072]{1,0:T(8,128)(2,1)}), bf16[768,768]{1,0:T(8,128)(2,1)}) %reduce-scatter.31.cloned.1.call-update) | async-done | bytes 1179664 | tf_op jit(solution)/shard_map/reduce_scatter | solution.py:242
  732.9 86.8 %reduce-scatter.37.cloned.1.call-done = bf16[768,768]{1,0:T(8,128)(2,1)} async-done(((bf16[3072,768]{1,0:T(8,128)(2,1)}), bf16[768,768]{1,0:T(8,128)(2,1)}) %reduce-scatter.37.cloned.1.call-update) | async-done | bytes 1179664 | tf_op jit(solution)/shard_map/reduce_scatter | solution.py:242
  858.9 35.7 %reduce-scatter.49.cloned.1.call-done = bf16[96,32]{1,0:T(8,128)(2,1)} async-done(((bf16[768,32]{1,0:T(8,128)(2,1)}), bf16[96,32]{1,0:T(8,128)(2,1)}) %reduce-scatter.49.cloned.1.call-update) | async-done | bytes 6160
  897.4 36.1 %reduce-scatter.45.cloned.1.call-done = bf16[96,576]{1,0:T(8,128)(2,1)} async-done(((bf16[768,576]{1,0:T(8,128)(2,1)}), bf16[96,576]{1,0:T(8,128)(2,1)}) %reduce-scatter.45.cloned.1.call-update) | async-done | bytes 110608
  934.5 35.7 %reduce-scatter.29.cloned.1.call-done = bf16[24,768]{1,0:T(8,128)(2,1)} async-done(((bf16[192,768]{1,0:T(8,128)(2,1)}), bf16[24,768]{1,0:T(8,128)(2,1)}) %reduce-scatter.29.cloned.1.call-update) | async-done | bytes 36880 | tf_op jit(solution)/shard_map/reduce_scatter | solution.py:242
  970.2 36.1 %reduce-scatter.27.cloned.1.call-done = bf16[24,768]{1,0:T(8,128)(2,1)} async-done(((bf16[192,768]{1,0:T(8,128)(2,1)}), bf16[24,768]{1,0:T(8,128)(2,1)}) %reduce-scatter.27.cloned.1.call-update) | async-done | bytes 36880 | tf_op jit(solution)/shard_map/reduce_scatter | solution.py:242
  1007.7 37.8 %reduce-scatter.43.cloned.1.call-done = bf16[96,576]{1,0:T(8,128)(2,1)} async-done(((bf16[768,576]{1,0:T(8,128)(2,1)}), bf16[96,576]{1,0:T(8,128)(2,1)}) %reduce-scatter.43.cloned.1.call-update) | async-done | bytes 110608
  1048.6 114.4 %all-gather.30.cloned.1.call-done = bf16[4096,768]{1,0:T(8,128)(2,1)} async-done(((bf16[1024,768]{1,0:T(8,128)(2,1)}), bf16[4096,768]{1,0:T(8,128)(2,1)}) %all-gather.30.cloned.1.call-update) | async-done | bytes 6291472 | tf_op jit(solution)/shard_map/all_gather | solution.py:235
  1171.6 29.6 %reduce-scatter.35.cloned.1.call-done = bf16[96,768]{1,0:T(8,128)(2,1)} async-done(((bf16[768,768]{1,0:T(8,128)(2,1)}), bf16[96,768]{1,0:T(8,128)(2,1)}) %reduce-scatter.35.cloned.1.call-update) | async-done | bytes 147472 | tf_op jit(solution)/shard_map/reduce_scatter | solution.py:242
  1201.1 40.4 %reduce-scatter.33.cloned.1.call-done = bf16[96,768]{1,0:T(8,128)(2,1)} async-done(((bf16[768,768]{1,0:T(8,128)(2,1)}), bf16[96,768]{1,0:T(8,128)(2,1)}) %reduce-scatter.33.cloned.1.call-update) | async-done | bytes 147472 | tf_op jit(solution)/shard_map/reduce_scatter | solution.py:242
  1244.6 37.0 %reduce-scatter.41.cloned.1.call-done = bf16[96,768]{1,0:T(8,128)(2,1)} async-done(((bf16[768,768]{1,0:T(8,128)(2,1)}), bf16[96,768]{1,0:T(8,128)(2,1)}) %reduce-scatter.41.cloned.1.call-update) | async-done | bytes 147472 | tf_op jit(solution)/shard_map/reduce_scatter | solution.py:242
  1281.6 40.4 %reduce-scatter.39.cloned.1.call-done = bf16[96,768]{1,0:T(8,128)(2,1)} async-done(((bf16[768,768]{1,0:T(8,128)(2,1)}), bf16[96,768]{1,0:T(8,128)(2,1)}) %reduce-scatter.39.cloned.1.call-update) | async-done | bytes 147472 | tf_op jit(solution)/shard_map/reduce_scatter | solution.py:242
  1324.3 114.4 %all-gather.28.cloned.1.call-done = bf16[4096,768]{1,0:T(8,128)(2,1)} async-done(((bf16[1024,768]{1,0:T(8,128)(2,1)}), bf16[4096,768]{1,0:T(8,128)(2,1)}) %all-gather.28.cloned.1.call-update) | async-done | bytes 6291472 | tf_op jit(solution)/shard_map/all_gather | solution.py:227
  1438.8 38.4 %psum.47 = f32[]{:T(128)} all-reduce(f32[]{:T(128)S(6)} %add.414), channel_id=1, replica_groups=mesh['dp'=8,'mp'=4] {'dp','mp'}, use_global_device_ids=true, to_apply=%region_65.66 | all-reduce | flops 1 | bytes 8 | tf_op jit(solution)/shard_map/psum | solution.py:263
  (439 shorter events, 443.0 us)
Async XLA Ops:
  7.2 30.5 %all-gather.36.cloned.1.call-start = ((), (), s32[]{:S(2)}) async-start(), calls=%async_computation.28 | async-start | bytes 1327104 | tf_op jit(solution)/shard_map/all_gather | solution.py:187
  9.7 54.5 %all-gather.40.cloned.1.call-start = ((), (), s32[]{:S(2)}) async-start(), calls=%async_computation.30 | async-start | bytes 1327104 | tf_op jit(solution)/shard_map/all_gather | solution.py:187
  10.7 156.8 %all-gather.32.cloned.1.call-start = ((), (), s32[]{:S(2)}) async-start(), calls=%async_computation.26 | async-start | bytes 4423680 | tf_op jit(solution)/shard_map/all_gather | solution.py:187
  24.4 172.1 %all-gather.34.cloned.1.call-start = ((), (), s32[]{:S(2)}) async-start(), calls=%async_computation.27 | async-start | bytes 1474560 | tf_op jit(solution)/shard_map/all_gather | solution.py:187
  35.5 221.6 %all-gather.38.cloned.1.call-start = ((), (), s32[]{:S(2)}) async-start(), calls=%async_computation.29 | async-start | bytes 5898240 | tf_op jit(solution)/shard_map/all_gather | solution.py:187
  37.8 308.6 %all-gather.42.cloned.1.call-start = ((), (), s32[]{:S(2)}) async-start(), calls=%async_computation.31 | async-start | bytes 5898240 | tf_op jit(solution)/shard_map/all_gather | solution.py:187
  64.3 338.0 %all-gather.44.cloned.1.call-start = ((), (), s32[]{:S(2)}) async-start(), calls=%async_computation.32 | async-start | bytes 1327104 | tf_op jit(solution)/shard_map/all_gather | solution.py:187
  65.0 339.6 %all-gather.46.cloned.1.call-start = ((), (), s32[]{:S(2)}) async-start(), calls=%async_computation.33 | async-start | bytes 1327104 | tf_op jit(solution)/shard_map/all_gather | solution.py:187
  65.8 567.3 %reduce-scatter.25.cloned.1.call-start = ((), (), s32[]{:S(2)}) async-start(), calls=%async_computation.17 | async-start | bytes 1474560 | tf_op jit(solution)/shard_map/reduce_scatter | solution.py:242
  530.5 112.8 %reduce-scatter.23.cloned.1.call-start = ((), (), s32[]{:S(2)}) async-start(), calls=%async_computation.16 | async-start | bytes 4423680 | tf_op jit(solution)/shard_map/reduce_scatter | solution.py:242
  577.4 153.8 %reduce-scatter.31.cloned.1.call-start = ((), (), s32[]{:S(2)}) async-start(), calls=%async_computation.20 | async-start | bytes 5898240 | tf_op jit(solution)/shard_map/reduce_scatter | solution.py:242
  588.0 231.7 %reduce-scatter.37.cloned.1.call-start = ((), (), s32[]{:S(2)}) async-start(), calls=%async_computation.23 | async-start | bytes 5898240 | tf_op jit(solution)/shard_map/reduce_scatter | solution.py:242
  602.4 255.0 %reduce-scatter.47.cloned.1.call-start = ((), (), s32[]{:S(2)}) async-start(), calls=%async_computation.36 | async-start | bytes 221184
  628.9 265.7 %reduce-scatter.49.cloned.1.call-start = ((), (), s32[]{:S(2)}) async-start(), calls=%async_computation.37 | async-start | bytes 221184
  629.8 303.7 %reduce-scatter.45.cloned.1.call-start = ((), (), s32[]{:S(2)}) async-start(), calls=%async_computation.35 | async-start | bytes 1105920
  631.3 338.9 %reduce-scatter.29.cloned.1.call-start = ((), (), s32[]{:S(2)}) async-start(), calls=%async_computation.19 | async-start | bytes 331776 | tf_op jit(solution)/shard_map/reduce_scatter | solution.py:242
  633.1 373.3 %reduce-scatter.27.cloned.1.call-start = ((), (), s32[]{:S(2)}) async-start(), calls=%async_computation.18 | async-start | bytes 331776 | tf_op jit(solution)/shard_map/reduce_scatter | solution.py:242
  633.6 411.9 %reduce-scatter.43.cloned.1.call-start = ((), (), s32[]{:S(2)}) async-start(), calls=%async_computation.34 | async-start | bytes 1105920
  645.6 517.4 %all-gather.30.cloned.1.call-start = ((), (), s32[]{:S(2)}) async-start(), calls=%async_computation.15 | async-start | bytes 7864320 | tf_op jit(solution)/shard_map/all_gather | solution.py:235
  654.5 546.6 %reduce-scatter.35.cloned.1.call-start = ((), (), s32[]{:S(2)}) async-start(), calls=%async_computation.22 | async-start | bytes 1327104 | tf_op jit(solution)/shard_map/reduce_scatter | solution.py:242
  656.2 585.3 %reduce-scatter.33.cloned.1.call-start = ((), (), s32[]{:S(2)}) async-start(), calls=%async_computation.21 | async-start | bytes 1327104 | tf_op jit(solution)/shard_map/reduce_scatter | solution.py:242
  731.2 550.4 %reduce-scatter.41.cloned.1.call-start = ((), (), s32[]{:S(2)}) async-start(), calls=%async_computation.25 | async-start | bytes 1327104 | tf_op jit(solution)/shard_map/reduce_scatter | solution.py:242
  732.9 589.0 %reduce-scatter.39.cloned.1.call-start = ((), (), s32[]{:S(2)}) async-start(), calls=%async_computation.24 | async-start | bytes 1327104 | tf_op jit(solution)/shard_map/reduce_scatter | solution.py:242
  819.7 619.0 %all-gather.28.cloned.1.call-start = ((), (), s32[]{:S(2)}) async-start(), calls=%async_computation.14 | async-start | bytes 7864320 | tf_op jit(solution)/shard_map/all_gather | solution.py:227
  (96 other events, 2655.8 us)
Sparse Core Ops, SparseCore 0:
  10.5 27.1 all-gather.35
  40.2 24.0 all-gather.39
  66.4 70.0 all-gather.31
  137.9 29.1 all-gather.33
  168.5 88.5 all-gather.37
  258.5 87.8 all-gather.41
  348.8 22.5 all-gather.43
  373.8 24.0 all-gather.45
  530.6 27.5 reduce-scatter.24
  577.5 65.7 reduce-scatter.22
  645.6 85.5 reduce-scatter.30
  733.9 85.7 reduce-scatter.36
  823.3 34.0 reduce-scatter.46
  861.1 33.4 reduce-scatter.48
  897.7 35.7 reduce-scatter.44
  937.3 32.8 reduce-scatter.28
  973.4 32.8 reduce-scatter.26
  1009.7 35.7 reduce-scatter.42
  1047.6 115.3 all-gather.29
  1166.1 34.9 reduce-scatter.34
  1204.7 36.7 reduce-scatter.32
  1244.7 36.7 reduce-scatter.40
  1285.1 36.7 reduce-scatter.38
  1323.4 115.3 all-gather.27

commit v2 on v0

v2 whole, which is shorter than its diff:
```python
import functools

import jax
import jax.numpy as jnp
from jax import lax
from jax.experimental import pallas as pl
from jax.experimental.pallas import tpu as pltpu
from jax.sharding import PartitionSpec as P

LOW = jnp.bfloat16
FULL = jnp.float32
HEAD_DIM = 64
SEG = 128
NSEG = 32
norm_eps = 1e-05
clip_level = 1.0
rate = 0.02
decay = 0.01
beta_one = 0.9
beta_two = 0.999
adam_eps = 1e-08
adam_step = 10
LANES = 2 * HEAD_DIM
TANH_A = 0.7978845608028654
TANH_B = 0.044715
VMEM_BYTES = 60 * 1024 * 1024
FLOPS = 1.15e9


def dot_nn(a, b):
    return lax.dot_general(a, b, (((1,), (0,)), ((), ())), preferred_element_type=FULL)


def dot_nt(a, b):
    return lax.dot_general(a, b, (((1,), (1,)), ((), ())), preferred_element_type=FULL)


def dot_tn(a, b):
    return lax.dot_general(a, b, (((0,), (0,)), ((), ())), preferred_element_type=FULL)


def normal(values):
    mean = jnp.mean(values, axis=-1, keepdims=True)
    centred = values - mean
    spread = jnp.mean(centred * centred, axis=-1, keepdims=True)
    scale = lax.rsqrt(spread + norm_eps)
    return centred * scale, scale


def normal_back(grad, unit, scale, gain):
    scaled = grad * gain
    one = jnp.mean(scaled, axis=-1, keepdims=True)
    two = jnp.mean(scaled * unit, axis=-1, keepdims=True)
    return scale * (scaled - one - unit * two)


def halves(block, low):
    zero = jnp.zeros_like(block)
    return jnp.concatenate([jnp.where(low, block, zero), jnp.where(low, zero, block)], axis=0)


def soft(query, keys, live, span):
    scores = jnp.where(live, dot_nt(query, keys), -1e30)
    parts = []
    for half in range(2):
        piece = scores[:, half * span : (half + 1) * span]
        weights = jnp.exp(piece - jnp.max(piece, axis=-1, keepdims=True))
        parts.append(weights * (1.0 / jnp.sum(weights, axis=-1, keepdims=True)))
    return parts


class Plan:
    def __init__(self, groups, pieces, rows, mp_at, dp_at, count=1):
        self.groups, self.pieces, self.rows = groups, pieces, rows
        self.mp_at, self.dp_at = mp_at, dp_at
        self.count = count

    def copies(self):
        return sum(len(places) for places, _ in self.pieces) * (self.groups // 2)


def fetch(plan, info, pieces, land, sems):
    size = plan.rows
    copies = []
    for (places, half), piece in zip(plan.pieces, pieces):
        for at, place in enumerate(places):
            start = pl.multiple_of(info[plan.dp_at + place] * size, 16)
            for inner in range(piece.shape[1]):
                copy = pltpu.make_async_copy(
                    piece.at[at, inner],
                    land(half * piece.shape[1] + inner, start, size),
                    sems.at[len(copies)],
                )
                copy.start()
                copies.append(copy)
    return copies


def padded(count):
    return -(-count // 16) * 16


def wait_all(copies):
    for copy in copies:
        copy.wait()


def turn(block):
    return jnp.concatenate([block[:, HEAD_DIM:], block[:, :HEAD_DIM]], axis=1)


def fetch_units(sections, up_all, down_all, w_up, w_down, sems):
    width = w_down.shape[1]
    copies = []
    for kind, (source, (base, size)) in enumerate(zip((up_all, down_all), sections)):
        for m in range(source.shape[0]):
            for at in range(source.shape[1]):
                if kind:
                    target = w_down.at[pl.ds(m * width + at * size, size), :]
                else:
                    target = w_up.at[pl.ds(at * size, size), m * width : (m + 1) * width]
                copy = pltpu.make_async_copy(
                    source.at[m, at, pl.ds(base, size), :],
                    target,
                    sems.at[kind, m * source.shape[1] + at],
                )
                copy.start()
                copies.append(copy)
    return copies


def fetch_out(section, plan, info, out_all, stage, sems):
    base, size = section
    copies = []
    for m in range(plan.groups):
        for at in range(out_all.shape[1]):
            copy = pltpu.make_async_copy(
                out_all.at[info[plan.mp_at + m], at, pl.ds(base, size), :],
                stage.at[m, pl.ds(at * size, size), :],
                sems.at[len(copies)],
            )
            copy.start()
            copies.append(copy)
    return copies


def pair_columns(stage, w_in):
    groups, width = stage.shape[:2]
    low = lax.broadcasted_iota(jnp.int32, (width, LANES), 1) < HEAD_DIM
    for part in range(3):
        base = part * width
        for m in range(groups):
            at = base + m * LANES
            w_in[:, at : at + LANES] = stage[m, :, part * LANES : (part + 1) * LANES]
        for m in range(0, groups, 2):
            at = base + (groups + m // 2) * LANES
            source = slice(3 * LANES, 4 * LANES) if part < 2 else slice(4 * LANES, 5 * LANES)
            left, right = stage[m, :, source], stage[m + 1, :, source]
            if part == 1:
                left = turn(left)
            else:
                right = turn(right)
            w_in[:, at : at + LANES] = jnp.where(low, left, right)


def pair_rows(stage, w_out, count):
    groups, rows = stage.shape[:2]
    share = w_out.shape[0] // groups // count
    step = rows // count
    for m in range(groups):
        parts = [stage[m, at * step : (at + 1) * step, :].astype(FULL)[:share] for at in range(count)]
        found = jnp.concatenate(parts, axis=0).astype(LOW)
        w_out[m * LANES : (m + 1) * LANES, :] = found[:LANES]
        goal = groups * LANES + m * HEAD_DIM
        w_out[goal : goal + HEAD_DIM, :] = found[LANES:]


def columns_of(block):
    at = [block[:, i * HEAD_DIM : (i + 1) * HEAD_DIM] for i in range(9)]
    order = ((0, 3), (1, 4), (2, 5), (6, 7))
    return [jnp.concatenate([at[i], at[j]], axis=1) for i, j in order] + [at[8]]


def heads_block_kernel(info, attend_in, bias, affine, position, out, small):
    rows = attend_in.shape[2]
    small[...] = jnp.zeros_like(small)
    small[0:6, :rows] = affine[0, 0]
    small[6:8, :rows] = bias[0]
    small[8:14, :rows] = affine[0, 1]
    small[16 : 16 + NSEG, :rows] = position[0]
    blocks = columns_of(attend_in[0, 0])
    blocks[4] = jnp.concatenate([blocks[4], small[...].T[:rows, :HEAD_DIM]], axis=1)
    for at, block in enumerate(blocks):
        out[:, at * LANES : (at + 1) * LANES] = block.astype(LOW)


def units_block_kernel(info, *refs):
    ins, out = refs[:-1], refs[-1]
    start = 0
    for source in ins:
        block = source[0, 0]
        rows = block.shape[0]
        if block.shape[1] != out.shape[1]:
            blocks = columns_of(block)
            blocks[4] = jnp.concatenate([blocks[4], jnp.zeros((rows, HEAD_DIM), FULL)], axis=1)
            blocks.append(jnp.zeros((rows, LANES), FULL))
            block = jnp.concatenate(blocks, axis=1)
        if padded(rows) > rows:
            block = jnp.concatenate([block, jnp.zeros((padded(rows) - rows, out.shape[1]), FULL)], axis=0)
        out[start : start + padded(rows), :] = block.astype(LOW)
        start += padded(rows)


def attend_kernel(plan, info, tok, *refs):
    pieces, refs = refs[:-9], refs[-9:]
    triple, context, w_in, affine_one, affine_two, position, b_up, stage, sems = refs
    step = pl.program_id(0)
    rows, width = tok.shape

    @pl.when(step == 0)
    def _():
        def land(m, start, size):
            return stage.at[m, pl.ds(start, size), :]

        wait_all(fetch(plan, info, pieces, land, sems))
        for m in range(plan.groups):
            small = stage[m, :, 4 * LANES : 5 * LANES].astype(FULL).T
            place = pl.multiple_of(info[plan.mp_at + m] * width, LANES)
            b_up[:, pl.ds(place, width)] = small[HEAD_DIM + 6 : HEAD_DIM + 7]
            if m == 0:
                affine_one[...] = small[HEAD_DIM : HEAD_DIM + 8]
                affine_two[...] = small[HEAD_DIM + 8 : HEAD_DIM + 16]
                position[...] = small[HEAD_DIM + 16 : HEAD_DIM + 16 + NSEG]
        pair_columns(stage, w_in)

    triple[...] = dot_nn(tok[...], w_in[...]).astype(LOW)
    low = lax.broadcasted_iota(jnp.int32, (SEG, LANES), 1) < HEAD_DIM
    spot = lax.broadcasted_iota(jnp.int32, (SEG, 2 * SEG), 1) % SEG
    for seg in range(rows // SEG):
        live = spot < info[step * (rows // SEG) + seg]
        here = slice(seg * SEG, (seg + 1) * SEG)
        for pair in range(width // LANES):
            at = pair * LANES
            query = triple[here, at : at + LANES] * LOW(HEAD_DIM ** (-0.5))
            keys = halves(triple[here, width + at : width + at + LANES], low)
            values = halves(triple[here, 2 * width + at : 2 * width + at + LANES], low)
            probs = jnp.concatenate([part.astype(LOW) for part in soft(query, keys, live, SEG)], axis=1)
            context[here, at : at + LANES] = dot_nn(probs, values).astype(LOW)


def feed_kernel(plan, sections, info, tok, context, affine, b_up, up_all, down_all, out_all, *refs):
    resid, hid_low, expanded, resid_two, first, tops, w_out, w_up, w_down, stage, sems, out_sems = refs
    step = pl.program_id(0)
    rows, width = tok.shape
    segs = rows // SEG

    @pl.when(step == 0)
    def _():
        outs = fetch_out(sections[2], plan, info, out_all, stage, out_sems)
        copies = fetch_units(sections[:2], up_all, down_all, w_up, w_down, sems)
        wait_all(outs)
        pair_rows(stage, w_out, plan.count)
        wait_all(copies)

    mixed = dot_nn(context[...], w_out[...])
    value = tok[...].astype(FULL) + mixed + affine[4:5, :]
    resid[...] = value
    hidden = normal(value)[0] * affine[0:1, :] + affine[1:2, :]
    low = hidden.astype(LOW)
    hid_low[...] = low
    total = hidden + affine[5:6, :]
    units = w_up.shape[1]
    block = width
    for at in range(0, units, block):
        up = dot_nn(low, w_up[:, at : at + block]) + b_up[:, at : at + block]
        expanded[:, at : at + block] = up.astype(LOW)
        curve = jnp.tanh(TANH_A * (up + TANH_B * up * up * up))
        active = (0.5 * up * (1.0 + curve)).astype(LOW)
        total = total + dot_nn(active, w_down[at : at + block, :])
    resid_two[...] = total
    result = normal(total)[0] * affine[2:3, :] + affine[3:4, :]
    row = lax.broadcasted_iota(jnp.int32, (SEG, 1), 0)
    for seg in range(segs):
        piece = result[seg * SEG : (seg + 1) * SEG, :]
        kept = jnp.where(row < info[step * segs + seg], piece, 0.0)
        first[seg * SEG : (seg + 1) * SEG, :] = kept.astype(LOW)
        tops[pl.ds(step * segs + seg, 1), :] = piece[0:1, :]


def feed_back_kernel(plan, sections, info, cot, back_heads, resid_two, expanded, resid, affine, *refs):
    ring, refs = refs[: plan.groups], refs[plan.groups :]
    up_all, down_all, grad_resid, active, grad_exp, grad_ret, grad_mixed, sums, bias = refs[:9]
    heads, w_up, w_down, sems = refs[9:]
    step = pl.program_id(0)
    rows, width = cot.shape
    segs = rows // SEG

    @pl.when(step == 0)
    def _():
        copies = fetch_units(sections[:2], up_all, down_all, w_up, w_down, sems)
        total = back_heads[...]
        for member in ring:
            total = total + member[...].astype(FULL)
        heads[...] = total
        wait_all(copies)

    row = lax.broadcasted_iota(jnp.int32, (SEG, 1), 0)
    first = info[plan.mp_at] * (pl.num_programs(0) * segs) + step * segs
    pieces = []
    for seg in range(segs):
        piece = cot[seg * SEG : (seg + 1) * SEG, :].astype(FULL)
        piece = jnp.where(row < info[step * segs + seg], piece, 0.0)
        pieces.append(jnp.where(row == 0, heads[pl.ds(first + seg, 1), :], piece))
    grad = jnp.concatenate(pieces, axis=0)
    unit, scale = normal(resid_two[...])

    @pl.when(step == 0)
    def _():
        sums[...] = jnp.zeros_like(sums)
        bias[...] = jnp.zeros_like(bias)

    back = normal_back(grad, unit, scale, affine[2:3, :])
    sums[2:3, :] += jnp.sum(grad * unit, axis=0, keepdims=True)
    sums[3:4, :] += jnp.sum(grad, axis=0, keepdims=True)
    sums[5:6, :] += jnp.sum(back, axis=0, keepdims=True)
    low = back.astype(LOW)
    grad_ret[...] = low
    units = w_up.shape[1]
    total = back
    block = width
    for at in range(0, units, block):
        grad_act = dot_nt(low, w_down[at : at + block, :])
        up = expanded[:, at : at + block].astype(FULL)
        square = up * up
        curve = jnp.tanh(TANH_A * (up + TANH_B * up * square))
        half = 0.5 * (1.0 + curve)
        active[:, at : at + block] = (up * half).astype(LOW)
        slope = half + 0.5 * up * (1.0 - curve * curve) * (TANH_A + 3.0 * TANH_A * TANH_B * square)
        wide = slope * grad_act
        bias[:, at : at + block] += jnp.sum(wide, axis=0, keepdims=True)
        short = wide.astype(LOW)
        grad_exp[:, at : at + block] = short
        total = total + dot_nt(short, w_up[:, at : at + block])
    unit, scale = normal(resid[...])
    back = normal_back(total, unit, scale, affine[0:1, :])
    sums[0:1, :] += jnp.sum(total * unit, axis=0, keepdims=True)
    sums[1:2, :] += jnp.sum(total, axis=0, keepdims=True)
    sums[4:5, :] += jnp.sum(back, axis=0, keepdims=True)
    grad_resid[...] = back
    grad_mixed[...] = back.astype(LOW)


def pair_back(query, keys, values, probs, down, low, span):
    grad_probs = dot_nt(down, values)
    scores = []
    for half in range(2):
        mine = probs[half]
        given = grad_probs[:, half * span : (half + 1) * span]
        product = mine * given
        inner = jnp.sum(product, axis=-1, keepdims=True)
        scores.append((product - mine * inner).astype(LOW))
    grad_scores = jnp.concatenate(scores, axis=1)
    probs = jnp.concatenate([part.astype(LOW) for part in probs], axis=1)
    grad_query = dot_nn(grad_scores, keys) * HEAD_DIM ** (-0.5)
    both = dot_tn(grad_scores, query)
    grad_key = jnp.where(low, both[:span], both[span:])
    both = dot_tn(probs, down)
    return grad_query, grad_key, jnp.where(low, both[:span], both[span:])


def attend_back_kernel(info, grad_resid, grad_mixed, triple, w_out, w_in, early, grad_in, grad_triple, grad_ctx):
    del early
    step = pl.program_id(0)
    rows, width = grad_resid.shape
    segs = rows // SEG
    grad_ctx[...] = dot_nt(grad_mixed[...], w_out[...]).astype(LOW)
    low = lax.broadcasted_iota(jnp.int32, (SEG, LANES), 1) < HEAD_DIM
    spot = lax.broadcasted_iota(jnp.int32, (SEG, 2 * SEG), 1) % SEG
    shrink = HEAD_DIM ** (-0.5)
    for seg in range(segs):
        live = spot < info[step * segs + seg]
        here = slice(seg * SEG, (seg + 1) * SEG)
        for pair in range(width // LANES):
            at = pair * LANES
            query = triple[here, at : at + LANES] * LOW(shrink)
            keys = halves(triple[here, width + at : width + at + LANES], low)
            values = halves(triple[here, 2 * width + at : 2 * width + at + LANES], low)
            probs = soft(query, keys, live, SEG)
            down = grad_ctx[here, at : at + LANES]
            found = pair_back(query, keys, values, probs, down, low, SEG)
            for part in range(3):
                goal = part * width + at
                grad_triple[here, goal : goal + LANES] = found[part].astype(LOW)
    grad_in[...] = (grad_resid[...] + dot_nt(grad_triple[...], w_in[...])).astype(LOW)


def unit_grad_kernel(
    plan, info, active, grad_ret, hid_low, grad_exp, context, grad_mixed, sums_one, sums_two, grad_heads, bias, bias_two, early, out, whole, mixing, small
):
    del early
    m = pl.program_id(0)
    size = plan.rows
    width = whole.shape[0]
    third = width // plan.groups
    share = third // out.shape[0]

    @pl.when(m == 0)
    def _():
        found = dot_tn(context[...], grad_mixed[...])
        for at in range(plan.groups):
            mixing[at * third : at * third + LANES, :] = found[at * LANES : (at + 1) * LANES]
            goal = plan.groups * LANES + at * HEAD_DIM
            mixing[at * third + LANES : (at + 1) * third, :] = found[goal : goal + HEAD_DIM]

    step = padded(size)
    for kind, (left, right) in enumerate(((active, grad_ret), (hid_low, grad_exp))):
        whole[...] = dot_tn(left[...], right[...])
        for at in range(out.shape[0]):
            out[at, 0, kind * step : kind * step + size, :] = whole[
                at * size : (at + 1) * size, :
            ].astype(LOW)
    leader = jnp.where(info[plan.mp_at] == 0, 1.0, 0.0)
    row = lax.broadcasted_iota(jnp.int32, (8, 1), 0)
    place = pl.multiple_of(info[plan.mp_at + m] * width, LANES)
    own = jnp.where(m == 0, 1.0, 0.0)
    biases = jnp.where(row == 6, bias[:, pl.ds(place, width)], bias_two[...] * own)
    small[0:8, :] = jnp.where(row < 6, sums_one[...], biases)
    small[8:16, :] = sums_two[...] * leader
    position = grad_heads[0:NSEG, :]
    for doc in range(1, grad_heads.shape[0] // NSEG):
        position = position + grad_heads[doc * NSEG : (doc + 1) * NSEG, :]
    small[16:, :] = position * leader
    gap = jnp.zeros((8, LANES - size), FULL)
    mine = mixing[pl.ds(pl.multiple_of(m * third, HEAD_DIM), third), :]
    for at in range(out.shape[0]):
        lines = small[:, at * size : (at + 1) * size]
        blocks = []
        for block in range(width // LANES):
            blocks += [lines[block * 8 : (block + 1) * 8], gap]
        rows = [jnp.concatenate(blocks, axis=1), mine[at * share : (at + 1) * share]]
        rest = out.shape[2] - 2 * step - share - 8
        if rest:
            rows.append(jnp.zeros((rest, width), FULL))
        out[at, 0, 2 * step :, :] = jnp.concatenate(rows, axis=0).astype(LOW)


def head_grad_kernel(plan, lists, info, tok, grad_triple, early, keep_a, send_a, keep_b, send_b, whole):
    del early
    size = plan.rows
    width = tok.shape[1]
    whole[...] = dot_tn(tok[...], grad_triple[...])
    low = lax.broadcasted_iota(jnp.int32, (size, LANES), 1) < HEAD_DIM
    for half, (keep, send) in enumerate(((keep_a, send_a), (keep_b, send_b))):
        for at, place in enumerate(lists[half]):
            for out, which in ((keep, place), (send, place ^ 1)):
                start = pl.multiple_of(info[plan.dp_at + which] * size, 8)
                for inner in range(plan.groups // 2):
                    m = half * (plan.groups // 2) + inner
                    for part in range(3):
                        goal = part * width + m * LANES
                        out[at, inner, :, part * LANES : (part + 1) * LANES] = whole[
                            pl.ds(start, size), goal : goal + LANES
                        ].astype(LOW)
                    blocks = []
                    for part in range(3):
                        goal = part * width + (plan.groups + m // 2) * LANES
                        blocks.append(whole[pl.ds(start, size), goal : goal + LANES])
                    if m % 2 == 0:
                        blocks = [blocks[0], turn(blocks[1]), blocks[2]]
                    else:
                        blocks = [turn(blocks[0]), blocks[1], turn(blocks[2])]
                    out[at, inner, :, 3 * LANES : 4 * LANES] = jnp.where(low, blocks[0], blocks[1]).astype(LOW)
                    out[at, inner, :, 4 * LANES : 5 * LANES] = jnp.where(low, blocks[2], 0.0).astype(LOW)


def spread_kernel(groups, mp_at, info, *refs):
    line, (tops, _, out, held, ready, in_sems, out_sems) = refs[:-7], refs[-7:]
    rows = held.shape[1]
    mine = info[mp_at]
    row = lax.broadcasted_iota(jnp.int32, (16, 1), 0)

    def take(at, step, part):
        place = mine + step
        slot = step % groups
        into = pltpu.make_async_copy(line[at], held.at[slot], in_sems.at[at])
        if ready is held:
            source = held.at[slot]
        else:
            source = ready.at[slot]
        goal = pl.ds(pl.multiple_of(place * rows, rows), rows)
        back = pltpu.make_async_copy(source, out.at[goal, :], out_sems.at[at])

        @pl.when(jnp.logical_and(place >= 0, place < groups))
        def _():
            if part == 0:
                into.start()
            elif part == 2:
                back.wait()
            else:
                into.wait()
                if ready is held:
                    segs = rows // SEG
                    for seg in range(segs):
                        near = held[slot, seg * SEG : seg * SEG + 16, :]
                        top = tops[pl.ds(place * segs + seg, 1), :].astype(held.dtype)
                        held[slot, seg * SEG : seg * SEG + 16, :] = jnp.where(row == 0, top, near)
                else:
                    ready[slot] = held[slot].astype(ready.dtype)
                back.start()

    for part in range(3):
        for at, step in enumerate(steps_of(groups)):
            take(at, step, part)


def steps_of(groups):
    return [0] + [-step for step in range(1, groups)] + [step for step in range(1, groups)]


def same_kernel(groups, mp_at, info, *refs):
    refs = list(refs)
    refs.insert(len(refs) - 2, refs[-3])
    spread_kernel(groups, mp_at, info, *refs)


def rows_of(block, width):
    return pl.BlockSpec((block, width), lambda i, c: (i, 0))


def load_own(section, source, target, sems):
    base, size = section
    copies = []
    for at in range(source.shape[0]):
        copy = pltpu.make_async_copy(
            source.at[at, pl.ds(base, size), :], target.at[pl.ds(at * size, size), :], sems.at[at]
        )
        copy.start()
        copies.append(copy)
    return copies


def own_out(stage, w_out, count):
    share = (w_out.shape[0] - HEAD_DIM) // count
    step = stage.shape[0] // count
    parts = [stage[at * step : (at + 1) * step, :].astype(FULL)[:share] for at in range(count)]
    parts.append(jnp.zeros((HEAD_DIM, stage.shape[1]), FULL))
    w_out[...] = jnp.concatenate(parts, axis=0).astype(LOW)


def ring_sum(plan, info, ring, total):
    for at, member in enumerate(ring):
        total[info[plan.mp_at + at]] = member[...].astype(FULL)
    found = total[0]
    for at in range(1, plan.groups):
        found = found + total[at]
    return found


def own_pairs(triple, here, live, low):
    zero = jnp.zeros((NSEG, LANES), LOW)
    block = [triple[here, at * LANES : (at + 1) * LANES] for at in range(5)]
    last = turn(block[3].astype(FULL)).astype(LOW)
    found = []
    for query, key, value in (
        (block[0], block[1], block[2]),
        (jnp.where(low, block[3], zero), jnp.where(low, last, zero), jnp.where(low, block[4], zero)),
    ):
        query = query * LOW(HEAD_DIM ** (-0.5))
        keys, values = halves(key, low), halves(value, low)
        found.append((query, keys, values, soft(query, keys, live, NSEG)))
    return found


def second_one_kernel(plan, sections, info, *refs):
    ring, refs = refs[: plan.groups], refs[plan.groups :]
    position, live, in_all, out_all, term, entry, tok, triple, context = refs[:9]
    heads, w_in, w_out, stage, sems = refs[9:]
    rows = entry.shape[0]
    copies = load_own(sections[0], in_all, w_in, sems.at[0])
    outs = load_own(sections[1], out_all, stage, sems.at[1])
    slots = ring[0].shape[0]
    for at in range(plan.groups):
        goal = pl.multiple_of(info[plan.mp_at + at] * slots, slots)
        heads[pl.ds(goal, slots), :] = ring[at][...]
    docs = rows // NSEG
    entry[...] = heads[...] + jnp.concatenate([position[...]] * docs, axis=0)
    tok[...] = entry[...].astype(LOW)
    wait_all(copies)
    triple[...] = dot_nn(tok[...], w_in[:, : 5 * LANES]).astype(LOW)
    low = lax.broadcasted_iota(jnp.int32, (NSEG, LANES), 1) < HEAD_DIM
    for doc in range(docs):
        here = slice(doc * NSEG, (doc + 1) * NSEG)
        mask = live[doc : doc + 1, :] > 0.5
        for pair, (_, _, values, probs) in enumerate(own_pairs(triple, here, mask, low)):
            probs = jnp.concatenate([part.astype(LOW) for part in probs], axis=1)
            context[here, pair * LANES : (pair + 1) * LANES] = dot_nn(probs, values).astype(LOW)
    wait_all(outs)
    own_out(stage, w_out, plan.count)
    term[...] = dot_nn(context[...], w_out[...]).astype(LOW)


def second_two_kernel(plan, sections, info, *refs):
    ring, refs = refs[: plan.groups], refs[plan.groups :]
    entry, affine, b_up, up_all, down_all, term, resid, hid_low, expanded, active = refs[:10]
    total, w_up, w_down, sems = refs[10:]
    copies = load_own(sections[2], up_all, w_up, sems.at[0])
    downs = load_own(sections[3], down_all, w_down, sems.at[1])
    value = entry[...] + ring_sum(plan, info, ring, total) + affine[4:5, :]
    resid[...] = value
    hid_low[...] = (normal(value)[0] * affine[0:1, :] + affine[1:2, :]).astype(LOW)
    wait_all(copies)
    up = dot_nn(hid_low[...], w_up[...]) + b_up[...]
    expanded[...] = up
    active[...] = (0.5 * up * (1.0 + jnp.tanh(TANH_A * (up + TANH_B * up * up * up)))).astype(LOW)
    wait_all(downs)
    term[...] = dot_nn(active[...], w_down[...]).astype(LOW)


def second_three_kernel(plan, sections, info, *refs):
    ring, refs = refs[: plan.groups], refs[plan.groups :]
    resid, expanded, top_grad, affine, up_all, down_all = refs[:6]
    term, second, back_two, grad_ret, grad_exp, sums, bias = refs[6:13]
    total, w_up, w_down, sems = refs[13:]
    copies = load_own(sections[3], down_all, w_down, sems.at[0])
    ups = load_own(sections[2], up_all, w_up, sems.at[1])
    hidden = normal(resid[...])[0] * affine[0:1, :] + affine[1:2, :]
    unit, scale = normal(hidden + ring_sum(plan, info, ring, total) + affine[5:6, :])
    second[...] = unit * affine[2:3, :] + affine[3:4, :]
    grad = top_grad[...]
    back = normal_back(grad, unit, scale, affine[2:3, :])
    back_two[...] = back
    sums[...] = jnp.zeros_like(sums)
    sums[2:3, :] = jnp.sum(grad * unit, axis=0, keepdims=True)
    sums[3:4, :] = jnp.sum(grad, axis=0, keepdims=True)
    sums[5:6, :] = jnp.sum(back, axis=0, keepdims=True)
    grad_ret[...] = back.astype(LOW)
    wait_all(copies)
    given = dot_nt(grad_ret[...], w_down[...])
    up = expanded[...]
    square = up * up
    curve = jnp.tanh(TANH_A * (up + TANH_B * up * square))
    half = 0.5 * (1.0 + curve)
    slope = half + 0.5 * up * (1.0 - curve * curve) * (TANH_A + 3.0 * TANH_A * TANH_B * square)
    wide = slope * given
    bias[...] = jnp.sum(wide, axis=0, keepdims=True)
    grad_exp[...] = wide.astype(LOW)
    wait_all(ups)
    term[...] = dot_nt(grad_exp[...], w_up[...]).astype(LOW)


def second_four_kernel(plan, sections, info, *refs):
    ring, refs = refs[: plan.groups], refs[plan.groups :]
    resid, back_two, triple, live, sums_in, affine, in_all, out_all = refs[:8]
    term, back_one, grad_mixed, grad_triple, sums = refs[8:13]
    total, w_in, w_out, stage, sems = refs[13:]
    outs = load_own(sections[1], out_all, stage, sems.at[0])
    copies = load_own(sections[0], in_all, w_in, sems.at[1])
    rows = resid.shape[0]
    grad = back_two[...] + ring_sum(plan, info, ring, total)
    unit, scale = normal(resid[...])
    back = normal_back(grad, unit, scale, affine[0:1, :])
    back_one[...] = back
    sums[...] = sums_in[...]
    sums[0:1, :] = jnp.sum(grad * unit, axis=0, keepdims=True)
    sums[1:2, :] = jnp.sum(grad, axis=0, keepdims=True)
    sums[4:5, :] = jnp.sum(back, axis=0, keepdims=True)
    grad_mixed[...] = back.astype(LOW)
    wait_all(outs)
    own_out(stage, w_out, plan.count)
    grad_ctx = dot_nt(grad_mixed[...], w_out[...]).astype(LOW)
    low = lax.broadcasted_iota(jnp.int32, (NSEG, LANES), 1) < HEAD_DIM
    for doc in range(rows // NSEG):
        here = slice(doc * NSEG, (doc + 1) * NSEG)
        mask = live[doc : doc + 1, :] > 0.5
        found = []
        for pair, (query, keys, values, probs) in enumerate(own_pairs(triple, here, mask, low)):
            down = grad_ctx[here, pair * LANES : (pair + 1) * LANES]
            found.append(pair_back(query, keys, values, probs, down, low, NSEG))
        blocks = list(found[0])
        blocks.append(jnp.where(low, found[1][0], turn(found[1][1])))
        blocks.append(jnp.where(low, found[1][2], 0.0))
        for at, block in enumerate(blocks):
            grad_triple[here, at * LANES : (at + 1) * LANES] = block.astype(LOW)
    wait_all(copies)
    term[...] = dot_nt(grad_triple[...], w_in[:, : 5 * LANES]).astype(LOW)


def second_grad_kernel(plan, info, tok, grad_triple, context, grad_mixed, hid_low, grad_exp, active, grad_ret, out):
    width = tok.shape[1]
    count, size = out.shape[0], plan.rows
    step = padded(size)
    share = width // plan.groups // count
    for kind, (left, right) in enumerate(
        ((tok, grad_triple), (hid_low, grad_exp), (active, grad_ret))
    ):
        value = dot_tn(left[...], right[...])
        if kind == 0:
            value = jnp.concatenate([value, jnp.zeros((width, LANES), FULL)], axis=1)
        for at in range(count):
            out[at, kind * step : kind * step + size, :] = value[at * size : (at + 1) * size].astype(LOW)
    value = dot_tn(context[...], grad_mixed[...])
    rest = out.shape[1] - 3 * step - share
    for at in range(count):
        rows = [value[at * share : (at + 1) * share]]
        if rest:
            rows.append(jnp.zeros((rest, width), FULL))
        out[at, 3 * step :, :] = jnp.concatenate(rows, axis=0).astype(LOW)


def collect_kernel(plan, info, *refs):
    count = plan.groups - 1
    unit_own, unit_ring, refs = refs[0], refs[1 : plan.groups], refs[plan.groups :]
    left, right, head_ring, refs = refs[0], refs[1], refs[2 : 2 + count], refs[2 + count :]
    second, unit_sum, head_sum, squares = refs
    total = unit_own[0].astype(FULL)
    for member in unit_ring:
        total = total + member[...].astype(FULL)
    unit_sum[...] = total
    heads = left[0].astype(FULL) + right[0].astype(FULL)
    for member in head_ring:
        heads = heads + member[...].astype(FULL)
    head_sum[...] = heads
    leader = jnp.where(info[plan.mp_at] == 0, 1.0, 0.0)
    step = padded(plan.rows)
    row = lax.broadcasted_iota(jnp.int32, (8, total.shape[1]), 0)
    lane = lax.broadcasted_iota(jnp.int32, (8, total.shape[1]), 1)
    once = jnp.logical_and(row >= 6, lane < LANES)

    def square(value):
        return jnp.sum(jnp.sum(value * value, axis=0, keepdims=True), axis=1, keepdims=True)

    small = total[2 * step : 2 * step + 8]
    found = square(total[: 2 * step]) + square(total[2 * step + 8 :])
    found = found + square(jnp.where(once, small, small * leader))
    found = found + square(heads) + square(second[...].astype(FULL))
    squares[...] = jnp.broadcast_to(found, squares.shape)


def update_kernel(plan, info, squares, unit_sum, head_sum, second, *refs):
    states, news, norm = refs[:7], refs[7:28], refs[28]
    total = squares[...]
    norm[...] = jnp.sqrt(total)
    factor = jnp.minimum(1.0, clip_level / jnp.sqrt(total[0:1, 0:1]))
    size, step = plan.rows, padded(plan.rows)
    share = states[1].shape[2]

    def put(kind, where, grad):
        state = states[kind]
        old = [state[(at, *where)] for at in range(3)]
        for at, value in enumerate(adam(old, grad, factor)):
            news[7 * at + kind][where] = value

    def columns(block):
        at = [block[:, i * HEAD_DIM : (i + 1) * HEAD_DIM] for i in range(9)]
        return jnp.concatenate([at[i] for i in (0, 2, 4, 1, 3, 5, 6, 7, 8)], axis=1)

    every = slice(None)
    put(0, (0, every, every), columns(head_sum[...]))
    put(0, (1, every, every), columns(second[:size, :].astype(FULL)))
    put(1, (0, every, every), unit_sum[2 * step + 8 : 2 * step + 8 + share, :])
    put(1, (1, every, every), second[3 * step : 3 * step + share, :].astype(FULL))
    put(2, (0, every, every), unit_sum[step : step + size, :])
    put(2, (1, every, every), second[step : step + size, :].astype(FULL))
    put(4, (0, every, every), unit_sum[:size, :])
    put(4, (1, every, every), second[2 * step : 2 * step + size, :].astype(FULL))
    small = unit_sum[2 * step : 2 * step + 8, :]
    put(3, (every, every), small[6:8, :size])
    put(5, (0, every, every), small[0:6, :size])
    put(5, (1, every, every), small[0:6, LANES : LANES + size])
    for block in range(NSEG // 8):
        goal = (block + 2) * LANES
        put(6, (slice(block * 8, (block + 1) * 8), every), small[:, goal : goal + size])


def own_rows(plan, rows, block, width):
    return pl.BlockSpec((block, width), lambda i, c: (c[plan.mp_at] * (rows // block) + i, 0))


WHOLE = pl.BlockSpec(memory_space=pltpu.VMEM)
OUTSIDE = pl.BlockSpec(memory_space=pl.ANY)


def shape(*dims, kind=LOW):
    return jax.ShapeDtypeStruct(dims, kind)


def run(kernel, steps, ins, outs, scratch, micros, info, args):
    return pl.pallas_call(
        kernel,
        grid_spec=pltpu.PrefetchScalarGridSpec(
            num_scalar_prefetch=1,
            grid=(steps,),
            in_specs=ins,
            out_specs=[spec for spec, _ in outs],
            scratch_shapes=scratch,
        ),
        out_shape=[kind for _, kind in outs],
        compiler_params=pltpu.CompilerParams(vmem_limit_bytes=VMEM_BYTES),
        cost_estimate=pl.CostEstimate(
            flops=int(micros * FLOPS), bytes_accessed=1024, transcendentals=0
        ),
    )(info, *args)


def layer_of(state, layer):
    return pl.BlockSpec((1, 1, *state.shape[2:]), lambda i, c: (0, layer, 0, 0))


def heads_block_of(info, attend_in, bias, affine, position):
    return run(
        heads_block_kernel,
        1,
        [layer_of(attend_in, 0), WHOLE, WHOLE, WHOLE],
        [(WHOLE, shape(attend_in.shape[2], 5 * LANES))],
        [pltpu.VMEM((LANES, LANES), FULL)],
        2,
        info,
        (attend_in, bias, affine, position),
    )[0]


def units_block_of(info, layer, states):
    rows = sum(padded(state.shape[2]) for state in states)
    return run(
        units_block_kernel,
        1,
        [layer_of(state, layer) for state in states],
        [(WHOLE, shape(rows, states[-1].shape[3]))],
        [],
        2,
        info,
        states,
    )[0]


def attend_forward(plan, info, tok, pieces, block=512):
    rows, width = tok.shape[0] // plan.groups, tok.shape[1]
    lanes = pieces[0].shape[-1]
    wide = rows_of(block, 3 * width)
    return run(
        functools.partial(attend_kernel, plan),
        rows // block,
        [own_rows(plan, rows, block, width)] + [OUTSIDE] * len(pieces),
        [
            (wide, shape(rows, 3 * width)),
            (rows_of(block, width), shape(rows, width)),
            (WHOLE, shape(width, 3 * width)),
            (WHOLE, shape(8, width, kind=FULL)),
            (WHOLE, shape(8, width, kind=FULL)),
            (WHOLE, shape(NSEG, width, kind=FULL)),
            (WHOLE, shape(1, plan.groups * width, kind=FULL)),
        ],
        [
            pltpu.VMEM((plan.groups, width, lanes), LOW),
            pltpu.SemaphoreType.DMA((plan.copies(),)),
        ],
        18,
        info,
        (tok, *pieces),
    )


def feed_forward(plan, sections, info, tok, context, affine, b_up, weights, block=256):
    rows, width = context.shape
    units = b_up.shape[1]
    line = rows_of(block, width)
    pieces = plan.groups * weights[0].shape[1]
    return run(
        functools.partial(feed_kernel, plan, sections),
        rows // block,
        [own_rows(plan, rows, block, width), line, WHOLE, WHOLE] + [OUTSIDE] * 3,
        [
            (line, shape(rows, width, kind=FULL)),
            (line, shape(rows, width)),
            (rows_of(block, units), shape(rows, units)),
            (line, shape(rows, width, kind=FULL)),
            (line, shape(rows, width)),
            (WHOLE, shape(rows // SEG, width, kind=FULL)),
            (WHOLE, shape(width, width)),
        ],
        [
            pltpu.VMEM((width, units), LOW),
            pltpu.VMEM((units, width), LOW),
            pltpu.VMEM((plan.groups, weights[2].shape[1] * sections[2][1], width), LOW),
            pltpu.SemaphoreType.DMA((2, pieces)),
            pltpu.SemaphoreType.DMA((pieces,)),
        ],
        24,
        info,
        (tok, context, affine, b_up, *weights),
    )


def feed_backward(plan, sections, info, cot, back_heads, ring, resid_two, expanded, resid, affine, weights, block=256):
    rows, width = resid.shape
    units = expanded.shape[1]
    line, wide = rows_of(block, width), rows_of(block, units)
    return run(
        functools.partial(feed_back_kernel, plan, sections),
        rows // block,
        [own_rows(plan, rows, block, width), WHOLE, line, wide, line, WHOLE]
        + [WHOLE] * plan.groups
        + [OUTSIDE] * 2,
        [
            (line, shape(rows, width, kind=FULL)),
            (wide, shape(rows, units)),
            (wide, shape(rows, units)),
            (line, shape(rows, width)),
            (line, shape(rows, width)),
            (WHOLE, shape(8, width, kind=FULL)),
            (WHOLE, shape(1, units, kind=FULL)),
            (WHOLE, shape(*back_heads.shape, kind=FULL)),
        ],
        [
            pltpu.VMEM((width, units), LOW),
            pltpu.VMEM((units, width), LOW),
            pltpu.SemaphoreType.DMA((2, plan.groups * weights[0].shape[1])),
        ],
        28,
        info,
        (cot, back_heads, resid_two, expanded, resid, affine, *ring, *weights[:2]),
    )


def attend_backward(info, grad_resid, grad_mixed, triple, w_out, w_in, early, block=256):
    rows, width = grad_resid.shape
    line, wide = rows_of(block, width), rows_of(block, 3 * width)
    return run(
        attend_back_kernel,
        rows // block,
        [line, line, wide, WHOLE, WHOLE, OUTSIDE],
        [(line, shape(rows, width)), (wide, shape(rows, 3 * width))],
        [pltpu.VMEM((block, width), LOW)],
        36,
        info,
        (grad_resid, grad_mixed, triple, w_out, w_in, early),
    )


def second_run(kernel, plan, sections, info, ring, args, weights, outs, scratch):
    count = weights[0].shape[0]
    return run(
        functools.partial(kernel, plan, sections),
        1,
        [WHOLE] * (len(ring) + len(args)) + [OUTSIDE] * len(weights),
        [(WHOLE, kind) for kind in outs],
        scratch + [pltpu.SemaphoreType.DMA((2, count))],
        5,
        info,
        (*ring, *args, *weights),
    )


def second_layer(sections, plan, info, ring, position, live, top_grad, affine, b_up, weights):
    rows, width = top_grad.shape
    groups = plan.groups
    in_all, out_all, up_all, down_all = weights
    own = width // groups
    tall = out_all.shape[0] * sections[1][1]
    full, low = shape(rows, width, kind=FULL), shape(rows, width)
    mixed = shape(rows, 5 * LANES)
    total = pltpu.VMEM((groups, rows, width), FULL)
    square = pltpu.VMEM((width, width), LOW)
    outer = [pltpu.VMEM((own + HEAD_DIM, width), LOW), pltpu.VMEM((tall, width), LOW)]

    term, entry, tok, triple, context = second_run(
        second_one_kernel, plan, sections, info, ring, (position, live), (in_all, out_all),
        [low, full, low, mixed, shape(rows, own + HEAD_DIM)],
        [pltpu.VMEM((rows, width), FULL), square] + outer,
    )
    term, resid, hid_low, expanded, active = second_run(
        second_two_kernel, plan, sections, info, around(term), (entry, affine, b_up), (up_all, down_all),
        [low, full, low, full, low],
        [total, square, square],
    )
    term, second, back_two, grad_ret, grad_exp, sums, bias = second_run(
        second_three_kernel, plan, sections, info, around(term), (resid, expanded, top_grad, affine), (up_all, down_all),
        [low, full, full, low, low, shape(8, width, kind=FULL), shape(1, width, kind=FULL)],
        [total, square, square],
    )
    term, back_one, grad_mixed, grad_triple, sums = second_run(
        second_four_kernel, plan, sections, info, around(term),
        (resid, back_two, triple, live, sums, affine), (in_all, out_all),
        [low, full, low, mixed, shape(8, width, kind=FULL)],
        [total, square] + outer,
    )
    saved = (tok, grad_triple, context, grad_mixed, hid_low, grad_exp, active, grad_ret)
    return second, back_one, around(term), sums, bias, saved


def second_grads_of(plan, count, info, saved):
    width = saved[0].shape[1]
    size = 3 * padded(plan.rows) + padded(width // plan.groups // count)
    return run(
        functools.partial(second_grad_kernel, plan),
        1,
        [WHOLE] * len(saved),
        [(WHOLE, shape(count, size, width))],
        [],
        5,
        info,
        saved,
    )[0]


def spread_out(groups, mp_at, info, line, tops, early, kind):
    count = len(line)
    rows, width = line[0].shape
    held = [pltpu.VMEM((groups, rows, width), line[0].dtype)]
    if tops is None:
        tops = jnp.zeros((8, width), FULL)
        held.append(pltpu.VMEM((groups, rows, width), kind))
        kernel = spread_kernel
    else:
        kernel = same_kernel
    return run(
        functools.partial(kernel, groups, mp_at),
        1,
        [OUTSIDE] * count + [WHOLE, OUTSIDE],
        [(OUTSIDE, shape(groups * rows, width, kind=kind))],
        held + [pltpu.SemaphoreType.DMA((count,)), pltpu.SemaphoreType.DMA((count,))],
        7,
        info,
        (*line, tops, early),
    )[0]


def unit_grads(plan, info, active, grad_ret, hid_low, grad_exp, context, grad_mixed, small, early):
    rows, width = grad_ret.shape
    fixed = pl.BlockSpec((rows, width), lambda m, c: (0, 0))
    moving = pl.BlockSpec((rows, width), lambda m, c: (0, c[plan.mp_at + m]))
    size = 2 * padded(plan.rows) + padded(width // plan.groups // plan.count + 8)
    out = pl.BlockSpec((plan.count, 1, size, width), lambda m, c: (0, m, 0, 0))
    square = pltpu.VMEM((width, width), FULL)
    return run(
        functools.partial(unit_grad_kernel, plan),
        plan.groups,
        [moving, fixed, fixed, moving, fixed, fixed] + [WHOLE] * len(small) + [OUTSIDE],
        [(out, shape(plan.count, plan.groups, size, width))],
        [square, square, pltpu.VMEM((width // LANES * 8, width), FULL)],
        19,
        info,
        (active, grad_ret, hid_low, grad_exp, context, grad_mixed, *small, early),
    )[0]


def collect(plan, info, unit_own, unit_ring, head_own, head_ring, second):
    return run(
        functools.partial(collect_kernel, plan),
        1,
        [WHOLE] * (4 + len(unit_ring) + len(head_ring)),
        [
            (WHOLE, shape(*unit_ring[0].shape, kind=FULL)),
            (WHOLE, shape(*head_ring[0].shape, kind=FULL)),
            (WHOLE, shape(8, LANES, kind=FULL)),
        ],
        [],
        4,
        info,
        (unit_own, *unit_ring, *head_own, *head_ring, second),
    )


def update(plan, info, squares, unit_sum, head_sum, second, states):
    outs = [(WHOLE, shape(*state.shape[1:], kind=FULL)) for _ in range(3) for state in states]
    return run(
        functools.partial(update_kernel, plan),
        1,
        [WHOLE] * (4 + len(states)),
        outs + [(WHOLE, shape(8, LANES, kind=FULL))],
        [],
        7,
        info,
        (squares, unit_sum, head_sum, second, *states),
    )


def head_grads(plan, lists, info, tok, grad_triple, early):
    rows, width = grad_triple.shape[0], tok.shape[1]
    out = shape(len(lists[0]), plan.groups // 2, plan.rows, 5 * LANES)
    return run(
        functools.partial(head_grad_kernel, plan, lists),
        1,
        [own_rows(plan, rows, rows, width), WHOLE, OUTSIDE],
        [(WHOLE, out)] * 4,
        [pltpu.VMEM((width, 3 * width), FULL)],
        10,
        info,
        (tok, grad_triple, early),
    )


def swap(value, bit, axis="dp"):
    return lax.ppermute(value, axis, [(i, i ^ bit) for i in range(lax.axis_size(axis))])


def ahead(value, step):
    size = lax.axis_size("mp")
    return lax.ppermute(value, "mp", [(i, (i + step) % size) for i in range(size)])


def onward(value, step):
    size = lax.axis_size("mp")
    return lax.ppermute(
        value, "mp", [(i, i + step) for i in range(size) if 0 <= i + step < size]
    )


def all_sum(value, axes):
    for axis in axes:
        bit = 1
        while bit < lax.axis_size(axis):
            value = value + swap(value, bit, axis)
            bit *= 2
    return value


def around(value):
    return [value] + [ahead(value, step) for step in range(1, lax.axis_size("mp"))]


def bits_of(count):
    bits, bit = [], 2
    while bit < count:
        bits.append(bit)
        bit *= 2
    return bits


def tie(value, *first):
    return lax.optimization_barrier((value, first))[0]


def gather(ring, gates):
    half = len(ring) // 2
    bits = bits_of(lax.axis_size("dp"))
    held = [[([0], jnp.stack(ring[:half])[None])], [([0], jnp.stack(ring[half:])[None])]]
    arrived = []
    for stage in range(len(bits)):
        arrived.append([])
        for which, order in enumerate((bits, bits[::-1])):
            bit = order[stage]
            places = sum((member[0] for member in held[which]), [])
            block = [member[1] for member in held[which]]
            block = block[0] if len(block) == 1 else jnp.concatenate(block)
            if stage < len(gates):
                block = tie(block, *gates[stage])
            got = swap(block, bit)
            arrived[-1].append(got)
            held[which] = [(places, block), ([j ^ bit for j in places], got)]
    pieces = []
    for which in range(2):
        for places, block in held[which]:
            pieces.append((places, which, block))
            pieces.append(([j ^ 1 for j in places], which, swap(block, 1)))
    return pieces, arrived


def pick(stack, order, count):
    return jnp.concatenate(
        [lax.dynamic_slice_in_dim(stack, order[at], 1) for at in range(count)]
    )


def straighten(pieces, device):
    merged = []
    for which in range(2):
        mine = [member for member in pieces if member[1] == which]
        places = sum((member[0] for member in mine), [])
        block = jnp.concatenate([member[2] for member in mine])
        order = sorted(range(len(places)), key=lambda at: places[at])
        block = pick(jnp.stack([block[at] for at in order]), device ^ jnp.arange(len(places)), len(places))
        count, groups, rows, lanes = block.shape
        block = block.transpose(1, 0, 2, 3).reshape(1, groups, count * rows, lanes)
        merged.append(([0], which, block))
    return merged


def places_of(order):
    places = [0]
    for bit in reversed(order):
        places = places + [place | bit for place in places]
    return places


def add(left, right):
    return (left.astype(FULL) + right.astype(FULL)).astype(LOW)


def reduce_dp(keep, send, order, early):
    got = tie(swap(send, 1), *early)
    for bit in order:
        half = keep.shape[0] // 2
        out = swap(add(keep[half:], got[half:]), bit)
        keep, got = add(keep[:half], got[:half]), out
    return keep[0], got[0]


def adam(state, grad, factor):
    clipped = grad * factor
    first = beta_one * state[1] + (1.0 - beta_one) * clipped
    second = beta_two * state[2] + (1.0 - beta_two) * clipped * clipped
    fixed_first = first / (1.0 - beta_one**adam_step)
    fixed_second = second / (1.0 - beta_two**adam_step)
    master = state[0] - rate * (
        fixed_first / (jnp.sqrt(fixed_second) + adam_eps) + decay * state[0]
    )
    return (master, first, second)


def shards(
    tokens,
    cotangent,
    counts,
    attend_in,
    attend_out,
    expand_in,
    expand_bias,
    expand_out,
    affine_state,
    position_state,
):
    shards_dp, groups = lax.axis_size("dp"), lax.axis_size("mp")
    device, mine = lax.axis_index("dp"), lax.axis_index("mp")
    width = tokens.shape[1]
    slots = counts.size // groups
    piece = width // shards_dp
    share = attend_out.shape[2]
    before = (mine - jnp.arange(groups)) % groups
    info = jnp.concatenate(
        [
            lax.dynamic_slice_in_dim(counts.reshape(-1), mine * slots, slots),
            before,
            device ^ jnp.arange(shards_dp),
        ]
    ).astype(jnp.int32)
    bits = bits_of(shards_dp)
    lists = (places_of(bits), places_of(bits[::-1]))
    mp_at, dp_at = slots, slots + groups

    heads_block = heads_block_of(info, attend_in, expand_bias, affine_state, position_state)
    units_block = units_block_of(info, 0, (expand_in, expand_out, attend_out))
    second_block = units_block_of(info, 1, (attend_in, expand_in, expand_out, attend_out))
    units_all = lax.all_gather(units_block, ("mp", "dp"), axis=0)
    units_all = units_all.reshape(groups, shards_dp, -1, width)
    heads_pieces, _ = gather(around(heads_block), [])
    second_all = lax.all_gather(second_block, "dp", axis=0)

    step, low_share = padded(piece), padded(share)
    units_sections = [(0, piece), (step, piece), (2 * step, low_share)]
    units = [units_all] * 3
    sections = [(0, piece), (3 * step, low_share), (step, piece), (2 * step, piece)]
    weights = [second_all] * 4
    load_info = info
    if piece % 16:
        heads_pieces = straighten(heads_pieces, device)
        load_info = info.at[dp_at].set(0)
        units = [
            units_all[:, :, base : base + rows].reshape(groups, 1, shards_dp * rows, width)
            for base, rows in units_sections
        ]
        weights = [
            second_all[:, base : base + rows].reshape(1, shards_dp * rows, width)
            for base, rows in sections
        ]
        units_sections = [(0, shards_dp * rows) for _, rows in units_sections]
        sections = [(0, shards_dp * rows) for _, rows in sections]

    def plan_of(pieces, rows):
        places = [(member[0], member[1]) for member in pieces]
        return Plan(groups, places, rows, mp_at, dp_at, shards_dp)

    heads_plan = plan_of(heads_pieces, heads_pieces[0][2].shape[2])
    own_plan = plan_of([], piece)
    heads_pieces = [member[2] for member in heads_pieces]

    triple, context, w_in, affine_one, affine_two, position, b_up = attend_forward(
        heads_plan, load_info, tokens, heads_pieces
    )
    resid, hid_low, expanded, resid_two, first, tops, w_out = feed_forward(
        own_plan, units_sections, info, tokens, context, affine_one, b_up, units
    )

    keep_heads = (counts > 0).astype(FULL)
    live = jnp.concatenate([keep_heads, keep_heads], axis=1)
    keep_heads = keep_heads.reshape(-1, 1)
    top_grad = cotangent.reshape(-1, SEG, width)[:, 0].astype(FULL) * keep_heads
    tops_ring = around(tops)
    second, back_heads, heads_ring, sums_two, bias_two, saved = second_layer(
        sections, own_plan, info, tops_ring, position, live, top_grad, affine_two, affine_one[7:8], weights
    )
    first_later = tie(first, *heads_ring[1:])
    out_line = [(onward(first_later, 1), onward(first_later, -1))]
    grad_resid, active, grad_exp, grad_ret, grad_mixed, sums_one, bias, grad_heads = feed_backward(
        own_plan, units_sections, info, cotangent, back_heads, heads_ring, resid_two, expanded, resid, affine_one, units
    )
    second_grads = second_grads_of(own_plan, shards_dp, tie(info, sums_one), saved)
    second_share = lax.psum_scatter(second_grads, "dp", scatter_dimension=0)
    out_line.append((onward(out_line[0][0], 1), onward(out_line[0][1], -1)))
    grad_in, grad_triple = attend_backward(
        tie(info, *out_line[0]), grad_resid, grad_mixed, triple, w_out, w_in, active
    )
    out_line.append((onward(out_line[1][0], 1), onward(out_line[1][1], -1)))
    small = (sums_one, sums_two, grad_heads, bias, bias_two)
    unit_out = unit_grads(
        own_plan,
        tie(info, *out_line[1]),
        active,
        grad_ret,
        hid_low,
        grad_exp,
        context,
        grad_mixed,
        small,
        grad_in,
    )
    unit_terms = lax.psum_scatter(unit_out, "dp", scatter_dimension=0)
    keep_a, send_a, keep_b, send_b = head_grads(own_plan, lists, info, tokens, grad_triple, unit_out)

    def in_line(own, line):
        return [own] + [pair[0] for pair in line] + [pair[1] for pair in line]

    grad_later = tie(grad_in, keep_a, *out_line[2])
    grad_line = [(onward(grad_later, 1), onward(grad_later, -1))]
    left_a, right_a = reduce_dp(keep_a, send_a, bits, out_line[2])
    left_b, right_b = reduce_dp(keep_b, send_b, bits[::-1], out_line[2])
    terms = [(left_a[s], right_a[s]) for s in range(1, groups // 2)]
    terms += [(left_b[s], right_b[s]) for s in range(groups - groups // 2)]
    head_ring = [
        ahead(tie(add(*term), *grad_line[0]), -at - 1) for at, term in enumerate(terms)
    ]
    merged = spread_out(
        groups,
        mp_at,
        info,
        in_line(first, out_line),
        second * keep_heads,
        grad_line[0][0],
        LOW,
    )
    grad_line.append((onward(grad_line[0][0], 1), onward(grad_line[0][1], -1)))
    unit_ring = [
        ahead(tie(unit_terms[at], *grad_line[1]), -at) for at in range(1, groups)
    ]
    unit_sum, head_sum, squares = collect(
        own_plan, info, unit_terms, unit_ring, (left_a, right_a), head_ring, second_share
    )
    last = tie(grad_line[1], *unit_ring)
    grad_line.append((onward(last[0], 1), onward(last[1], -1)))
    squares = all_sum(squares, ("dp", "mp"))
    input_grad = spread_out(
        groups, mp_at, info, in_line(grad_in, grad_line), None, grad_triple, FULL
    )
    states = (
        attend_in,
        attend_out,
        expand_in,
        expand_bias,
        expand_out,
        affine_state,
        position_state,
    )
    *updated, norm = update(own_plan, info, squares, unit_sum, head_sum, second_share, states)
    return (merged, input_grad, norm[0, 0], *updated)


def solution(mesh):
    in_specs = (
        P("dp", None),
        P("dp", None),
        P("dp", None),
        P(None, None, "dp", "mp"),
        P(None, None, ("mp", "dp"), None),
        P(None, None, "dp", "mp"),
        P(None, None, ("mp", "dp")),
        P(None, None, ("mp", "dp"), None),
        P(None, None, None, "dp"),
        P(None, None, "dp"),
    )
    out_specs = (
        P("dp", None),
        P("dp", None),
        P(),
        P(None, "dp", "mp"),
        P(None, ("mp", "dp"), None),
        P(None, "dp", "mp"),
        P(None, ("mp", "dp")),
        P(None, ("mp", "dp"), None),
        P(None, None, "dp"),
        P(None, "dp"),
        P(None, "dp", "mp"),
        P(None, ("mp", "dp"), None),
        P(None, "dp", "mp"),
        P(None, ("mp", "dp")),
        P(None, ("mp", "dp"), None),
        P(None, None, "dp"),
        P(None, "dp"),
        P(None, "dp", "mp"),
        P(None, ("mp", "dp"), None),
        P(None, "dp", "mp"),
        P(None, ("mp", "dp")),
        P(None, ("mp", "dp"), None),
        P(None, None, "dp"),
        P(None, "dp"),
    )
    return jax.shard_map(shards, mesh=mesh, in_specs=in_specs, out_specs=out_specs, check_vma=False)
```

time: 2040 us -> 553 us (0.27)
  waiting for transfers between devices: 1400 us -> 217 us
  Pallas kernels: 0 us -> 195 us
  matrix products: 176 us -> 0 us
  other arithmetic: 180 us -> 7.03 us
  blocking collectives: 146 us -> 0 us
  local copies, waits for them, and re-layouts: 114 us -> 16.2 us
  starting transfers between devices: 1.16 us -> 92.9 us
    psum x4 -> x0, waiting for transfers between devices: 1190 us -> none  [the longest x1 391 us: forward(): lax.psum(matmul(activated, w_down).astype(jnp.bfloat16), 'mp')]
    pallas_call x0 -> x18, Pallas kernels: none -> 195 us  [run(): pl.pallas_call(kernel, grid_spec=pltpu.PrefetchScalarGridSpec(num_scalar_...]
    dot_general x40 -> x0, matrix products: 176 us -> none  [the longest x11 68.4 us: matmul(): return jnp.dot(left, right, preferred_element_type=jnp.float32)]
    ppermute x0 -> x55, waiting for transfers between devices: none -> 167 us  [the longest x12 70.6 us: onward(): lax.ppermute(value, 'mp', [(i, i + step) for i in range(size) if 0 <= i +...]
    reduce_sum x28 -> x0, other arithmetic: 127 us -> none  [the longest x5 37.4 us: layer_norm(): mean = jnp.mean(values, axis=-1, keepdims=True)]
    psum x5 -> x0, blocking collectives: 108 us -> none  [the longest x1 39.5 us: shards(): lax.psum(matrix_squares + leader * small_squares, ('dp', 'mp'))]
    ppermute x0 -> x55, starting transfers between devices: none -> 92.8 us  [the longest x24 38.2 us: ahead(): lax.ppermute(value, 'mp', [(i, (i + step) % size) for i in range(size)])]
    unnamed x19 -> x4, waiting for transfers between devices: 88.2 us -> 0.07 us
  transfers between devices with their start and end apart: 14 -> 59, of which waited for: 12 -> 34; matrix products, arithmetic and copies ran while one was open for 12% -> 3% of each run, Pallas kernels for 0% -> 26%
where the time goes in v2:
time: 553 us; the launch traced here: 543 us
  waiting for transfers between devices  217 us (39%)
  Pallas kernels  195 us (35%)
  starting transfers between devices  92.9 us (17%)
  local copies, waits for them, and re-layouts  16.2 us (3%)
  between operations  14.8 us (3%)
  other arithmetic  7.03 us (1%)
    pallas_call x18, Pallas kernels, run(): pl.pallas_call(kernel, grid_spec=pltpu.PrefetchScalarGridSpec(num_scalar_...  195 us
    ppermute x12, waiting for transfers between devices, onward(): lax.ppermute(value, 'mp', [(i, i + step) for i in range(size) if 0 <= i +...  70.6 us
    ppermute x19, waiting for transfers between devices, swap(): lax.ppermute(value, axis, [(i, i ^ bit) for i in range(lax.axis_size(axis...  69.9 us
    ppermute x24, starting transfers between devices, ahead(): lax.ppermute(value, 'mp', [(i, (i + step) % size) for i in range(size)])  38.2 us
    all_gather x1, waiting for transfers between devices, shards(): units_all = lax.all_gather(units_block, ('mp', 'dp'), axis=0)  34 us
    ppermute x12, starting transfers between devices, onward(): lax.ppermute(value, 'mp', [(i, i + step) for i in range(size) if 0 <= i +...  33 us
    ppermute x24, waiting for transfers between devices, ahead(): lax.ppermute(value, 'mp', [(i, (i + step) % size) for i in range(size)])  26.6 us
    ppermute x19, starting transfers between devices, swap(): lax.ppermute(value, axis, [(i, i ^ bit) for i in range(lax.axis_size(axis...  21.5 us
  transfers between devices with their start and end apart: 59, of which 34 were waited for; matrix products, arithmetic and copies ran while one was open for 3% of the time, Pallas kernels for 26%

profile of v2, /device:TPU:0, one launch (start us, length us, event | category | flops | bytes accessed | tf_op | source)
XLA Modules:
  0.0 543.2 jit_solution(2461344715914956486)
XLA Ops:
  23.1 8.2 %collective-permute-done.5 = bf16[96,640]{1,0:T(8,128)(2,1)S(1)} collective-permute-done((bf16[96,640]{1,0:T(8,128)(2,1)}, bf16[96,640]{1,0:T(8,128)(2,1)S(1)}, u32[]{:S(2)}, u32[]{:S(2)}) %collective-permute-start.5) | collective-permute-done | bytes 122912 | tf_op jit(solution)/shard_map/ppermute | solution.py:1099
  47.0 13.7 %collective-permute-done.9.refs_6_ = bf16[2,2,96,640]{3,2,1,0:T(8,128)(2,1)S(1)} collective-permute-done((bf16[2,2,96,640]{3,2,1,0:T(8,128)(2,1)S(1)}, bf16[2,2,96,640]{3,2,1,0:T(8,128)(2,1)S(1)}, u32[]{:S(2)}, u32[]{:S(2)}) %collective-permute-start.9) | collective-permute-done | bytes 491552 | tf_op jit(solution)/shard_map/ppermute | solution.py:1094
  64.1 18.9 %shard_map.290 = (bf16[1024,2304]{1,0:T(8,128)(2,1)}, bf16[1024,768]{1,0:T(8,128)(2,1)}, bf16[768,2304]{1,0:T(8,128)(2,1)}, f32[8,768]{1,0:T(8,128)}, f32[8,768]...) custom-call(s32[20]{0:T(128)} %pad_add_fusion.info, bf16[4096,768]{1,0:T(8,128)(2,1)} %tok.5, ...), custom_call_target="tpu_custom_call" | custom-call | flops 20700000256 | bytes 1024 | tf_op jit(solution)/shard_map/pallas_call | solution.py:788
  83.0 34.0 %all-gather.5.cloned.1.call-done = bf16[7168,768]{1,0:T(8,128)(2,1)} async-done(((bf16[224,768]{1,0:T(8,128)(2,1)}), bf16[7168,768]{1,0:T(8,128)(2,1)}) %all-gather.5.cloned.1.call-update) | async-done | bytes 11010064 | tf_op jit(solution)/shard_map/all_gather | solution.py:1244
  117.0 24.4 %shard_map.292 = (f32[1024,768]{1,0:T(8,128)}, bf16[1024,768]{1,0:T(8,128)(2,1)}, bf16[1024,3072]{1,0:T(8,128)(2,1)}, f32[1024,768]{1,0:T(8,128)}, bf16[1024,768...) custom-call(s32[20]{0:T(128)} %pad_add_fusion.info, bf16[4096,768]{1,0:T(8,128)(2,1)} %tok.5, ...), custom_call_target="tpu_custom_call" | custom-call | flops 27599998976 | bytes 1024 | tf_op jit(solution)/shard_map/pallas_call | solution.py:788
  146.9 6.7 %all-gather.7.cloned.1.call-done = bf16[2560,768]{1,0:T(8,128)(2,1)} async-done(((bf16[320,768]{1,0:T(8,128)(2,1)}), bf16[2560,768]{1,0:T(8,128)(2,1)}) %all-gather.7.cloned.1.call-update) | async-done | bytes 3932176 | tf_op jit(solution)/shard_map/all_gather | solution.py:1247
  181.5 5.0 shard_map.296
  194.4 5.2 shard_map.297
  211.7 27.7 %shard_map.298 = (f32[1024,768]{1,0:T(8,128)}, bf16[1024,3072]{1,0:T(8,128)(2,1)}, bf16[1024,3072]{1,0:T(8,128)(2,1)}, bf16[1024,768]{1,0:T(8,128)(2,1)}, bf16[1...) custom-call(s32[20]{0:T(128)} %pad_add_fusion.info, bf16[4096,768]{1,0:T(8,128)(2,1)} %cot.1, ...), custom_call_target="tpu_custom_call" | custom-call | flops 32199999488 | bytes 1024 | tf_op jit(solution)/shard_map/pallas_call | solution.py:788
  249.6 36.3 %shard_map.299 = (bf16[1024,768]{1,0:T(8,128)(2,1)}, bf16[1024,2304]{1,0:T(8,128)(2,1)}) custom-call(s32[20]{0:T(128)} %pad_add_fusion.info, f32[1024,768]{1,0:T(8,128)} %get-tuple-element.138.grad_resid, bf16[1024,768]{1,0:T(8,128)(2,1)} %get-tuple-element.139.grad_mixed, bf16[1024,2304]{1,0:T(8,128)(2,1)} %get-tuple-element.140.triple, ...), custom_call_target="tpu_custom_call" | custom-call | flops 41400000512 | bytes 1024 | tf_op jit(solution)/shard_map/pallas_call | solution.py:788
  285.9 18.4 %shard_map.300.early = bf16[8,4,224,768]{3,2,1,0:T(8,128)(2,1)} custom-call(s32[20]{0:T(128)} %pad_add_fusion.info, bf16[1024,3072]{1,0:T(8,128)(2,1)} %get-tuple-element.143.early.active, bf16[1024,768]{1,0:T(8,128)(2,1)} %get-tuple-element.147.grad_ret, bf16[1024,768]{1,0:T(8,128)(2,1)} %get-tuple-element.148.hid_low, ...), custom_call_target="tpu_custom_call" | custom-call | flops 21849999360 | bytes 1024 | tf_op jit(solution)/shard_map/pallas_call | solution.py:788
  315.3 11.3 %shard_map.301 = (bf16[4,2,96,640]{3,2,1,0:T(8,128)(2,1)}, bf16[4,2,96,640]{3,2,1,0:T(8,128)(2,1)}, bf16[4,2,96,640]{3,2,1,0:T(8,128)(2,1)}, bf16[4,2,96,640]{3,2,1,0:T(8,128)(2,1)}) custom-call(s32[20]{0:T(128)} %pad_add_fusion.info, bf16[4096,768]{1,0:T(8,128)(2,1)} %tok.5, bf16[1024,2304]{1,0:T(8,128)(2,1)} %get-tuple-element.145.grad_triple.refs_8_, ...), custom_call_target="tpu_custom_call" | custom-call | flops 11500000256 | bytes 1024 | tf_op jit(solution)/shard_map/pallas_call | solution.py:788
  326.6 16.0 %collective-permute-done.28.refs_3_ = bf16[1024,768]{1,0:T(8,128)(2,1)S(1)} collective-permute-done((bf16[1024,768]{1,0:T(8,128)(2,1)}, bf16[1024,768]{1,0:T(8,128)(2,1)S(1)}, u32[]{:S(2)}, u32[]{:S(2)}) %collective-permute-start.28) | collective-permute-done | bytes 1572896 | tf_op jit(solution)/shard_map/ppermute | solution.py:1104
  353.8 24.6 %collective-permute-done.32.refs_8_.refs_1_ = bf16[1024,768]{1,0:T(8,128)(2,1)} collective-permute-done((bf16[1024,768]{1,0:T(8,128)(2,1)S(1)}, bf16[1024,768]{1,0:T(8,128)(2,1)}, u32[]{:S(2)}, u32[]{:S(2)}) %collective-permute-start.32) | collective-permute-done | bytes 1572896 | tf_op jit(solution)/shard_map/ppermute | solution.py:1104
  378.4 5.6 %collective-permute-start.33 = (bf16[1024,768]{1,0:T(8,128)(2,1)}, bf16[1024,768]{1,0:T(8,128)(2,1)}, u32[]{:S(2)}, u32[]{:S(2)}) collective-permute-start(bf16[1024,768]{1,0:T(8,128)(2,1)} %collective-permute-done.32.refs_8_.refs_1_), channel_id=1, source_target_pairs={{0,1},{1,2},{2,3},{4,5},{5,6},{6,7},{8,9},{9,10},{10,11},{12,13},{... | collective-permute-start | bytes 4718600 | tf_op jit(solution)/shard_map/ppermute | solution.py:1104
  389.2 8.1 %collective-permute-done.46 = bf16[2,2,96,640]{3,2,1,0:T(8,128)(2,1)S(1)} collective-permute-done((bf16[2,2,96,640]{3,2,1,0:T(8,128)(2,1)S(1)}, bf16[2,2,96,640]{3,2,1,0:T(8,128)(2,1)S(1)}, u32[]{:S(2)}, u32[]{:S(2)}) %collective-permute-start.46) | collective-permute-done | bytes 491552 | tf_op jit(solution)/shard_map/ppermute | solution.py:1094
  407.4 8.3 %collective-permute-done.33.refs_2_ = bf16[1024,768]{1,0:T(8,128)(2,1)} collective-permute-done((bf16[1024,768]{1,0:T(8,128)(2,1)}, bf16[1024,768]{1,0:T(8,128)(2,1)}, u32[]{:S(2)}, u32[]{:S(2)}) %collective-permute-start.33) | collective-permute-done | bytes 1572896 | tf_op jit(solution)/shard_map/ppermute | solution.py:1104
  415.7 13.7 %collective-permute-done.35.refs_5_ = bf16[1024,768]{1,0:T(8,128)(2,1)} collective-permute-done((bf16[1024,768]{1,0:T(8,128)(2,1)}, bf16[1024,768]{1,0:T(8,128)(2,1)}, u32[]{:S(2)}, u32[]{:S(2)}) %collective-permute-start.35) | collective-permute-done | bytes 1572896 | tf_op jit(solution)/shard_map/ppermute | solution.py:1104
  437.3 9.4 %reduce-scatter.5.cloned.1.call-done = bf16[1,320,768]{2,1,0:T(8,128)(2,1)} async-done(((bf16[8,320,768]{2,1,0:T(8,128)(2,1)}), bf16[1,320,768]{2,1,0:T(8,128)(2,1)}) %reduce-scatter.5.cloned.1.call-update) | async-done | bytes 491536 | tf_op jit(solution)/shard_map/reduce_scatter | solution.py:1298
  446.7 6.3 %collective-permute-done.48.refs_7_ = bf16[96,640]{1,0:T(8,128)(2,1)S(1)} collective-permute-done((bf16[96,640]{1,0:T(8,128)(2,1)S(1)}, bf16[96,640]{1,0:T(8,128)(2,1)S(1)}, u32[]{:S(2)}, u32[]{:S(2)}) %collective-permute-start.48) | collective-permute-done | bytes 122912 | tf_op jit(solution)/shard_map/ppermute | solution.py:1099
  473.5 32.2 %collective-permute-done.53 = f32[8,128]{1,0:T(8,128)S(1)} collective-permute-done((f32[8,128]{1,0:T(8,128)S(1)}, f32[8,128]{1,0:T(8,128)S(1)}, u32[]{:S(2)}, u32[]{:S(2)}) %collective-permute-start.53) | collective-permute-done | bytes 4128 | tf_op jit(solution)/shard_map/ppermute | solution.py:1094
  506.9 6.7 %shard_map.302 = bf16[4096,768]{1,0:T(8,128)(2,1)} custom-call(s32[20]{0:T(128)} %pad_add_fusion.info, bf16[1024,768]{1,0:T(8,128)(2,1)} %get-tuple-element.131.refs_0_, bf16[1024,768]{1,0:T(8,128)(2,1)} %copy-done.9, bf16[1024,768]{1,0:T(8,128)(2,1)} %collective-permute-done.27.refs_2_, bf16[1024,768]{1,0:T(8,128)(2,1)} %copy-done.10, ...), custom_call_target="tpu_custom_call" | custom-call | flops 8049999872 | bytes 1024 | tf_op jit(solution)/shard_map/pallas_call | solution.py:788
  514.2 7.4 %shard_map.306 = (f32[2,96,576]{2,1,0:T(8,128)}, f32[2,24,768]{2,1,0:T(8,128)}, f32[2,96,768]{2,1,0:T(8,128)}, f32[2,96]{1,0:T(2,128)}, f32[2,96,768]{2,1,0:T(8,...) custom-call(s32[20]{0:T(128)} %pad_add_fusion.info, ...), custom_call_target="tpu_custom_call" | custom-call | flops 8049999872 | bytes 1024 | tf_op jit(solution)/shard_map/pallas_call | solution.py:788
  528.4 7.8 %shard_map.303 = f32[4096,768]{1,0:T(8,128)} custom-call(s32[20]{0:T(128)} %pad_add_fusion.info, bf16[1024,768]{1,0:T(8,128)(2,1)} %get-tuple-element.156.early.refs_0_, bf16[1024,768]{1,0:T(8,128)(2,1)} %collective-permute-done.32.refs_8_.refs_1_, bf16[1024,768]{1,0:T(8,128)(2,1)} %collective-permute-done.33.refs_2_, bf16[1024,768]{1,0:T(8,128)(2,1)} %copy-done.11, ...), custom_call_target="tpu_custom_call" | custom-call | flops 8049999872 | bytes 1024 | tf_op jit(solution)/shard_map/pallas_call | solution.py:788
  (230 shorter events, 172.3 us)
Async XLA Ops:
  7.2 109.8 %all-gather.5.cloned.1.call-start = ((), (), s32[]{:S(2)}) async-start(), calls=%async_computation.4 | async-start | bytes 11354112 | tf_op jit(solution)/shard_map/all_gather | solution.py:1244
  11.1 142.5 %all-gather.7.cloned.1.call-start = ((), (), s32[]{:S(2)}) async-start(), calls=%async_computation.5 | async-start | bytes 4423680 | tf_op jit(solution)/shard_map/all_gather | solution.py:1247
  13.9 392.2 %reduce-scatter.3.cloned.1.call-start = ((), (), s32[]{:S(2)}) async-start(), calls=%async_computation.2 | async-start | bytes 12386304 | tf_op jit(solution)/shard_map/reduce_scatter | solution.py:1317
  39.8 20.9 %collective-permute-start.9 = (bf16[2,2,96,640]{3,2,1,0:T(8,128)(2,1)S(1)}, bf16[2,2,96,640]{3,2,1,0:T(8,128)(2,1)S(1)}, u32[]{:S(2)}, u32[]{:S(2)}) collective-permute-start(bf16[2,2,96,640]{3,2,1,0:T(8,128)(2,1)S(1)} %pad_maximum_fusion.1.refs_4_), channel_id=1, source_target_pairs={{0,8},{4,12},{8,0},{12,4},{16,24},{20,28},{24,16},{28,20},{1,9},{5... | collective-permute-start | bytes 1474568 | tf_op jit(solution)/shard_map/ppermute | solution.py:1094
  207.4 32.0 %collective-permute-start.26 = (bf16[1024,768]{1,0:T(8,128)(2,1)S(1)}, bf16[1024,768]{1,0:T(8,128)(2,1)S(1)}, u32[]{:S(2)}, u32[]{:S(2)}) collective-permute-start(bf16[1024,768]{1,0:T(8,128)(2,1)S(1)} %copy-done.7), channel_id=1, source_target_pairs={{0,1},{1,2},{2,3},{4,5},{5,6},{6,7},{8,9},{9,10},{10,11},{12,13},{... | collective-permute-start | bytes 4718600 | tf_op jit(solution)/shard_map/ppermute | solution.py:1104
  210.4 33.3 %collective-permute-start.29 = (bf16[1024,768]{1,0:T(8,128)(2,1)S(1)}, bf16[1024,768]{1,0:T(8,128)(2,1)}, u32[]{:S(2)}, u32[]{:S(2)}) collective-permute-start(bf16[1024,768]{1,0:T(8,128)(2,1)S(1)} %copy-done.7), channel_id=1, source_target_pairs={{1,0},{2,1},{3,2},{5,4},{6,5},{7,6},{9,8},{10,9},{11,10},{13,12},{... | collective-permute-start | bytes 4718600 | tf_op jit(solution)/shard_map/ppermute | solution.py:1104
  243.7 42.2 %collective-permute-start.27 = (bf16[1024,768]{1,0:T(8,128)(2,1)S(1)}, bf16[1024,768]{1,0:T(8,128)(2,1)}, u32[]{:S(2)}, u32[]{:S(2)}) collective-permute-start(bf16[1024,768]{1,0:T(8,128)(2,1)S(1)} %collective-permute-done.26.refs_1_), channel_id=1, source_target_pairs={{0,1},{1,2},{2,3},{4,5},{5,6},{6,7},{8,9},{9,10},{10,11},{12,13},{... | collective-permute-start | bytes 4718600 | tf_op jit(solution)/shard_map/ppermute | solution.py:1104
  248.1 37.9 %collective-permute-start.30 = (bf16[1024,768]{1,0:T(8,128)(2,1)}, bf16[1024,768]{1,0:T(8,128)(2,1)}, u32[]{:S(2)}, u32[]{:S(2)}) collective-permute-start(bf16[1024,768]{1,0:T(8,128)(2,1)} %collective-permute-done.29.refs_4_), channel_id=1, source_target_pairs={{1,0},{2,1},{3,2},{5,4},{6,5},{7,6},{9,8},{10,9},{11,10},{13,12},{... | collective-permute-start | bytes 4718600 | tf_op jit(solution)/shard_map/ppermute | solution.py:1104
  304.3 142.3 %reduce-scatter.5.cloned.1.call-start = ((), (), s32[]{:S(2)}) async-start(), calls=%async_computation.3 | async-start | bytes 4423680 | tf_op jit(solution)/shard_map/reduce_scatter | solution.py:1298
  309.1 33.5 %collective-permute-start.28 = (bf16[1024,768]{1,0:T(8,128)(2,1)}, bf16[1024,768]{1,0:T(8,128)(2,1)S(1)}, u32[]{:S(2)}, u32[]{:S(2)}) collective-permute-start(bf16[1024,768]{1,0:T(8,128)(2,1)} %collective-permute-done.27.refs_2_), channel_id=1, source_target_pairs={{0,1},{1,2},{2,3},{4,5},{5,6},{6,7},{8,9},{9,10},{10,11},{12,13},{... | collective-permute-start | bytes 4718600 | tf_op jit(solution)/shard_map/ppermute | solution.py:1104
  313.8 32.6 %collective-permute-start.31 = (bf16[1024,768]{1,0:T(8,128)(2,1)}, bf16[1024,768]{1,0:T(8,128)(2,1)}, u32[]{:S(2)}, u32[]{:S(2)}) collective-permute-start(bf16[1024,768]{1,0:T(8,128)(2,1)} %collective-permute-done.30.refs_5_), channel_id=1, source_target_pairs={{1,0},{2,1},{3,2},{5,4},{6,5},{7,6},{9,8},{10,9},{11,10},{13,12},{... | collective-permute-start | bytes 4718600 | tf_op jit(solution)/shard_map/ppermute | solution.py:1104
  346.4 32.0 %collective-permute-start.32 = (bf16[1024,768]{1,0:T(8,128)(2,1)S(1)}, bf16[1024,768]{1,0:T(8,128)(2,1)}, u32[]{:S(2)}, u32[]{:S(2)}) collective-permute-start(bf16[1024,768]{1,0:T(8,128)(2,1)S(1)} %copy-done.8), channel_id=1, source_target_pairs={{0,1},{1,2},{2,3},{4,5},{5,6},{6,7},{8,9},{9,10},{10,11},{12,13},{... | collective-permute-start | bytes 4718600 | tf_op jit(solution)/shard_map/ppermute | solution.py:1104
  349.7 34.3 %collective-permute-start.34 = (bf16[1024,768]{1,0:T(8,128)(2,1)S(1)}, bf16[1024,768]{1,0:T(8,128)(2,1)}, u32[]{:S(2)}, u32[]{:S(2)}) collective-permute-start(bf16[1024,768]{1,0:T(8,128)(2,1)S(1)} %copy-done.8), channel_id=1, source_target_pairs={{1,0},{2,1},{3,2},{5,4},{6,5},{7,6},{9,8},{10,9},{11,10},{13,12},{... | collective-permute-start | bytes 4718600 | tf_op jit(solution)/shard_map/ppermute | solution.py:1104
  351.1 37.0 %collective-permute-start.41 = (bf16[4,2,96,640]{3,2,1,0:T(8,128)(2,1)}, bf16[4,2,96,640]{3,2,1,0:T(8,128)(2,1)S(1)}, u32[]{:S(2)}, u32[]{:S(2)}) collective-permute-start(bf16[4,2,96,640]{3,2,1,0:T(8,128)(2,1)} %get-tuple-element.162), channel_id=1, source_target_pairs={{0,4},{4,0},{8,12},{12,8},{16,20},{20,16},{24,28},{28,24},{1,5},{5... | collective-permute-start | bytes 2949128 | tf_op jit(solution)/shard_map/ppermute | solution.py:1094
  378.4 37.3 %collective-permute-start.33 = (bf16[1024,768]{1,0:T(8,128)(2,1)}, bf16[1024,768]{1,0:T(8,128)(2,1)}, u32[]{:S(2)}, u32[]{:S(2)}) collective-permute-start(bf16[1024,768]{1,0:T(8,128)(2,1)} %collective-permute-done.32.refs_8_.refs_1_), channel_id=1, source_target_pairs={{0,1},{1,2},{2,3},{4,5},{5,6},{6,7},{8,9},{9,10},{10,11},{12,13},{... | collective-permute-start | bytes 4718600 | tf_op jit(solution)/shard_map/ppermute | solution.py:1104
  384.1 45.3 %collective-permute-start.35 = (bf16[1024,768]{1,0:T(8,128)(2,1)}, bf16[1024,768]{1,0:T(8,128)(2,1)}, u32[]{:S(2)}, u32[]{:S(2)}) collective-permute-start(bf16[1024,768]{1,0:T(8,128)(2,1)} %collective-permute-done.34.refs_4_), channel_id=1, source_target_pairs={{1,0},{2,1},{3,2},{5,4},{6,5},{7,6},{9,8},{10,9},{11,10},{13,12},{... | collective-permute-start | bytes 4718600 | tf_op jit(solution)/shard_map/ppermute | solution.py:1104
  399.3 35.8 %collective-permute-start.43 = (bf16[1,2,96,640]{3,2,1,0:T(8,128)(2,1)S(1)}, bf16[1,2,96,640]{3,2,1,0:T(8,128)(2,1)S(1)}, u32[]{:S(2)}, u32[]{:S(2)}) collective-permute-start(bf16[1,2,96,640]{3,2,1,0:T(8,128)(2,1)S(1)} %get-tuple-element.261), channel_id=1, source_target_pairs={{0,16},{4,20},{8,24},{12,28},{16,0},{20,4},{24,8},{28,12},{1,17},{... | collective-permute-start | bytes 737288 | tf_op jit(solution)/shard_map/ppermute | solution.py:1094
  403.7 32.0 %collective-permute-start.49 = (bf16[96,640]{1,0:T(8,128)(2,1)S(1)}, bf16[96,640]{1,0:T(8,128)(2,1)S(1)}, u32[]{:S(2)}, u32[]{:S(2)}) collective-permute-start(bf16[96,640]{1,0:T(8,128)(2,1)S(1)} %get-tuple-element.169), channel_id=1, source_target_pairs={{0,1},{1,2},{2,3},{3,0},{4,5},{5,6},{6,7},{7,4},{8,9},{9,10},{10,1... | collective-permute-start | bytes 368648 | tf_op jit(solution)/shard_map/ppermute | solution.py:1099
  429.4 23.7 %collective-permute-start.38 = (bf16[224,768]{1,0:T(8,128)(2,1)S(1)}, bf16[224,768]{1,0:T(8,128)(2,1)S(1)}, u32[]{:S(2)}, u32[]{:S(2)}) collective-permute-start(bf16[224,768]{1,0:T(8,128)(2,1)S(1)} %get-tuple-element.159), channel_id=1, source_target_pairs={{0,1},{1,2},{2,3},{3,0},{4,5},{5,6},{6,7},{7,4},{8,9},{9,10},{10,1... | collective-permute-start | bytes 1032200 | tf_op jit(solution)/shard_map/ppermute | solution.py:1099
  432.7 20.4 %collective-permute-start.37 = (bf16[224,768]{1,0:T(8,128)(2,1)S(1)}, bf16[224,768]{1,0:T(8,128)(2,1)S(1)}, u32[]{:S(2)}, u32[]{:S(2)}) collective-permute-start(bf16[224,768]{1,0:T(8,128)(2,1)S(1)} %get-tuple-element.158), channel_id=1, source_target_pairs={{0,2},{1,3},{2,0},{3,1},{4,6},{5,7},{6,4},{7,5},{8,10},{9,11},{10,... | collective-permute-start | bytes 1032200 | tf_op jit(solution)/shard_map/ppermute | solution.py:1099
  432.7 20.4 %collective-permute-start.36 = (bf16[224,768]{1,0:T(8,128)(2,1)S(1)}, bf16[224,768]{1,0:T(8,128)(2,1)S(1)}, u32[]{:S(2)}, u32[]{:S(2)}) collective-permute-start(bf16[224,768]{1,0:T(8,128)(2,1)S(1)} %get-tuple-element.157), channel_id=1, source_target_pairs={{0,3},{1,0},{2,1},{3,2},{4,7},{5,4},{6,5},{7,6},{8,11},{9,8},{10,9... | collective-permute-start | bytes 1032200 | tf_op jit(solution)/shard_map/ppermute | solution.py:1099
  465.0 61.6 %collective-permute-start.39 = (bf16[1024,768]{1,0:T(8,128)(2,1)}, bf16[1024,768]{1,0:T(8,128)(2,1)S(1)}, u32[]{:S(2)}, u32[]{:S(2)}) collective-permute-start(bf16[1024,768]{1,0:T(8,128)(2,1)} %collective-permute-done.33.refs_2_), channel_id=1, source_target_pairs={{0,1},{1,2},{2,3},{4,5},{5,6},{6,7},{8,9},{9,10},{10,11},{12,13},{... | collective-permute-start | bytes 4718600 | tf_op jit(solution)/shard_map/ppermute | solution.py:1104
  468.8 57.8 %collective-permute-start.40 = (bf16[1024,768]{1,0:T(8,128)(2,1)}, bf16[1024,768]{1,0:T(8,128)(2,1)S(1)}, u32[]{:S(2)}, u32[]{:S(2)}) collective-permute-start(bf16[1024,768]{1,0:T(8,128)(2,1)} %collective-permute-done.35.refs_5_), channel_id=1, source_target_pairs={{1,0},{2,1},{3,2},{5,4},{6,5},{7,6},{9,8},{10,9},{11,10},{13,12},{... | collective-permute-start | bytes 4718600 | tf_op jit(solution)/shard_map/ppermute | solution.py:1104
  470.1 35.6 %collective-permute-start.53 = (f32[8,128]{1,0:T(8,128)S(1)}, f32[8,128]{1,0:T(8,128)S(1)}, u32[]{:S(2)}, u32[]{:S(2)}) collective-permute-start(f32[8,128]{1,0:T(8,128)S(1)} %add.79), channel_id=1, source_target_pairs={{0,1},{1,0},{2,3},{3,2},{4,5},{5,4},{6,7},{7,6},{8,9},{9,8},{10,11... | collective-permute-start | bytes 12296 | tf_op jit(solution)/shard_map/ppermute | solution.py:1094
  (76 other events, 709.5 us)
Sparse Core Ops, SparseCore 0:
  11.5 105.4 all-gather.4
  119.5 34.1 all-gather.6
  304.5 87.9 reduce-scatter.2
  396.4 50.2 reduce-scatter.4

commit v3 on v2

--- a/solution.py
+++ b/solution.py
@@ -79,7 +79,7 @@
         return sum(len(places) for places, _ in self.pieces) * (self.groups // 2)
 
 
-def fetch(plan, info, pieces, land, sems):
+def fetch(plan, info, pieces, land, sems, begin=True):
     size = plan.rows
     copies = []
     for (places, half), piece in zip(plan.pieces, pieces):
@@ -91,7 +91,8 @@
                     land(half * piece.shape[1] + inner, start, size),
                     sems.at[len(copies)],
                 )
-                copy.start()
+                if begin:
+                    copy.start()
                 copies.append(copy)
     return copies
 
@@ -109,24 +110,27 @@
     return jnp.concatenate([block[:, HEAD_DIM:], block[:, :HEAD_DIM]], axis=1)
 
 
-def fetch_units(sections, up_all, down_all, w_up, w_down, sems):
+def fetch_units(plan, section, info, pieces, down_all, w_up, w_down, sems, begin=True):
     width = w_down.shape[1]
+    base, size = section
+
+    def up(m, start, rows):
+        place = pl.multiple_of(info[plan.mp_at + m] * width, LANES)
+        return w_up.at[pl.ds(start, rows), pl.ds(place, width)]
+
+    ups = fetch(plan, info, pieces, up, sems.at[0], begin)
     copies = []
-    for kind, (source, (base, size)) in enumerate(zip((up_all, down_all), sections)):
-        for m in range(source.shape[0]):
-            for at in range(source.shape[1]):
-                if kind:
-                    target = w_down.at[pl.ds(m * width + at * size, size), :]
-                else:
-                    target = w_up.at[pl.ds(at * size, size), m * width : (m + 1) * width]
-                copy = pltpu.make_async_copy(
-                    source.at[m, at, pl.ds(base, size), :],
-                    target,
-                    sems.at[kind, m * source.shape[1] + at],
-                )
+    for m in range(down_all.shape[0]):
+        for at in range(down_all.shape[1]):
+            copy = pltpu.make_async_copy(
+                down_all.at[m, at, pl.ds(base, size), :],
+                w_down.at[pl.ds(m * width + at * size, size), :],
+                sems.at[1, m * down_all.shape[1] + at],
+            )
+            if begin:
                 copy.start()
-                copies.append(copy)
-    return copies
+            copies.append(copy)
+    return ups, copies
 
 
 def fetch_out(section, plan, info, out_all, stage, sems):
@@ -212,8 +216,8 @@
 
 
 def attend_kernel(plan, info, tok, *refs):
-    pieces, refs = refs[:-9], refs[-9:]
-    triple, context, w_in, affine_one, affine_two, position, b_up, stage, sems = refs
+    pieces, refs = refs[:-10], refs[-10:]
+    triple, context, chances, w_in, affine_one, affine_two, position, b_up, stage, sems = refs
     step = pl.program_id(0)
     rows, width = tok.shape
 
@@ -245,10 +249,12 @@
             keys = halves(triple[here, width + at : width + at + LANES], low)
             values = halves(triple[here, 2 * width + at : 2 * width + at + LANES], low)
             probs = jnp.concatenate([part.astype(LOW) for part in soft(query, keys, live, SEG)], axis=1)
+            chances[here, 2 * at : 2 * at + 2 * SEG] = probs
             context[here, at : at + LANES] = dot_nn(probs, values).astype(LOW)
 
 
-def feed_kernel(plan, sections, info, tok, context, affine, b_up, up_all, down_all, out_all, *refs):
+def feed_kernel(plan, sections, info, tok, context, affine, b_up, down_all, out_all, *refs):
+    pieces, refs = refs[: len(plan.pieces)], refs[len(plan.pieces) :]
     resid, hid_low, expanded, resid_two, first, tops, w_out, w_up, w_down, stage, sems, out_sems = refs
     step = pl.program_id(0)
     rows, width = tok.shape
@@ -256,11 +262,10 @@
 
     @pl.when(step == 0)
     def _():
-        outs = fetch_out(sections[2], plan, info, out_all, stage, out_sems)
-        copies = fetch_units(sections[:2], up_all, down_all, w_up, w_down, sems)
+        outs = fetch_out(sections[1], plan, info, out_all, stage, out_sems)
+        fetch_units(plan, sections[0], info, pieces, down_all, w_up, w_down, sems)
         wait_all(outs)
         pair_rows(stage, w_out, plan.count)
-        wait_all(copies)
 
     mixed = dot_nn(context[...], w_out[...])
     value = tok[...].astype(FULL) + mixed + affine[4:5, :]
@@ -271,6 +276,13 @@
     total = hidden + affine[5:6, :]
     units = w_up.shape[1]
     block = width
+
+    @pl.when(step == 0)
+    def _():
+        ups, downs = fetch_units(plan, sections[0], info, pieces, down_all, w_up, w_down, sems, False)
+        wait_all(ups)
+        wait_all(downs)
+
     for at in range(0, units, block):
         up = dot_nn(low, w_up[:, at : at + block]) + b_up[:, at : at + block]
         expanded[:, at : at + block] = up.astype(LOW)
@@ -289,29 +301,29 @@
 
 def feed_back_kernel(plan, sections, info, cot, back_heads, resid_two, expanded, resid, affine, *refs):
     ring, refs = refs[: plan.groups], refs[plan.groups :]
-    up_all, down_all, grad_resid, active, grad_exp, grad_ret, grad_mixed, sums, bias = refs[:9]
-    heads, w_up, w_down, sems = refs[9:]
+    pieces, refs = refs[: len(plan.pieces)], refs[len(plan.pieces) :]
+    down_all, grad_resid, active, grad_exp, grad_ret, grad_mixed, sums, bias = refs[:8]
+    heads, w_up, w_down, sems = refs[8:]
     step = pl.program_id(0)
     rows, width = cot.shape
     segs = rows // SEG
 
     @pl.when(step == 0)
     def _():
-        copies = fetch_units(sections[:2], up_all, down_all, w_up, w_down, sems)
+        fetch_units(plan, sections[0], info, pieces, down_all, w_up, w_down, sems)
         total = back_heads[...]
         for member in ring:
             total = total + member[...].astype(FULL)
         heads[...] = total
-        wait_all(copies)
 
     row = lax.broadcasted_iota(jnp.int32, (SEG, 1), 0)
     first = info[plan.mp_at] * (pl.num_programs(0) * segs) + step * segs
-    pieces = []
+    blocks = []
     for seg in range(segs):
         piece = cot[seg * SEG : (seg + 1) * SEG, :].astype(FULL)
         piece = jnp.where(row < info[step * segs + seg], piece, 0.0)
-        pieces.append(jnp.where(row == 0, heads[pl.ds(first + seg, 1), :], piece))
-    grad = jnp.concatenate(pieces, axis=0)
+        blocks.append(jnp.where(row == 0, heads[pl.ds(first + seg, 1), :], piece))
+    grad = jnp.concatenate(blocks, axis=0)
     unit, scale = normal(resid_two[...])
 
     @pl.when(step == 0)
@@ -328,6 +340,13 @@
     units = w_up.shape[1]
     total = back
     block = width
+
+    @pl.when(step == 0)
+    def _():
+        ups, downs = fetch_units(plan, sections[0], info, pieces, down_all, w_up, w_down, sems, False)
+        wait_all(downs)
+        wait_all(ups)
+
     for at in range(0, units, block):
         grad_act = dot_nt(low, w_down[at : at + block, :])
         up = expanded[:, at : at + block].astype(FULL)
@@ -368,37 +387,44 @@
     return grad_query, grad_key, jnp.where(low, both[:span], both[span:])
 
 
-def attend_back_kernel(info, grad_resid, grad_mixed, triple, w_out, w_in, early, grad_in, grad_triple, grad_ctx):
+def attend_back_kernel(info, grad_resid, grad_mixed, triple, chances, context, w_out, w_in, early, grad_in, grad_triple, grad_ctx):
     del early
-    step = pl.program_id(0)
     rows, width = grad_resid.shape
-    segs = rows // SEG
     grad_ctx[...] = dot_nt(grad_mixed[...], w_out[...]).astype(LOW)
     low = lax.broadcasted_iota(jnp.int32, (SEG, LANES), 1) < HEAD_DIM
-    spot = lax.broadcasted_iota(jnp.int32, (SEG, 2 * SEG), 1) % SEG
-    shrink = HEAD_DIM ** (-0.5)
-    for seg in range(segs):
-        live = spot < info[step * segs + seg]
+    for seg in range(rows // SEG):
         here = slice(seg * SEG, (seg + 1) * SEG)
         for pair in range(width // LANES):
             at = pair * LANES
-            query = triple[here, at : at + LANES] * LOW(shrink)
+            query = triple[here, at : at + LANES] * LOW(HEAD_DIM ** (-0.5))
             keys = halves(triple[here, width + at : width + at + LANES], low)
             values = halves(triple[here, 2 * width + at : 2 * width + at + LANES], low)
-            probs = soft(query, keys, live, SEG)
+            probs = chances[here, 2 * at : 2 * at + 2 * SEG]
             down = grad_ctx[here, at : at + LANES]
-            found = pair_back(query, keys, values, probs, down, low, SEG)
-            for part in range(3):
+            product = down.astype(FULL) * context[here, at : at + LANES].astype(FULL)
+            left = jnp.sum(jnp.where(low, product, 0.0), axis=-1, keepdims=True)
+            right = jnp.sum(jnp.where(low, 0.0, product), axis=-1, keepdims=True)
+            grad_probs = dot_nt(down, values)
+            scores = [grad_probs[:, :SEG] - left, grad_probs[:, SEG:] - right]
+            grad_scores = (probs.astype(FULL) * jnp.concatenate(scores, axis=1)).astype(LOW)
+            grad_query = dot_nn(grad_scores, keys) * HEAD_DIM ** (-0.5)
+            both = dot_tn(grad_scores, query)
+            grad_key = jnp.where(low, both[:SEG], both[SEG:])
+            both = dot_tn(probs, down)
+            grad_value = jnp.where(low, both[:SEG], both[SEG:])
+            for part, found in enumerate((grad_query, grad_key, grad_value)):
                 goal = part * width + at
-                grad_triple[here, goal : goal + LANES] = found[part].astype(LOW)
+                grad_triple[here, goal : goal + LANES] = found.astype(LOW)
     grad_in[...] = (grad_resid[...] + dot_nt(grad_triple[...], w_in[...])).astype(LOW)
 
 
 def unit_grad_kernel(
-    plan, info, active, grad_ret, hid_low, grad_exp, context, grad_mixed, sums_one, sums_two, grad_heads, bias, bias_two, early, out, whole, mixing, small
+    plan, info, active, grad_ret, hid_low, grad_exp, context, grad_mixed, sums_one, sums_two, grad_heads, bias, bias_two, *refs
 ):
-    del early
+    saved, (out, whole, mixing, small, second) = refs[:-5], refs[-5:]
     m = pl.program_id(0)
+    extra = second.shape[1] // plan.groups
+    rest_at = out.shape[2] - extra
     size = plan.rows
     width = whole.shape[0]
     third = width // plan.groups
@@ -406,12 +432,16 @@
 
     @pl.when(m == 0)
     def _():
+        second_grads_into(plan, *saved, second)
         found = dot_tn(context[...], grad_mixed[...])
         for at in range(plan.groups):
             mixing[at * third : at * third + LANES, :] = found[at * LANES : (at + 1) * LANES]
             goal = plan.groups * LANES + at * HEAD_DIM
             mixing[at * third + LANES : (at + 1) * third, :] = found[goal : goal + HEAD_DIM]
 
+    part = pl.ds(pl.multiple_of(m * extra, 16), extra)
+    for at in range(out.shape[0]):
+        out[at, 0, rest_at:, :] = second[at, part, :]
     step = padded(size)
     for kind, (left, right) in enumerate(((active, grad_ret), (hid_low, grad_exp))):
         whole[...] = dot_tn(left[...], right[...])
@@ -438,10 +468,10 @@
         for block in range(width // LANES):
             blocks += [lines[block * 8 : (block + 1) * 8], gap]
         rows = [jnp.concatenate(blocks, axis=1), mine[at * share : (at + 1) * share]]
-        rest = out.shape[2] - 2 * step - share - 8
+        rest = rest_at - 2 * step - share - 8
         if rest:
             rows.append(jnp.zeros((rest, width), FULL))
-        out[at, 0, 2 * step :, :] = jnp.concatenate(rows, axis=0).astype(LOW)
+        out[at, 0, 2 * step : rest_at, :] = jnp.concatenate(rows, axis=0).astype(LOW)
 
 
 def head_grad_kernel(plan, lists, info, tok, grad_triple, early, keep_a, send_a, keep_b, send_b, whole):
@@ -473,22 +503,36 @@
                     out[at, inner, :, 4 * LANES : 5 * LANES] = jnp.where(low, blocks[2], 0.0).astype(LOW)
 
 
-def spread_kernel(groups, mp_at, info, *refs):
-    line, (tops, _, out, held, ready, in_sems, out_sems) = refs[:-7], refs[-7:]
+def tops_kernel(info, tops, rows, out, held, in_sems, out_sems):
+    row = lax.broadcasted_iota(jnp.int32, (16, 1), 0)
+    parts = in_sems.shape[0]
+    segs = tops.shape[0] // parts
+    ins, outs = [], []
+    for part in range(parts):
+        where = pl.ds(part * segs * SEG, segs * SEG)
+        ins.append(pltpu.make_async_copy(rows.at[where, :], held.at[where, :], in_sems.at[part]))
+        outs.append(pltpu.make_async_copy(held.at[where, :], out.at[where, :], out_sems.at[part]))
+        ins[-1].start()
+    for part in range(parts):
+        ins[part].wait()
+        for seg in range(part * segs, (part + 1) * segs):
+            near = slice(seg * SEG, seg * SEG + 16)
+            held[near, :] = jnp.where(row == 0, tops[seg : seg + 1, :].astype(LOW), held[near, :])
+        outs[part].start()
+    wait_all(outs)
+
+
+def spread_kernel(groups, mp_at, steps, info, *refs):
+    count = len(steps)
+    line, (out, held, ready, in_sems, out_sems) = refs[:count], refs[-5:]
     rows = held.shape[1]
     mine = info[mp_at]
-    row = lax.broadcasted_iota(jnp.int32, (16, 1), 0)
 
     def take(at, step, part):
         place = mine + step
-        slot = step % groups
-        into = pltpu.make_async_copy(line[at], held.at[slot], in_sems.at[at])
-        if ready is held:
-            source = held.at[slot]
-        else:
-            source = ready.at[slot]
+        into = pltpu.make_async_copy(line[at], held.at[at], in_sems.at[at])
         goal = pl.ds(pl.multiple_of(place * rows, rows), rows)
-        back = pltpu.make_async_copy(source, out.at[goal, :], out_sems.at[at])
+        back = pltpu.make_async_copy(ready.at[at], out.at[goal, :], out_sems.at[at])
 
         @pl.when(jnp.logical_and(place >= 0, place < groups))
         def _():
@@ -498,29 +542,12 @@
                 back.wait()
             else:
                 into.wait()
-                if ready is held:
-                    segs = rows // SEG
-                    for seg in range(segs):
-                        near = held[slot, seg * SEG : seg * SEG + 16, :]
-                        top = tops[pl.ds(place * segs + seg, 1), :].astype(held.dtype)
-                        held[slot, seg * SEG : seg * SEG + 16, :] = jnp.where(row == 0, top, near)
-                else:
-                    ready[slot] = held[slot].astype(ready.dtype)
+                ready[at] = held[at].astype(ready.dtype)
                 back.start()
 
     for part in range(3):
-        for at, step in enumerate(steps_of(groups)):
+        for at, step in enumerate(steps):
             take(at, step, part)
-
-
-def steps_of(groups):
-    return [0] + [-step for step in range(1, groups)] + [step for step in range(1, groups)]
-
-
-def same_kernel(groups, mp_at, info, *refs):
-    refs = list(refs)
-    refs.insert(len(refs) - 2, refs[-3])
-    spread_kernel(groups, mp_at, info, *refs)
 
 
 def rows_of(block, width):
@@ -609,7 +636,7 @@
     resid[...] = value
     hid_low[...] = (normal(value)[0] * affine[0:1, :] + affine[1:2, :]).astype(LOW)
     wait_all(copies)
-    up = dot_nn(hid_low[...], w_up[...]) + b_up[...]
+    up = dot_nn(hid_low[...], w_up[...]) + b_up[7:8, :]
     expanded[...] = up
     active[...] = (0.5 * up * (1.0 + jnp.tanh(TANH_A * (up + TANH_B * up * up * up)))).astype(LOW)
     wait_all(downs)
@@ -685,9 +712,9 @@
     term[...] = dot_nt(grad_triple[...], w_in[:, : 5 * LANES]).astype(LOW)
 
 
-def second_grad_kernel(plan, info, tok, grad_triple, context, grad_mixed, hid_low, grad_exp, active, grad_ret, out):
+def second_grads_into(plan, tok, grad_triple, context, grad_mixed, hid_low, grad_exp, active, grad_ret, out):
     width = tok.shape[1]
-    count, size = out.shape[0], plan.rows
+    count, size = plan.count, plan.rows
     step = padded(size)
     share = width // plan.groups // count
     for kind, (left, right) in enumerate(
@@ -711,8 +738,12 @@
     count = plan.groups - 1
     unit_own, unit_ring, refs = refs[0], refs[1 : plan.groups], refs[plan.groups :]
     left, right, head_ring, refs = refs[0], refs[1], refs[2 : 2 + count], refs[2 + count :]
-    second, unit_sum, head_sum, squares = refs
-    total = unit_own[0].astype(FULL)
+    unit_sum, head_sum, second, squares = refs
+    tall = unit_sum.shape[0]
+    extra = unit_own.shape[1] - tall
+    for m in range(plan.groups):
+        second[m * extra : (m + 1) * extra, :] = unit_own[m, tall:, :].astype(FULL)
+    total = unit_own[0, :tall].astype(FULL)
     for member in unit_ring:
         total = total + member[...].astype(FULL)
     unit_sum[...] = total
@@ -732,7 +763,7 @@
     small = total[2 * step : 2 * step + 8]
     found = square(total[: 2 * step]) + square(total[2 * step + 8 :])
     found = found + square(jnp.where(once, small, small * leader))
-    found = found + square(heads) + square(second[...].astype(FULL))
+    found = found + square(heads) + square(second[...])
     squares[...] = jnp.broadcast_to(found, squares.shape)
 
 
@@ -756,13 +787,13 @@
 
     every = slice(None)
     put(0, (0, every, every), columns(head_sum[...]))
-    put(0, (1, every, every), columns(second[:size, :].astype(FULL)))
+    put(0, (1, every, every), columns(second[:size, :]))
     put(1, (0, every, every), unit_sum[2 * step + 8 : 2 * step + 8 + share, :])
-    put(1, (1, every, every), second[3 * step : 3 * step + share, :].astype(FULL))
+    put(1, (1, every, every), second[3 * step : 3 * step + share, :])
     put(2, (0, every, every), unit_sum[step : step + size, :])
-    put(2, (1, every, every), second[step : step + size, :].astype(FULL))
+    put(2, (1, every, every), second[step : step + size, :])
     put(4, (0, every, every), unit_sum[:size, :])
-    put(4, (1, every, every), second[2 * step : 2 * step + size, :].astype(FULL))
+    put(4, (1, every, every), second[2 * step : 2 * step + size, :])
     small = unit_sum[2 * step : 2 * step + 8, :]
     put(3, (every, every), small[6:8, :size])
     put(5, (0, every, every), small[0:6, :size])
@@ -784,7 +815,7 @@
     return jax.ShapeDtypeStruct(dims, kind)
 
 
-def run(kernel, steps, ins, outs, scratch, micros, info, args):
+def run(kernel, steps, ins, outs, scratch, micros, info, args, aliases=None):
     return pl.pallas_call(
         kernel,
         grid_spec=pltpu.PrefetchScalarGridSpec(
@@ -795,6 +826,7 @@
             scratch_shapes=scratch,
         ),
         out_shape=[kind for _, kind in outs],
+        input_output_aliases=aliases or {},
         compiler_params=pltpu.CompilerParams(vmem_limit_bytes=VMEM_BYTES),
         cost_estimate=pl.CostEstimate(
             flops=int(micros * FLOPS), bytes_accessed=1024, transcendentals=0
@@ -844,6 +876,7 @@
         [
             (wide, shape(rows, 3 * width)),
             (rows_of(block, width), shape(rows, width)),
+            (rows_of(block, 2 * width), shape(rows, 2 * width)),
             (WHOLE, shape(width, 3 * width)),
             (WHOLE, shape(8, width, kind=FULL)),
             (WHOLE, shape(8, width, kind=FULL)),
@@ -860,15 +893,16 @@
     )
 
 
-def feed_forward(plan, sections, info, tok, context, affine, b_up, weights, block=256):
+def feed_forward(plan, sections, info, tok, context, affine, b_up, pieces, weights, block=512):
     rows, width = context.shape
     units = b_up.shape[1]
     line = rows_of(block, width)
-    pieces = plan.groups * weights[0].shape[1]
+    downs = plan.groups * weights[0].shape[1]
     return run(
         functools.partial(feed_kernel, plan, sections),
         rows // block,
-        [own_rows(plan, rows, block, width), line, WHOLE, WHOLE] + [OUTSIDE] * 3,
+        [own_rows(plan, rows, block, width), line, WHOLE, WHOLE]
+        + [OUTSIDE] * (2 + len(pieces)),
         [
             (line, shape(rows, width, kind=FULL)),
             (line, shape(rows, width)),
@@ -881,17 +915,17 @@
         [
             pltpu.VMEM((width, units), LOW),
             pltpu.VMEM((units, width), LOW),
-            pltpu.VMEM((plan.groups, weights[2].shape[1] * sections[2][1], width), LOW),
-            pltpu.SemaphoreType.DMA((2, pieces)),
-            pltpu.SemaphoreType.DMA((pieces,)),
+            pltpu.VMEM((plan.groups, weights[1].shape[1] * sections[1][1], width), LOW),
+            pltpu.SemaphoreType.DMA((2, max(downs, plan.copies()))),
+            pltpu.SemaphoreType.DMA((downs,)),
         ],
         24,
         info,
-        (tok, context, affine, b_up, *weights),
-    )
-
-
-def feed_backward(plan, sections, info, cot, back_heads, ring, resid_two, expanded, resid, affine, weights, block=256):
+        (tok, context, affine, b_up, *weights, *pieces),
+    )
+
+
+def feed_backward(plan, sections, info, cot, back_heads, ring, resid_two, expanded, resid, affine, pieces, weights, block=256):
     rows, width = resid.shape
     units = expanded.shape[1]
     line, wide = rows_of(block, width), rows_of(block, units)
@@ -900,7 +934,7 @@
         rows // block,
         [own_rows(plan, rows, block, width), WHOLE, line, wide, line, WHOLE]
         + [WHOLE] * plan.groups
-        + [OUTSIDE] * 2,
+        + [OUTSIDE] * (1 + len(pieces)),
         [
             (line, shape(rows, width, kind=FULL)),
             (wide, shape(rows, units)),
@@ -914,26 +948,26 @@
         [
             pltpu.VMEM((width, units), LOW),
             pltpu.VMEM((units, width), LOW),
-            pltpu.SemaphoreType.DMA((2, plan.groups * weights[0].shape[1])),
+            pltpu.SemaphoreType.DMA((2, max(plan.groups * weights[0].shape[1], plan.copies()))),
         ],
         28,
         info,
-        (cot, back_heads, resid_two, expanded, resid, affine, *ring, *weights[:2]),
-    )
-
-
-def attend_backward(info, grad_resid, grad_mixed, triple, w_out, w_in, early, block=256):
+        (cot, back_heads, resid_two, expanded, resid, affine, *ring, *pieces, weights[0]),
+    )
+
+
+def attend_backward(info, grad_resid, grad_mixed, triple, chances, context, w_out, w_in, early, block=512):
     rows, width = grad_resid.shape
     line, wide = rows_of(block, width), rows_of(block, 3 * width)
     return run(
         attend_back_kernel,
         rows // block,
-        [line, line, wide, WHOLE, WHOLE, OUTSIDE],
+        [line, line, wide, rows_of(block, 2 * width), line, WHOLE, WHOLE, OUTSIDE],
         [(line, shape(rows, width)), (wide, shape(rows, 3 * width))],
         [pltpu.VMEM((block, width), LOW)],
-        36,
+        30,
         info,
-        (grad_resid, grad_mixed, triple, w_out, w_in, early),
+        (grad_resid, grad_mixed, triple, chances, context, w_out, w_in, early),
     )
 
 
@@ -988,76 +1022,95 @@
     return second, back_one, around(term), sums, bias, saved
 
 
-def second_grads_of(plan, count, info, saved):
-    width = saved[0].shape[1]
-    size = 3 * padded(plan.rows) + padded(width // plan.groups // count)
+def second_rows(plan, width):
+    size = 3 * padded(plan.rows) + padded(width // plan.groups // plan.count)
+    return -(-size // (16 * plan.groups)) * 16 * plan.groups
+
+
+def place_tops(info, tops, rows):
     return run(
-        functools.partial(second_grad_kernel, plan),
+        tops_kernel,
         1,
-        [WHOLE] * len(saved),
-        [(WHOLE, shape(count, size, width))],
-        [],
-        5,
+        [WHOLE, OUTSIDE],
+        [(OUTSIDE, shape(*rows.shape))],
+        [
+            pltpu.VMEM(rows.shape, LOW),
+            pltpu.SemaphoreType.DMA((8,)),
+            pltpu.SemaphoreType.DMA((8,)),
+        ],
+        4,
         info,
-        saved,
+        (tops, rows),
     )[0]
 
 
-def spread_out(groups, mp_at, info, line, tops, early, kind):
+def spread_out(groups, mp_at, info, line, steps, before):
     count = len(line)
     rows, width = line[0].shape
-    held = [pltpu.VMEM((groups, rows, width), line[0].dtype)]
-    if tops is None:
-        tops = jnp.zeros((8, width), FULL)
-        held.append(pltpu.VMEM((groups, rows, width), kind))
-        kernel = spread_kernel
-    else:
-        kernel = same_kernel
+    again = before.shape[0] == groups * rows
     return run(
-        functools.partial(kernel, groups, mp_at),
+        functools.partial(spread_kernel, groups, mp_at, steps),
         1,
-        [OUTSIDE] * count + [WHOLE, OUTSIDE],
-        [(OUTSIDE, shape(groups * rows, width, kind=kind))],
-        held + [pltpu.SemaphoreType.DMA((count,)), pltpu.SemaphoreType.DMA((count,))],
-        7,
+        [OUTSIDE] * (count + 1),
+        [(OUTSIDE, shape(groups * rows, width, kind=FULL))],
+        [
+            pltpu.VMEM((count, rows, width), line[0].dtype),
+            pltpu.VMEM((count, rows, width), FULL),
+            pltpu.SemaphoreType.DMA((count,)),
+            pltpu.SemaphoreType.DMA((count,)),
+        ],
+        3 if again else 6,
         info,
-        (*line, tops, early),
+        (*line, before),
+        {count + 1: 0} if again else None,
     )[0]
 
 
-def unit_grads(plan, info, active, grad_ret, hid_low, grad_exp, context, grad_mixed, small, early):
+def unit_rows(plan, width):
+    return 2 * padded(plan.rows) + padded(width // plan.groups // plan.count + 8)
+
+
+def unit_grads(plan, info, active, grad_ret, hid_low, grad_exp, context, grad_mixed, small, saved):
     rows, width = grad_ret.shape
     fixed = pl.BlockSpec((rows, width), lambda m, c: (0, 0))
     moving = pl.BlockSpec((rows, width), lambda m, c: (0, c[plan.mp_at + m]))
-    size = 2 * padded(plan.rows) + padded(width // plan.groups // plan.count + 8)
+    tall = second_rows(plan, width)
+    size = unit_rows(plan, width) + tall // plan.groups
     out = pl.BlockSpec((plan.count, 1, size, width), lambda m, c: (0, m, 0, 0))
     square = pltpu.VMEM((width, width), FULL)
     return run(
         functools.partial(unit_grad_kernel, plan),
         plan.groups,
-        [moving, fixed, fixed, moving, fixed, fixed] + [WHOLE] * len(small) + [OUTSIDE],
+        [moving, fixed, fixed, moving, fixed, fixed] + [WHOLE] * (len(small) + len(saved)),
         [(out, shape(plan.count, plan.groups, size, width))],
-        [square, square, pltpu.VMEM((width // LANES * 8, width), FULL)],
+        [
+            square,
+            square,
+            pltpu.VMEM((width // LANES * 8, width), FULL),
+            pltpu.VMEM((plan.count, tall, width), LOW),
+        ],
         19,
         info,
-        (active, grad_ret, hid_low, grad_exp, context, grad_mixed, *small, early),
+        (active, grad_ret, hid_low, grad_exp, context, grad_mixed, *small, *saved),
     )[0]
 
 
-def collect(plan, info, unit_own, unit_ring, head_own, head_ring, second):
+def collect(plan, info, unit_own, unit_ring, head_own, head_ring):
+    extra = (unit_own.shape[1] - unit_ring[0].shape[0]) * plan.groups
     return run(
         functools.partial(collect_kernel, plan),
         1,
-        [WHOLE] * (4 + len(unit_ring) + len(head_ring)),
+        [WHOLE] * (3 + len(unit_ring) + len(head_ring)),
         [
             (WHOLE, shape(*unit_ring[0].shape, kind=FULL)),
             (WHOLE, shape(*head_ring[0].shape, kind=FULL)),
+            (WHOLE, shape(extra, unit_own.shape[2], kind=FULL)),
             (WHOLE, shape(8, LANES, kind=FULL)),
         ],
         [],
         4,
         info,
-        (unit_own, *unit_ring, *head_own, *head_ring, second),
+        (unit_own, *unit_ring, *head_own, *head_ring),
     )
 
 
@@ -1131,7 +1184,7 @@
     return lax.optimization_barrier((value, first))[0]
 
 
-def gather(ring, gates):
+def gather(ring, gates, hold=()):
     half = len(ring) // 2
     bits = bits_of(lax.axis_size("dp"))
     held = [[([0], jnp.stack(ring[:half])[None])], [([0], jnp.stack(ring[half:])[None])]]
@@ -1152,7 +1205,7 @@
     for which in range(2):
         for places, block in held[which]:
             pieces.append((places, which, block))
-            pieces.append(([j ^ 1 for j in places], which, swap(block, 1)))
+            pieces.append(([j ^ 1 for j in places], which, swap(tie(block, *hold), 1)))
     return pieces, arrived
 
 
@@ -1239,16 +1292,19 @@
     mp_at, dp_at = slots, slots + groups
 
     heads_block = heads_block_of(info, attend_in, expand_bias, affine_state, position_state)
-    units_block = units_block_of(info, 0, (expand_in, expand_out, attend_out))
+    up_block = units_block_of(info, 0, (expand_in,))
+    units_block = units_block_of(info, 0, (expand_out, attend_out))
     second_block = units_block_of(info, 1, (attend_in, expand_in, expand_out, attend_out))
     units_all = lax.all_gather(units_block, ("mp", "dp"), axis=0)
     units_all = units_all.reshape(groups, shards_dp, -1, width)
-    heads_pieces, _ = gather(around(heads_block), [])
+    heads_ring = around(heads_block)
+    heads_pieces, heads_got = gather(heads_ring, [])
     second_all = lax.all_gather(second_block, "dp", axis=0)
 
     step, low_share = padded(piece), padded(share)
-    units_sections = [(0, piece), (step, piece), (2 * step, low_share)]
-    units = [units_all] * 3
+    up_ring = around(tie(up_block, *heads_ring[1:]))
+    units_sections = [(0, piece), (step, low_share)]
+    units = [units_all] * 2
     sections = [(0, piece), (3 * step, low_share), (step, piece), (2 * step, piece)]
     weights = [second_all] * 4
     load_info = info
@@ -1274,11 +1330,16 @@
     own_plan = plan_of([], piece)
     heads_pieces = [member[2] for member in heads_pieces]
 
-    triple, context, w_in, affine_one, affine_two, position, b_up = attend_forward(
+    triple, context, chances, w_in, affine_one, affine_two, position, b_up = attend_forward(
         heads_plan, load_info, tokens, heads_pieces
     )
+    up_pieces, _ = gather(up_ring, heads_got[-1:], (b_up,))
+    if piece % 16:
+        up_pieces = straighten([(p, w, b[:, :, :piece]) for p, w, b in up_pieces], device)
+    up_plan = plan_of(up_pieces, up_pieces[0][2].shape[2])
+    up_pieces = [member[2] for member in up_pieces]
     resid, hid_low, expanded, resid_two, first, tops, w_out = feed_forward(
-        own_plan, units_sections, info, tokens, context, affine_one, b_up, units
+        up_plan, units_sections, load_info, tokens, context, affine_one, b_up, up_pieces, units
     )
 
     keep_heads = (counts > 0).astype(FULL)
@@ -1287,24 +1348,27 @@
     top_grad = cotangent.reshape(-1, SEG, width)[:, 0].astype(FULL) * keep_heads
     tops_ring = around(tops)
     second, back_heads, heads_ring, sums_two, bias_two, saved = second_layer(
-        sections, own_plan, info, tops_ring, position, live, top_grad, affine_two, affine_one[7:8], weights
-    )
-    first_later = tie(first, *heads_ring[1:])
-    out_line = [(onward(first_later, 1), onward(first_later, -1))]
+        sections, own_plan, info, tops_ring, position, live, top_grad, affine_two, affine_one, weights
+    )
+    out_rows = lax.all_gather(first, "mp", axis=0, tiled=True)
     grad_resid, active, grad_exp, grad_ret, grad_mixed, sums_one, bias, grad_heads = feed_backward(
-        own_plan, units_sections, info, cotangent, back_heads, heads_ring, resid_two, expanded, resid, affine_one, units
-    )
-    second_grads = second_grads_of(own_plan, shards_dp, tie(info, sums_one), saved)
-    second_share = lax.psum_scatter(second_grads, "dp", scatter_dimension=0)
-    out_line.append((onward(out_line[0][0], 1), onward(out_line[0][1], -1)))
-    grad_in, grad_triple = attend_backward(
-        tie(info, *out_line[0]), grad_resid, grad_mixed, triple, w_out, w_in, active
-    )
-    out_line.append((onward(out_line[1][0], 1), onward(out_line[1][1], -1)))
+        up_plan,
+        units_sections,
+        load_info,
+        cotangent,
+        back_heads,
+        heads_ring,
+        resid_two,
+        expanded,
+        resid,
+        affine_one,
+        up_pieces,
+        units,
+    )
     small = (sums_one, sums_two, grad_heads, bias, bias_two)
     unit_out = unit_grads(
         own_plan,
-        tie(info, *out_line[1]),
+        info,
         active,
         grad_ret,
         hid_low,
@@ -1312,45 +1376,45 @@
         context,
         grad_mixed,
         small,
-        grad_in,
+        saved,
     )
     unit_terms = lax.psum_scatter(unit_out, "dp", scatter_dimension=0)
-    keep_a, send_a, keep_b, send_b = head_grads(own_plan, lists, info, tokens, grad_triple, unit_out)
-
-    def in_line(own, line):
-        return [own] + [pair[0] for pair in line] + [pair[1] for pair in line]
-
-    grad_later = tie(grad_in, keep_a, *out_line[2])
-    grad_line = [(onward(grad_later, 1), onward(grad_later, -1))]
-    left_a, right_a = reduce_dp(keep_a, send_a, bits, out_line[2])
-    left_b, right_b = reduce_dp(keep_b, send_b, bits[::-1], out_line[2])
+    grad_in, grad_triple = attend_backward(
+        info, grad_resid, grad_mixed, triple, chances, context, w_out, w_in, unit_out
+    )
+    merged = place_tops(info, second * keep_heads, out_rows)
+    keep_a, send_a, keep_b, send_b = head_grads(own_plan, lists, tie(info, merged), tokens, grad_triple, unit_out)
+
+    grad_line = [(onward(grad_in, 1), onward(grad_in, -1))]
+    left_a, right_a = reduce_dp(keep_a, send_a, bits, grad_line[0])
+    left_b, right_b = reduce_dp(keep_b, send_b, bits[::-1], grad_line[0])
     terms = [(left_a[s], right_a[s]) for s in range(1, groups // 2)]
     terms += [(left_b[s], right_b[s]) for s in range(groups - groups // 2)]
+    last = tie(grad_line[0], keep_a)
+    grad_line.append((onward(last[0], 1), onward(last[1], -1)))
     head_ring = [
-        ahead(tie(add(*term), *grad_line[0]), -at - 1) for at, term in enumerate(terms)
+        ahead(tie(add(*term), *grad_line[1]), -at - 1) for at, term in enumerate(terms)
     ]
-    merged = spread_out(
+    unit_ring = [
+        ahead(tie(unit_terms[at, : unit_rows(own_plan, width)], *grad_line[1]), -at)
+        for at in range(1, groups)
+    ]
+    unit_sum, head_sum, second_sum, squares = collect(
+        own_plan, info, unit_terms, unit_ring, (left_a, right_a), head_ring
+    )
+    squares = all_sum(squares, ("mp",))
+    last = tie(grad_line[1], squares)
+    grad_line.append((onward(last[0], 1), onward(last[1], -1)))
+    squares = all_sum(squares, ("dp",))
+    input_grad = spread_out(
         groups,
         mp_at,
         info,
-        in_line(first, out_line),
-        second * keep_heads,
-        grad_line[0][0],
-        LOW,
-    )
-    grad_line.append((onward(grad_line[0][0], 1), onward(grad_line[0][1], -1)))
-    unit_ring = [
-        ahead(tie(unit_terms[at], *grad_line[1]), -at) for at in range(1, groups)
-    ]
-    unit_sum, head_sum, squares = collect(
-        own_plan, info, unit_terms, unit_ring, (left_a, right_a), head_ring, second_share
-    )
-    last = tie(grad_line[1], *unit_ring)
-    grad_line.append((onward(last[0], 1), onward(last[1], -1)))
-    squares = all_sum(squares, ("dp", "mp"))
-    input_grad = spread_out(
-        groups, mp_at, info, in_line(grad_in, grad_line), None, grad_triple, FULL
-    )
+        [grad_in, *grad_line[0], *grad_line[1]],
+        (0, -1, 1, -2, 2),
+        grad_line[1][0],
+    )
+    input_grad = spread_out(groups, mp_at, info, grad_line[2], (-3, 3), input_grad)
     states = (
         attend_in,
         attend_out,
@@ -1360,7 +1424,8 @@
         affine_state,
         position_state,
     )
-    *updated, norm = update(own_plan, info, squares, unit_sum, head_sum, second_share, states)
+    assert groups == 4
+    *updated, norm = update(own_plan, info, squares, unit_sum, head_sum, second_sum, states)
     return (merged, input_grad, norm[0, 0], *updated)
 
 

time: 553 us -> 495 us (0.90)
  waiting for transfers between devices: 217 us -> 163 us
  Pallas kernels: 195 us -> 186 us
    ppermute x24 -> x27, waiting for transfers between devices: 26.6 us -> 74.3 us  [ahead(): lax.ppermute(value, 'mp', [(i, (i + step) % size) for i in range(size)])]
    all_gather x1, waiting for transfers between devices: 34 us -> 0.01 us  [shards(): units_all = lax.all_gather(units_block, ('mp', 'dp'), axis=0)]
    ppermute x12 -> x6, waiting for transfers between devices: 70.6 us -> 36.7 us  [onward(): lax.ppermute(value, 'mp', [(i, i + step) for i in range(size) if 0 <= i +...]
    ppermute x19 -> x27, waiting for transfers between devices: 69.9 us -> 47.5 us  [swap(): lax.ppermute(value, axis, [(i, i ^ bit) for i in range(lax.axis_size(axis...]
    ppermute x12 -> x6, starting transfers between devices: 33 us -> 15.8 us  [onward(): lax.ppermute(value, 'mp', [(i, i + step) for i in range(size) if 0 <= i +...]
    ppermute x19 -> x27, starting transfers between devices: 21.5 us -> 34.6 us  [swap(): lax.ppermute(value, axis, [(i, i ^ bit) for i in range(lax.axis_size(axis...]
    ppermute x24 -> x27, starting transfers between devices: 38.2 us -> 47.7 us  [ahead(): lax.ppermute(value, 'mp', [(i, (i + step) % size) for i in range(size)])]
    reduce_scatter x1 -> x0, waiting for transfers between devices: 9.4 us -> none  [shards(): second_share = lax.psum_scatter(second_grads, 'dp', scatter_dimension=0)]
  transfers between devices with their start and end apart: 59 -> 64, of which waited for: 34 -> 38; matrix products, arithmetic and copies ran while one was open for 3% -> 3% of each run, Pallas kernels for 26% -> 36%
where the time goes in v3:
time: 495 us; the launch traced here: 488 us
  Pallas kernels  186 us (38%)
  waiting for transfers between devices  163 us (33%)
  starting transfers between devices  98.3 us (20%)
  local copies, waits for them, and re-layouts  18.4 us (4%)
  between operations  14.6 us (3%)
  other arithmetic  7.1 us (1%)
    pallas_call x19, Pallas kernels, run(): pl.pallas_call(kernel, grid_spec=pltpu.PrefetchScalarGridSpec(num_scalar_...  186 us
    ppermute x27, waiting for transfers between devices, ahead(): lax.ppermute(value, 'mp', [(i, (i + step) % size) for i in range(size)])  74.3 us
    ppermute x27, starting transfers between devices, ahead(): lax.ppermute(value, 'mp', [(i, (i + step) % size) for i in range(size)])  47.7 us
    ppermute x27, waiting for transfers between devices, swap(): lax.ppermute(value, axis, [(i, i ^ bit) for i in range(lax.axis_size(axis...  47.5 us
    ppermute x6, waiting for transfers between devices, onward(): lax.ppermute(value, 'mp', [(i, i + step) for i in range(size) if 0 <= i +...  36.7 us
    ppermute x27, starting transfers between devices, swap(): lax.ppermute(value, axis, [(i, i ^ bit) for i in range(lax.axis_size(axis...  34.6 us
    ppermute x6, starting transfers between devices, onward(): lax.ppermute(value, 'mp', [(i, i + step) for i in range(size) if 0 <= i +...  15.8 us
    unnamed x94, local copies, waits for them, and re-layouts  14.1 us
  transfers between devices with their start and end apart: 64, of which 38 were waited for; matrix products, arithmetic and copies ran while one was open for 3% of the time, Pallas kernels for 36%

profile of v3, /device:TPU:0, one launch (start us, length us, event | category | flops | bytes accessed | tf_op | source)
XLA Modules:
  0.0 487.6 jit_solution(8378061264088493786)
XLA Ops:
  42.6 5.9 %collective-permute-start.16 = (bf16[96,768]{1,0:T(8,128)(2,1)}, bf16[96,768]{1,0:T(8,128)(2,1)S(1)}, u32[]{:S(2)}, u32[]{:S(2)}) collective-permute-start(bf16[96,768]{1,0:T(8,128)(2,1)} %shard_map.292), channel_id=1, source_target_pairs={{0,2},{1,3},{2,0},{3,1},{4,6},{5,7},{6,4},{7,5},{8,10},{9,11},{10,... | collective-permute-start | bytes 442376 | tf_op jit(solution)/shard_map/ppermute | solution.py:1152
  49.0 8.8 %collective-permute-done.16 = bf16[96,768]{1,0:T(8,128)(2,1)S(1)} collective-permute-done((bf16[96,768]{1,0:T(8,128)(2,1)}, bf16[96,768]{1,0:T(8,128)(2,1)S(1)}, u32[]{:S(2)}, u32[]{:S(2)}) %collective-permute-start.16) | collective-permute-done | bytes 147488 | tf_op jit(solution)/shard_map/ppermute | solution.py:1152
  59.3 5.3 %collective-permute-start.11 = (bf16[96,768]{1,0:T(8,128)(2,1)}, bf16[96,768]{1,0:T(8,128)(2,1)S(1)}, u32[]{:S(2)}, u32[]{:S(2)}) collective-permute-start(bf16[96,768]{1,0:T(8,128)(2,1)} %shard_map.292), channel_id=1, source_target_pairs={{0,1},{1,2},{2,3},{3,0},{4,5},{5,6},{6,7},{7,4},{8,9},{9,10},{10,1... | collective-permute-start | bytes 442376 | tf_op jit(solution)/shard_map/ppermute | solution.py:1152
  72.6 14.2 %collective-permute-done.12 = bf16[1,2,96,768]{3,2,1,0:T(8,128)(2,1)S(1)} collective-permute-done((bf16[1,2,96,768]{3,2,1,0:T(8,128)(2,1)S(1)}, bf16[1,2,96,768]{3,2,1,0:T(8,128)(2,1)S(1)}, u32[]{:S(2)}, u32[]{:S(2)}) %collective-permute-start.12) | collective-permute-done | bytes 294944 | tf_op jit(solution)/shard_map/ppermute | solution.py:1147
  92.3 18.0 %shard_map.290 = (bf16[1024,2304]{1,0:T(8,128)(2,1)}, bf16[1024,768]{1,0:T(8,128)(2,1)}, bf16[1024,1536]{1,0:T(8,128)(2,1)}, bf16[768,2304]{1,0:T(8,128)(2,1)}, ...) custom-call(s32[20]{0:T(128)} %pad_add_fusion.info, bf16[4096,768]{1,0:T(8,128)(2,1)} %tok.5, ...), custom_call_target="tpu_custom_call" | custom-call | flops 20700000256 | bytes 1024 | tf_op jit(solution)/shard_map/pallas_call | solution.py:819
  115.7 25.3 %shard_map.293 = (f32[1024,768]{1,0:T(8,128)}, bf16[1024,768]{1,0:T(8,128)(2,1)}, bf16[1024,3072]{1,0:T(8,128)(2,1)}, f32[1024,768]{1,0:T(8,128)}, bf16[1024,768...) custom-call(s32[20]{0:T(128)} %pad_add_fusion.info, bf16[4096,768]{1,0:T(8,128)(2,1)} %tok.5, ...), custom_call_target="tpu_custom_call" | custom-call | flops 27599998976 | bytes 1024 | tf_op jit(solution)/shard_map/pallas_call | solution.py:819
  148.5 4.9 %shard_map.295 = (bf16[32,768]{1,0:T(8,128)(2,1)}, f32[32,768]{1,0:T(8,128)}, bf16[32,768]{1,0:T(8,128)(2,1)}, bf16[32,640]{1,0:T(8,128)(2,1)}, bf16[32,256]{1,0:T(8,128)(2,1)}) custom-call(s32[20]{0:T(128)} %pad_add_fusion.info, f32[8,768]{1,0:T(8,128)} %get-tuple-element.131.refs_0_, f32[8,768]{1,0:T(8,128)} %copy-done.40, f32[8,768]{1,0:T(8,128)} %copy-done.41, ...), custom_call_target="tpu_custom_call" | custom-call | flops 5750000128 | bytes 1024 | tf_op jit(solution)/shard_map/pallas_call | solution.py:819
  184.2 5.0 %shard_map.297 = (bf16[32,768]{1,0:T(8,128)(2,1)}, f32[32,768]{1,0:T(8,128)}, f32[32,768]{1,0:T(8,128)}, bf16[32,768]{1,0:T(8,128)(2,1)}, bf16[32,768]{1,0:T(8,1...) custom-call(s32[20]{0:T(128)} %pad_add_fusion.info, bf16[32,768]{1,0:T(8,128)(2,1)} %get-tuple-element.136.refs_0_, ...), custom_call_target="tpu_custom_call" | custom-call | flops 5750000128 | bytes 1024 | tf_op jit(solution)/shard_map/pallas_call | solution.py:819
  202.2 5.1 %shard_map.299 = (bf16[32,768]{1,0:T(8,128)(2,1)}, f32[32,768]{1,0:T(8,128)}, bf16[32,768]{1,0:T(8,128)(2,1)}, bf16[32,640]{1,0:T(8,128)(2,1)}, f32[8,768]{1,0:T(8,128)}) custom-call(s32[20]{0:T(128)} %pad_add_fusion.info, bf16[32,768]{1,0:T(8,128)(2,1)} %get-tuple-element.141.refs_0_, bf16[32,768]{1,0:T(8,128)(2,1)} %copy-done.31, ...), custom_call_target="tpu_custom_call" | custom-call | flops 5750000128 | bytes 1024 | tf_op jit(solution)/shard_map/pallas_call | solution.py:819
  215.0 6.5 %collective-permute-done.35.refs_2_ = bf16[32,768]{1,0:T(8,128)(2,1)S(1)} collective-permute-done((bf16[32,768]{1,0:T(8,128)(2,1)}, bf16[32,768]{1,0:T(8,128)(2,1)S(1)}, u32[]{:S(2)}, u32[]{:S(2)}) %collective-permute-start.35) | collective-permute-done | bytes 49184 | tf_op jit(solution)/shard_map/ppermute | solution.py:1152
  222.1 28.8 %shard_map.300 = (f32[1024,768]{1,0:T(8,128)}, bf16[1024,3072]{1,0:T(8,128)(2,1)}, bf16[1024,3072]{1,0:T(8,128)(2,1)}, bf16[1024,768]{1,0:T(8,128)(2,1)}, bf16[1...) custom-call(s32[20]{0:T(128)} %pad_add_fusion.info, bf16[4096,768]{1,0:T(8,128)(2,1)} %cot.1, ...), custom_call_target="tpu_custom_call" | custom-call | flops 32199999488 | bytes 1024 | tf_op jit(solution)/shard_map/pallas_call | solution.py:819
  250.9 20.5 %shard_map.301.early = bf16[8,4,304,768]{3,2,1,0:T(8,128)(2,1)} custom-call(s32[20]{0:T(128)} %pad_add_fusion.info, bf16[1024,3072]{1,0:T(8,128)(2,1)} %get-tuple-element.156.active, bf16[1024,768]{1,0:T(8,128)(2,1)} %get-tuple-element.157.grad_ret, bf16[1024,768]{1,0:T(8,128)(2,1)} %get-tuple-element.158.hid_low, ...), custom_call_target="tpu_custom_call" | custom-call | flops 21849999360 | bytes 1024 | tf_op jit(solution)/shard_map/pallas_call | solution.py:819
  273.0 25.1 %shard_map.302 = (bf16[1024,768]{1,0:T(8,128)(2,1)}, bf16[1024,2304]{1,0:T(8,128)(2,1)}) custom-call(s32[20]{0:T(128)} %pad_add_fusion.info, f32[1024,768]{1,0:T(8,128)} %get-tuple-element.150.grad_resid, bf16[1024,768]{1,0:T(8,128)(2,1)} %get-tuple-element.151.grad_mixed, bf16[1024,2304]{1,0:T(8,128)(2,1)} %get-tuple-element.152.triple, ...), custom_call_target="tpu_custom_call" | custom-call | flops 34500001792 | bytes 1024 | tf_op jit(solution)/shard_map/pallas_call | solution.py:819
  304.1 7.2 %shard_map.298 = bf16[4096,768]{1,0:T(8,128)(2,1)} custom-call(s32[20]{0:T(128)} %pad_add_fusion.info, f32[32,768]{1,0:T(8,128)} %broadcast_multiply_fusion.tops, bf16[4096,768]{1,0:T(8,128)(2,1)} %all-gather.6.cloned.1.call-done.rows), custom_call_target="tpu_custom_call" | custom-call | flops 4600000000 | bytes 1024 | tf_op jit(solution)/shard_map/pallas_call | solution.py:819
  311.3 10.1 %shard_map.303 = (bf16[4,2,96,640]{3,2,1,0:T(8,128)(2,1)}, bf16[4,2,96,640]{3,2,1,0:T(8,128)(2,1)}, bf16[4,2,96,640]{3,2,1,0:T(8,128)(2,1)}, bf16[4,2,96,640]{3,2,1,0:T(8,128)(2,1)}) custom-call(s32[20]{0:T(128)} %pad_add_fusion.info, bf16[4096,768]{1,0:T(8,128)(2,1)} %tok.5, bf16[1024,2304]{1,0:T(8,128)(2,1)} %get-tuple-element.175.grad_triple, ...), custom_call_target="tpu_custom_call" | custom-call | flops 11500000256 | bytes 1024 | tf_op jit(solution)/shard_map/pallas_call | solution.py:819
  321.9 14.0 %collective-permute-done.37.refs_1_ = bf16[1024,768]{1,0:T(8,128)(2,1)S(1)} collective-permute-done((bf16[1024,768]{1,0:T(8,128)(2,1)}, bf16[1024,768]{1,0:T(8,128)(2,1)S(1)}, u32[]{:S(2)}, u32[]{:S(2)}) %collective-permute-start.37) | collective-permute-done | bytes 1572896 | tf_op jit(solution)/shard_map/ppermute | solution.py:1157
  348.4 8.9 %collective-permute-done.49 = bf16[2,2,96,640]{3,2,1,0:T(8,128)(2,1)S(1)} collective-permute-done((bf16[2,2,96,640]{3,2,1,0:T(8,128)(2,1)S(1)}, bf16[2,2,96,640]{3,2,1,0:T(8,128)(2,1)S(1)}, u32[]{:S(2)}, u32[]{:S(2)}) %collective-permute-start.49) | collective-permute-done | bytes 491552 | tf_op jit(solution)/shard_map/ppermute | solution.py:1147
  362.9 7.1 %collective-permute-done.50 = bf16[1,2,96,640]{3,2,1,0:T(8,128)(2,1)S(1)} collective-permute-done((bf16[1,2,96,640]{3,2,1,0:T(8,128)(2,1)S(1)}, bf16[1,2,96,640]{3,2,1,0:T(8,128)(2,1)S(1)}, u32[]{:S(2)}, u32[]{:S(2)}) %collective-permute-start.50) | collective-permute-done | bytes 245792 | tf_op jit(solution)/shard_map/ppermute | solution.py:1147
  374.2 5.5 %collective-permute-done.40.refs_4_ = bf16[1024,768]{1,0:T(8,128)(2,1)S(1)} collective-permute-done((bf16[1024,768]{1,0:T(8,128)(2,1)}, bf16[1024,768]{1,0:T(8,128)(2,1)S(1)}, u32[]{:S(2)}, u32[]{:S(2)}) %collective-permute-start.40) | collective-permute-done | bytes 1572896 | tf_op jit(solution)/shard_map/ppermute | solution.py:1157
  393.1 22.5 %collective-permute-done.47.refs_6_ = bf16[96,640]{1,0:T(8,128)(2,1)S(1)} collective-permute-done((bf16[96,640]{1,0:T(8,128)(2,1)S(1)}, bf16[96,640]{1,0:T(8,128)(2,1)S(1)}, u32[]{:S(2)}, u32[]{:S(2)}) %collective-permute-start.47) | collective-permute-done | bytes 122912 | tf_op jit(solution)/shard_map/ppermute | solution.py:1152
  420.8 8.0 %collective-permute-start.53 = (f32[8,128]{1,0:T(8,128)}, f32[8,128]{1,0:T(8,128)S(1)}, u32[]{:S(2)}, u32[]{:S(2)}) collective-permute-start(f32[8,128]{1,0:T(8,128)} %get-tuple-element.190), channel_id=1, source_target_pairs={{0,1},{1,0},{2,3},{3,2},{4,5},{5,4},{6,7},{7,6},{8,9},{9,8},{10,11... | collective-permute-start | bytes 12296 | tf_op jit(solution)/shard_map/ppermute | solution.py:1147
  447.4 6.1 %shard_map.305.refs_2_ = f32[4096,768]{1,0:T(8,128)} custom-call(s32[20]{0:T(128)} %pad_add_fusion.info, bf16[1024,768]{1,0:T(8,128)(2,1)} %get-tuple-element.173.refs_0_, bf16[1024,768]{1,0:T(8,128)(2,1)} %copy-done.13, bf16[1024,768]{1,0:T(8,128)(2,1)} %collective-permute-done.38.refs_2_, bf16[1024,768]{1,0:T(8,128)(2,1)} %collective-permute-done.39.refs_3_.refs_5_, ...), custom_call_target="tpu_custom_call" | custom-call | flops 6899999744 | bytes 1024 | tf_op jit(solution)/shard_map/pallas_call | solution.py:819
  454.2 7.5 %shard_map.307 = (f32[2,96,576]{2,1,0:T(8,128)}, f32[2,24,768]{2,1,0:T(8,128)}, f32[2,96,768]{2,1,0:T(8,128)}, f32[2,96]{1,0:T(2,128)}, f32[2,96,768]{2,1,0:T(8,...) custom-call(s32[20]{0:T(128)} %pad_add_fusion.info, ...), custom_call_target="tpu_custom_call" | custom-call | flops 8049999872 | bytes 1024 | tf_op jit(solution)/shard_map/pallas_call | solution.py:819
  466.7 4.9 collective-permute-done.55.refs_0_
  (251 shorter events, 198.0 us)
Async XLA Ops:
  7.2 108.5 %all-gather.8.cloned.1.call-start = ((), (), s32[]{:S(2)}) async-start(), calls=%async_computation.3 | async-start | bytes 6488064 | tf_op jit(solution)/shard_map/all_gather | solution.py:1298
  11.1 134.8 %all-gather.10.cloned.1.call-start = ((), (), s32[]{:S(2)}) async-start(), calls=%async_computation.4 | async-start | bytes 4423680 | tf_op jit(solution)/shard_map/all_gather | solution.py:1302
  23.0 281.1 %all-gather.6.cloned.1.call-start = ((), (), s32[]{:S(2)}) async-start(), calls=%async_computation.1 | async-start | bytes 7864320 | tf_op jit(solution)/shard_map/all_gather | solution.py:1353
  32.7 26.5 %collective-permute-start.9 = (bf16[2,2,96,640]{3,2,1,0:T(8,128)(2,1)S(1)}, bf16[2,2,96,640]{3,2,1,0:T(8,128)(2,1)S(1)}, u32[]{:S(2)}, u32[]{:S(2)}) collective-permute-start(bf16[2,2,96,640]{3,2,1,0:T(8,128)(2,1)S(1)} %pad_maximum_fusion.1.refs_4_), channel_id=1, source_target_pairs={{0,8},{4,12},{8,0},{12,4},{16,24},{20,28},{24,16},{28,20},{1,9},{5... | collective-permute-start | bytes 1474568 | tf_op jit(solution)/shard_map/ppermute | solution.py:1147
  64.7 23.9 %collective-permute-start.8 = (bf16[2,2,96,640]{3,2,1,0:T(8,128)(2,1)S(1)}, bf16[2,2,96,640]{3,2,1,0:T(8,128)(2,1)}, u32[]{:S(2)}, u32[]{:S(2)}) collective-permute-start(bf16[2,2,96,640]{3,2,1,0:T(8,128)(2,1)S(1)} %pad_maximum_fusion.1.refs_4_), channel_id=1, source_target_pairs={{0,4},{4,0},{8,12},{12,8},{16,20},{20,16},{24,28},{28,24},{1,5},{5... | collective-permute-start | bytes 1474568 | tf_op jit(solution)/shard_map/ppermute | solution.py:1147
  64.7 26.0 %collective-permute-start.2 = (bf16[2,2,96,640]{3,2,1,0:T(8,128)(2,1)S(1)}, bf16[2,2,96,640]{3,2,1,0:T(8,128)(2,1)S(1)}, u32[]{:S(2)}, u32[]{:S(2)}) collective-permute-start(bf16[2,2,96,640]{3,2,1,0:T(8,128)(2,1)S(1)} %pad_maximum_fusion.refs_0_), channel_id=1, source_target_pairs={{0,4},{4,0},{8,12},{12,8},{16,20},{20,16},{24,28},{28,24},{1,5},{5... | collective-permute-start | bytes 1474568 | tf_op jit(solution)/shard_map/ppermute | solution.py:1147
  65.2 25.5 %collective-permute-start.10 = (bf16[2,2,96,640]{3,2,1,0:T(8,128)(2,1)S(1)}, bf16[2,2,96,640]{3,2,1,0:T(8,128)(2,1)S(1)}, u32[]{:S(2)}, u32[]{:S(2)}) collective-permute-start(bf16[2,2,96,640]{3,2,1,0:T(8,128)(2,1)S(1)} %collective-permute-done.9.refs_6_), channel_id=1, source_target_pairs={{0,4},{4,0},{8,12},{12,8},{16,20},{20,16},{24,28},{28,24},{1,5},{5... | collective-permute-start | bytes 1474568 | tf_op jit(solution)/shard_map/ppermute | solution.py:1147
  69.8 22.5 %collective-permute-start.4 = (bf16[2,2,96,640]{3,2,1,0:T(8,128)(2,1)}, bf16[2,2,96,640]{3,2,1,0:T(8,128)(2,1)}, u32[]{:S(2)}, u32[]{:S(2)}) collective-permute-start(bf16[2,2,96,640]{3,2,1,0:T(8,128)(2,1)} %collective-permute-done.3.refs_2_), channel_id=1, source_target_pairs={{0,4},{4,0},{8,12},{12,8},{16,20},{20,16},{24,28},{28,24},{1,5},{5... | collective-permute-start | bytes 1474568 | tf_op jit(solution)/shard_map/ppermute | solution.py:1147
  86.8 24.0 %collective-permute-start.20 = (bf16[2,2,96,768]{3,2,1,0:T(8,128)(2,1)S(1)}, bf16[2,2,96,768]{3,2,1,0:T(8,128)(2,1)S(1)}, u32[]{:S(2)}, u32[]{:S(2)}) collective-permute-start(bf16[2,2,96,768]{3,2,1,0:T(8,128)(2,1)S(1)} %constant_dynamic-update-slice_fusion.2.refs_4_.refs_8_), channel_id=1, source_target_pairs={{0,8},{4,12},{8,0},{12,4},{16,24},{20,28},{24,16},{28,20},{1,9},{5... | collective-permute-start | bytes 1769480 | tf_op jit(solution)/shard_map/ppermute | solution.py:1147
  88.6 22.3 %collective-permute-start.14 = (bf16[2,2,96,768]{3,2,1,0:T(8,128)(2,1)S(1)}, bf16[2,2,96,768]{3,2,1,0:T(8,128)(2,1)S(1)}, u32[]{:S(2)}, u32[]{:S(2)}) collective-permute-start(bf16[2,2,96,768]{3,2,1,0:T(8,128)(2,1)S(1)} %constant_dynamic-update-slice_fusion.refs_0_.refs_4_), channel_id=1, source_target_pairs={{0,16},{4,20},{8,24},{12,28},{16,0},{20,4},{24,8},{28,12},{1,17},{... | collective-permute-start | bytes 1769480 | tf_op jit(solution)/shard_map/ppermute | solution.py:1147
  141.1 244.2 %reduce-scatter.2.cloned.1.call-start = ((), (), s32[]{:S(2)}) async-start(), calls=%async_computation.2 | async-start | bytes 16809984 | tf_op jit(solution)/shard_map/reduce_scatter | solution.py:1381
  298.1 37.8 %collective-permute-start.37 = (bf16[1024,768]{1,0:T(8,128)(2,1)}, bf16[1024,768]{1,0:T(8,128)(2,1)S(1)}, u32[]{:S(2)}, u32[]{:S(2)}) collective-permute-start(bf16[1024,768]{1,0:T(8,128)(2,1)} %get-tuple-element.173.refs_0_), channel_id=1, source_target_pairs={{0,1},{1,2},{2,3},{4,5},{5,6},{6,7},{8,9},{9,10},{10,11},{12,13},{... | collective-permute-start | bytes 4718600 | tf_op jit(solution)/shard_map/ppermute | solution.py:1157
  302.8 37.3 %collective-permute-start.38 = (bf16[1024,768]{1,0:T(8,128)(2,1)}, bf16[1024,768]{1,0:T(8,128)(2,1)}, u32[]{:S(2)}, u32[]{:S(2)}) collective-permute-start(bf16[1024,768]{1,0:T(8,128)(2,1)} %get-tuple-element.173.refs_0_), channel_id=1, source_target_pairs={{1,0},{2,1},{3,2},{5,4},{6,5},{7,6},{9,8},{10,9},{11,10},{13,12},{... | collective-permute-start | bytes 4718600 | tf_op jit(solution)/shard_map/ppermute | solution.py:1157
  321.4 23.3 %collective-permute-start.48 = (bf16[4,2,96,640]{3,2,1,0:T(8,128)(2,1)}, bf16[4,2,96,640]{3,2,1,0:T(8,128)(2,1)S(1)}, u32[]{:S(2)}, u32[]{:S(2)}) collective-permute-start(bf16[4,2,96,640]{3,2,1,0:T(8,128)(2,1)} %get-tuple-element.186), channel_id=1, source_target_pairs={{0,4},{4,0},{8,12},{12,8},{16,20},{20,16},{24,28},{28,24},{1,5},{5... | collective-permute-start | bytes 2949128 | tf_op jit(solution)/shard_map/ppermute | solution.py:1147
  321.4 25.0 %collective-permute-start.44 = (bf16[4,2,96,640]{3,2,1,0:T(8,128)(2,1)}, bf16[4,2,96,640]{3,2,1,0:T(8,128)(2,1)S(1)}, u32[]{:S(2)}, u32[]{:S(2)}) collective-permute-start(bf16[4,2,96,640]{3,2,1,0:T(8,128)(2,1)} %get-tuple-element.182), channel_id=1, source_target_pairs={{0,4},{4,0},{8,12},{12,8},{16,20},{20,16},{24,28},{28,24},{1,5},{5... | collective-permute-start | bytes 2949128 | tf_op jit(solution)/shard_map/ppermute | solution.py:1147
  340.1 34.1 %collective-permute-start.39 = (bf16[1024,768]{1,0:T(8,128)(2,1)S(1)}, bf16[1024,768]{1,0:T(8,128)(2,1)}, u32[]{:S(2)}, u32[]{:S(2)}) collective-permute-start(bf16[1024,768]{1,0:T(8,128)(2,1)S(1)} %collective-permute-done.37.refs_1_), channel_id=1, source_target_pairs={{0,1},{1,2},{2,3},{4,5},{5,6},{6,7},{8,9},{9,10},{10,11},{12,13},{... | collective-permute-start | bytes 4718600 | tf_op jit(solution)/shard_map/ppermute | solution.py:1157
  343.4 36.3 %collective-permute-start.40 = (bf16[1024,768]{1,0:T(8,128)(2,1)}, bf16[1024,768]{1,0:T(8,128)(2,1)S(1)}, u32[]{:S(2)}, u32[]{:S(2)}) collective-permute-start(bf16[1024,768]{1,0:T(8,128)(2,1)} %collective-permute-done.38.refs_2_), channel_id=1, source_target_pairs={{1,0},{2,1},{3,2},{5,4},{6,5},{7,6},{9,8},{10,9},{11,10},{13,12},{... | collective-permute-start | bytes 4718600 | tf_op jit(solution)/shard_map/ppermute | solution.py:1157
  358.9 31.7 %collective-permute-start.46 = (bf16[1,2,96,640]{3,2,1,0:T(8,128)(2,1)S(1)}, bf16[1,2,96,640]{3,2,1,0:T(8,128)(2,1)S(1)}, u32[]{:S(2)}, u32[]{:S(2)}) collective-permute-start(bf16[1,2,96,640]{3,2,1,0:T(8,128)(2,1)S(1)} %get-tuple-element.275), channel_id=1, source_target_pairs={{0,16},{4,20},{8,24},{12,28},{16,0},{20,4},{24,8},{28,12},{1,17},{... | collective-permute-start | bytes 737288 | tf_op jit(solution)/shard_map/ppermute | solution.py:1147
  386.5 29.0 %collective-permute-start.43 = (bf16[224,768]{1,0:T(8,128)(2,1)S(1)}, bf16[224,768]{1,0:T(8,128)(2,1)S(1)}, u32[]{:S(2)}, u32[]{:S(2)}) collective-permute-start(bf16[224,768]{1,0:T(8,128)(2,1)S(1)} %get-tuple-element.181), channel_id=1, source_target_pairs={{0,1},{1,2},{2,3},{3,0},{4,5},{5,6},{6,7},{7,4},{8,9},{9,10},{10,1... | collective-permute-start | bytes 1032200 | tf_op jit(solution)/shard_map/ppermute | solution.py:1152
  388.4 27.2 %collective-permute-start.42 = (bf16[224,768]{1,0:T(8,128)(2,1)S(1)}, bf16[224,768]{1,0:T(8,128)(2,1)S(1)}, u32[]{:S(2)}, u32[]{:S(2)}) collective-permute-start(bf16[224,768]{1,0:T(8,128)(2,1)S(1)} %get-tuple-element.180), channel_id=1, source_target_pairs={{0,2},{1,3},{2,0},{3,1},{4,6},{5,7},{6,4},{7,5},{8,10},{9,11},{10,... | collective-permute-start | bytes 1032200 | tf_op jit(solution)/shard_map/ppermute | solution.py:1152
  390.6 24.9 %collective-permute-start.41 = (bf16[224,768]{1,0:T(8,128)(2,1)S(1)}, bf16[224,768]{1,0:T(8,128)(2,1)S(1)}, u32[]{:S(2)}, u32[]{:S(2)}) collective-permute-start(bf16[224,768]{1,0:T(8,128)(2,1)S(1)} %get-tuple-element.179), channel_id=1, source_target_pairs={{0,3},{1,0},{2,1},{3,2},{4,7},{5,4},{6,5},{7,6},{8,11},{9,8},{10,9... | collective-permute-start | bytes 1032200 | tf_op jit(solution)/shard_map/ppermute | solution.py:1152
  392.1 23.4 %collective-permute-start.47 = (bf16[96,640]{1,0:T(8,128)(2,1)S(1)}, bf16[96,640]{1,0:T(8,128)(2,1)S(1)}, u32[]{:S(2)}, u32[]{:S(2)}) collective-permute-start(bf16[96,640]{1,0:T(8,128)(2,1)S(1)} %fusion), channel_id=1, source_target_pairs={{0,3},{1,0},{2,1},{3,2},{4,7},{5,4},{6,5},{7,6},{8,11},{9,8},{10,9... | collective-permute-start | bytes 368648 | tf_op jit(solution)/shard_map/ppermute | solution.py:1152
  435.8 35.8 %collective-permute-start.55 = (bf16[1024,768]{1,0:T(8,128)(2,1)}, bf16[1024,768]{1,0:T(8,128)(2,1)S(1)}, u32[]{:S(2)}, u32[]{:S(2)}) collective-permute-start(bf16[1024,768]{1,0:T(8,128)(2,1)} %collective-permute-done.39.refs_3_.refs_5_), channel_id=1, source_target_pairs={{0,1},{1,2},{2,3},{4,5},{5,6},{6,7},{8,9},{9,10},{10,11},{12,13},{... | collective-permute-start | bytes 4718600 | tf_op jit(solution)/shard_map/ppermute | solution.py:1157
  439.8 35.8 %collective-permute-start.56 = (bf16[1024,768]{1,0:T(8,128)(2,1)}, bf16[1024,768]{1,0:T(8,128)(2,1)S(1)}, u32[]{:S(2)}, u32[]{:S(2)}) collective-permute-start(bf16[1024,768]{1,0:T(8,128)(2,1)} %copy-done.12), channel_id=1, source_target_pairs={{1,0},{2,1},{3,2},{5,4},{6,5},{7,6},{9,8},{10,9},{11,10},{13,12},{... | collective-permute-start | bytes 4718600 | tf_op jit(solution)/shard_map/ppermute | solution.py:1157
  (84 other events, 781.8 us)
Sparse Core Ops, SparseCore 0:
  11.5 87.7 all-gather.7
  101.7 35.8 all-gather.9
  141.2 130.2 all-gather.5
  274.9 110.3 reduce-scatter.1

commit v4 on v3

--- a/solution.py
+++ b/solution.py
@@ -738,7 +738,7 @@
     count = plan.groups - 1
     unit_own, unit_ring, refs = refs[0], refs[1 : plan.groups], refs[plan.groups :]
     left, right, head_ring, refs = refs[0], refs[1], refs[2 : 2 + count], refs[2 + count :]
-    unit_sum, head_sum, second, squares = refs
+    unit_sum, head_sum, second, squares, ends = refs
     tall = unit_sum.shape[0]
     extra = unit_own.shape[1] - tall
     for m in range(plan.groups):
@@ -746,6 +746,14 @@
     total = unit_own[0, :tall].astype(FULL)
     for member in unit_ring:
         total = total + member[...].astype(FULL)
+    tail = slice(2 * padded(plan.rows), tall)
+    ends[info[plan.mp_at]] = unit_own[0, tail].astype(FULL)
+    for at, member in enumerate(unit_ring):
+        ends[info[plan.mp_at + plan.groups - 1 - at]] = member[tail, :].astype(FULL)
+    found = ends[0]
+    for at in range(1, plan.groups):
+        found = found + ends[at]
+    total = jnp.concatenate([total[: 2 * padded(plan.rows)], found], axis=0)
     unit_sum[...] = total
     heads = left[0].astype(FULL) + right[0].astype(FULL)
     for member in head_ring:
@@ -1107,7 +1115,7 @@
             (WHOLE, shape(extra, unit_own.shape[2], kind=FULL)),
             (WHOLE, shape(8, LANES, kind=FULL)),
         ],
-        [],
+        [pltpu.VMEM((plan.groups, unit_ring[0].shape[0] - 2 * padded(plan.rows), unit_own.shape[2]), FULL)],
         4,
         info,
         (unit_own, *unit_ring, *head_own, *head_ring),
@@ -1395,8 +1403,14 @@
     head_ring = [
         ahead(tie(add(*term), *grad_line[1]), -at - 1) for at, term in enumerate(terms)
     ]
+    tall = unit_rows(own_plan, width)
+    line = lax.broadcasted_iota(jnp.int32, (tall, width), 0) - 2 * step
+    lane = lax.broadcasted_iota(jnp.int32, (tall, width), 1)
+    shared = (line >= 0) & (line < 8) & ~((line >= 6) & (lane < LANES))
     unit_ring = [
-        ahead(tie(unit_terms[at, : unit_rows(own_plan, width)], *grad_line[1]), -at)
+        ahead(
+            tie(jnp.where(shared, unit_terms[0, :tall], unit_terms[at, :tall]), *grad_line[1]), -at
+        )
         for at in range(1, groups)
     ]
     unit_sum, head_sum, second_sum, squares = collect(

time: 495 us -> 496 us (level)
  waiting for transfers between devices: 163 us -> 168 us
where the time goes in v4:
time: 496 us; the launch traced here: 489 us
  Pallas kernels  186 us (38%)
  waiting for transfers between devices  168 us (34%)
  starting transfers between devices  94.9 us (19%)
  local copies, waits for them, and re-layouts  17.2 us (3%)
  between operations  14.9 us (3%)
  other arithmetic  8.73 us (2%)
    pallas_call x19, Pallas kernels, run(): pl.pallas_call(kernel, grid_spec=pltpu.PrefetchScalarGridSpec(num_scalar_...  186 us
    ppermute x27, waiting for transfers between devices, ahead(): lax.ppermute(value, 'mp', [(i, (i + step) % size) for i in range(size)])  74.9 us
    ppermute x27, waiting for transfers between devices, swap(): lax.ppermute(value, axis, [(i, i ^ bit) for i in range(lax.axis_size(axis...  50.8 us
    ppermute x27, starting transfers between devices, ahead(): lax.ppermute(value, 'mp', [(i, (i + step) % size) for i in range(size)])  47.4 us
    ppermute x6, waiting for transfers between devices, onward(): lax.ppermute(value, 'mp', [(i, i + step) for i in range(size) if 0 <= i +...  36.2 us
    ppermute x27, starting transfers between devices, swap(): lax.ppermute(value, axis, [(i, i ^ bit) for i in range(lax.axis_size(axis...  31.4 us
    ppermute x6, starting transfers between devices, onward(): lax.ppermute(value, 'mp', [(i, i + step) for i in range(size) if 0 <= i +...  15.9 us
    unnamed x94, local copies, waits for them, and re-layouts  14.2 us
  transfers between devices with their start and end apart: 64, of which 38 were waited for; matrix products, arithmetic and copies ran while one was open for 3% of the time, Pallas kernels for 36%

profile of v4, /device:TPU:0, one launch (start us, length us, event | category | flops | bytes accessed | tf_op | source)
XLA Modules:
  0.0 489.0 jit_solution(6600810671213144773)
XLA Ops:
  42.6 5.9 %collective-permute-start.16 = (bf16[96,768]{1,0:T(8,128)(2,1)}, bf16[96,768]{1,0:T(8,128)(2,1)S(1)}, u32[]{:S(2)}, u32[]{:S(2)}) collective-permute-start(bf16[96,768]{1,0:T(8,128)(2,1)} %shard_map.292), channel_id=1, source_target_pairs={{0,2},{1,3},{2,0},{3,1},{4,6},{5,7},{6,4},{7,5},{8,10},{9,11},{10,... | collective-permute-start | bytes 442376 | tf_op jit(solution)/shard_map/ppermute | solution.py:1160
  49.0 8.8 %collective-permute-done.16 = bf16[96,768]{1,0:T(8,128)(2,1)S(1)} collective-permute-done((bf16[96,768]{1,0:T(8,128)(2,1)}, bf16[96,768]{1,0:T(8,128)(2,1)S(1)}, u32[]{:S(2)}, u32[]{:S(2)}) %collective-permute-start.16) | collective-permute-done | bytes 147488 | tf_op jit(solution)/shard_map/ppermute | solution.py:1160
  59.3 5.3 %collective-permute-start.11 = (bf16[96,768]{1,0:T(8,128)(2,1)}, bf16[96,768]{1,0:T(8,128)(2,1)S(1)}, u32[]{:S(2)}, u32[]{:S(2)}) collective-permute-start(bf16[96,768]{1,0:T(8,128)(2,1)} %shard_map.292), channel_id=1, source_target_pairs={{0,1},{1,2},{2,3},{3,0},{4,5},{5,6},{6,7},{7,4},{8,9},{9,10},{10,1... | collective-permute-start | bytes 442376 | tf_op jit(solution)/shard_map/ppermute | solution.py:1160
  72.6 14.2 %collective-permute-done.12 = bf16[1,2,96,768]{3,2,1,0:T(8,128)(2,1)S(1)} collective-permute-done((bf16[1,2,96,768]{3,2,1,0:T(8,128)(2,1)S(1)}, bf16[1,2,96,768]{3,2,1,0:T(8,128)(2,1)S(1)}, u32[]{:S(2)}, u32[]{:S(2)}) %collective-permute-start.12) | collective-permute-done | bytes 294944 | tf_op jit(solution)/shard_map/ppermute | solution.py:1155
  92.3 17.9 %shard_map.290 = (bf16[1024,2304]{1,0:T(8,128)(2,1)}, bf16[1024,768]{1,0:T(8,128)(2,1)}, bf16[1024,1536]{1,0:T(8,128)(2,1)}, bf16[768,2304]{1,0:T(8,128)(2,1)}, ...) custom-call(s32[20]{0:T(128)} %pad_add_fusion.info, bf16[4096,768]{1,0:T(8,128)(2,1)} %tok.5, ...), custom_call_target="tpu_custom_call" | custom-call | flops 20700000256 | bytes 1024 | tf_op jit(solution)/shard_map/pallas_call | solution.py:827
  115.7 25.5 %shard_map.293 = (f32[1024,768]{1,0:T(8,128)}, bf16[1024,768]{1,0:T(8,128)(2,1)}, bf16[1024,3072]{1,0:T(8,128)(2,1)}, f32[1024,768]{1,0:T(8,128)}, bf16[1024,768...) custom-call(s32[20]{0:T(128)} %pad_add_fusion.info, bf16[4096,768]{1,0:T(8,128)(2,1)} %tok.5, ...), custom_call_target="tpu_custom_call" | custom-call | flops 27599998976 | bytes 1024 | tf_op jit(solution)/shard_map/pallas_call | solution.py:827
  184.4 5.0 %shard_map.297 = (bf16[32,768]{1,0:T(8,128)(2,1)}, f32[32,768]{1,0:T(8,128)}, f32[32,768]{1,0:T(8,128)}, bf16[32,768]{1,0:T(8,128)(2,1)}, bf16[32,768]{1,0:T(8,1...) custom-call(s32[20]{0:T(128)} %pad_add_fusion.info, bf16[32,768]{1,0:T(8,128)(2,1)} %get-tuple-element.136.refs_0_, ...), custom_call_target="tpu_custom_call" | custom-call | flops 5750000128 | bytes 1024 | tf_op jit(solution)/shard_map/pallas_call | solution.py:827
  202.3 5.1 %shard_map.299 = (bf16[32,768]{1,0:T(8,128)(2,1)}, f32[32,768]{1,0:T(8,128)}, bf16[32,768]{1,0:T(8,128)(2,1)}, bf16[32,640]{1,0:T(8,128)(2,1)}, f32[8,768]{1,0:T(8,128)}) custom-call(s32[20]{0:T(128)} %pad_add_fusion.info, bf16[32,768]{1,0:T(8,128)(2,1)} %get-tuple-element.141.refs_0_, bf16[32,768]{1,0:T(8,128)(2,1)} %copy-done.31, ...), custom_call_target="tpu_custom_call" | custom-call | flops 5750000128 | bytes 1024 | tf_op jit(solution)/shard_map/pallas_call | solution.py:827
  215.1 6.5 %collective-permute-done.35.refs_2_ = bf16[32,768]{1,0:T(8,128)(2,1)S(1)} collective-permute-done((bf16[32,768]{1,0:T(8,128)(2,1)}, bf16[32,768]{1,0:T(8,128)(2,1)S(1)}, u32[]{:S(2)}, u32[]{:S(2)}) %collective-permute-start.35) | collective-permute-done | bytes 49184 | tf_op jit(solution)/shard_map/ppermute | solution.py:1160
  222.3 28.5 %shard_map.300 = (f32[1024,768]{1,0:T(8,128)}, bf16[1024,3072]{1,0:T(8,128)(2,1)}, bf16[1024,3072]{1,0:T(8,128)(2,1)}, bf16[1024,768]{1,0:T(8,128)(2,1)}, bf16[1...) custom-call(s32[20]{0:T(128)} %pad_add_fusion.info, bf16[4096,768]{1,0:T(8,128)(2,1)} %cot.1, ...), custom_call_target="tpu_custom_call" | custom-call | flops 32199999488 | bytes 1024 | tf_op jit(solution)/shard_map/pallas_call | solution.py:827
  250.8 20.5 %shard_map.301.early = bf16[8,4,304,768]{3,2,1,0:T(8,128)(2,1)} custom-call(s32[20]{0:T(128)} %pad_add_fusion.info, bf16[1024,3072]{1,0:T(8,128)(2,1)} %get-tuple-element.156.active, bf16[1024,768]{1,0:T(8,128)(2,1)} %get-tuple-element.157.grad_ret, bf16[1024,768]{1,0:T(8,128)(2,1)} %get-tuple-element.158.hid_low, ...), custom_call_target="tpu_custom_call" | custom-call | flops 21849999360 | bytes 1024 | tf_op jit(solution)/shard_map/pallas_call | solution.py:827
  272.8 24.9 %shard_map.302 = (bf16[1024,768]{1,0:T(8,128)(2,1)}, bf16[1024,2304]{1,0:T(8,128)(2,1)}) custom-call(s32[20]{0:T(128)} %pad_add_fusion.info, f32[1024,768]{1,0:T(8,128)} %get-tuple-element.150.grad_resid, bf16[1024,768]{1,0:T(8,128)(2,1)} %get-tuple-element.151.grad_mixed, bf16[1024,2304]{1,0:T(8,128)(2,1)} %get-tuple-element.152.triple, ...), custom_call_target="tpu_custom_call" | custom-call | flops 34500001792 | bytes 1024 | tf_op jit(solution)/shard_map/pallas_call | solution.py:827
  303.8 7.2 %shard_map.298 = bf16[4096,768]{1,0:T(8,128)(2,1)} custom-call(s32[20]{0:T(128)} %pad_add_fusion.info, f32[32,768]{1,0:T(8,128)} %broadcast_multiply_fusion.tops, bf16[4096,768]{1,0:T(8,128)(2,1)} %all-gather.6.cloned.1.call-done.rows), custom_call_target="tpu_custom_call" | custom-call | flops 4600000000 | bytes 1024 | tf_op jit(solution)/shard_map/pallas_call | solution.py:827
  311.0 10.1 %shard_map.303 = (bf16[4,2,96,640]{3,2,1,0:T(8,128)(2,1)}, bf16[4,2,96,640]{3,2,1,0:T(8,128)(2,1)}, bf16[4,2,96,640]{3,2,1,0:T(8,128)(2,1)}, bf16[4,2,96,640]{3,2,1,0:T(8,128)(2,1)}) custom-call(s32[20]{0:T(128)} %pad_add_fusion.info, bf16[4096,768]{1,0:T(8,128)(2,1)} %tok.5, bf16[1024,2304]{1,0:T(8,128)(2,1)} %get-tuple-element.175.grad_triple, ...), custom_call_target="tpu_custom_call" | custom-call | flops 11500000256 | bytes 1024 | tf_op jit(solution)/shard_map/pallas_call | solution.py:827
  321.6 13.8 %collective-permute-done.37.refs_1_ = bf16[1024,768]{1,0:T(8,128)(2,1)S(1)} collective-permute-done((bf16[1024,768]{1,0:T(8,128)(2,1)}, bf16[1024,768]{1,0:T(8,128)(2,1)S(1)}, u32[]{:S(2)}, u32[]{:S(2)}) %collective-permute-start.37) | collective-permute-done | bytes 1572896 | tf_op jit(solution)/shard_map/ppermute | solution.py:1165
  348.1 9.2 %collective-permute-done.49 = bf16[2,2,96,640]{3,2,1,0:T(8,128)(2,1)S(1)} collective-permute-done((bf16[2,2,96,640]{3,2,1,0:T(8,128)(2,1)S(1)}, bf16[2,2,96,640]{3,2,1,0:T(8,128)(2,1)S(1)}, u32[]{:S(2)}, u32[]{:S(2)}) %collective-permute-start.49) | collective-permute-done | bytes 491552 | tf_op jit(solution)/shard_map/ppermute | solution.py:1155
  359.7 10.3 %collective-permute-done.50 = bf16[1,2,96,640]{3,2,1,0:T(8,128)(2,1)S(1)} collective-permute-done((bf16[1,2,96,640]{3,2,1,0:T(8,128)(2,1)S(1)}, bf16[1,2,96,640]{3,2,1,0:T(8,128)(2,1)S(1)}, u32[]{:S(2)}, u32[]{:S(2)}) %collective-permute-start.50) | collective-permute-done | bytes 245792 | tf_op jit(solution)/shard_map/ppermute | solution.py:1155
  373.5 5.5 %collective-permute-done.40.refs_4_ = bf16[1024,768]{1,0:T(8,128)(2,1)S(1)} collective-permute-done((bf16[1024,768]{1,0:T(8,128)(2,1)}, bf16[1024,768]{1,0:T(8,128)(2,1)S(1)}, u32[]{:S(2)}, u32[]{:S(2)}) %collective-permute-start.40) | collective-permute-done | bytes 1572896 | tf_op jit(solution)/shard_map/ppermute | solution.py:1165
  380.2 5.6 %reduce-scatter.2.cloned.1.call-done = bf16[1,4,304,768]{3,2,1,0:T(8,128)(2,1)} async-done(((bf16[8,4,304,768]{3,2,1,0:T(8,128)(2,1)}), bf16[1,4,304,768]{3,2,1,0:T(8,128)(2,1)}) %reduce-scatter.2.cloned.1.call-update) | async-done | bytes 1867792 | tf_op jit(solution)/shard_map/reduce_scatter | solution.py:1389
  393.6 23.1 %collective-permute-done.47.refs_6_ = bf16[96,640]{1,0:T(8,128)(2,1)S(1)} collective-permute-done((bf16[96,640]{1,0:T(8,128)(2,1)S(1)}, bf16[96,640]{1,0:T(8,128)(2,1)S(1)}, u32[]{:S(2)}, u32[]{:S(2)}) %collective-permute-start.47) | collective-permute-done | bytes 122912 | tf_op jit(solution)/shard_map/ppermute | solution.py:1160
  422.0 8.0 %collective-permute-start.53 = (f32[8,128]{1,0:T(8,128)}, f32[8,128]{1,0:T(8,128)S(1)}, u32[]{:S(2)}, u32[]{:S(2)}) collective-permute-start(f32[8,128]{1,0:T(8,128)} %get-tuple-element.190), channel_id=1, source_target_pairs={{0,1},{1,0},{2,3},{3,2},{4,5},{5,4},{6,7},{7,6},{8,9},{9,8},{10,11... | collective-permute-start | bytes 12296 | tf_op jit(solution)/shard_map/ppermute | solution.py:1155
  448.3 6.1 %shard_map.305.refs_2_ = f32[4096,768]{1,0:T(8,128)} custom-call(s32[20]{0:T(128)} %pad_add_fusion.info, bf16[1024,768]{1,0:T(8,128)(2,1)} %get-tuple-element.173.refs_0_, bf16[1024,768]{1,0:T(8,128)(2,1)} %copy-done.13, bf16[1024,768]{1,0:T(8,128)(2,1)} %collective-permute-done.38.refs_2_, bf16[1024,768]{1,0:T(8,128)(2,1)} %collective-permute-done.39.refs_3_.refs_5_, ...), custom_call_target="tpu_custom_call" | custom-call | flops 6899999744 | bytes 1024 | tf_op jit(solution)/shard_map/pallas_call | solution.py:827
  455.0 7.5 %shard_map.307 = (f32[2,96,576]{2,1,0:T(8,128)}, f32[2,24,768]{2,1,0:T(8,128)}, f32[2,96,768]{2,1,0:T(8,128)}, f32[2,96]{1,0:T(2,128)}, f32[2,96,768]{2,1,0:T(8,...) custom-call(s32[20]{0:T(128)} %pad_add_fusion.info, ...), custom_call_target="tpu_custom_call" | custom-call | flops 8049999872 | bytes 1024 | tf_op jit(solution)/shard_map/pallas_call | solution.py:827
  467.6 5.2 %collective-permute-done.55.refs_0_ = bf16[1024,768]{1,0:T(8,128)(2,1)S(1)} collective-permute-done((bf16[1024,768]{1,0:T(8,128)(2,1)}, bf16[1024,768]{1,0:T(8,128)(2,1)S(1)}, u32[]{:S(2)}, u32[]{:S(2)}) %collective-permute-start.55) | collective-permute-done | bytes 1572896 | tf_op jit(solution)/shard_map/ppermute | solution.py:1165
  (253 shorter events, 194.5 us)
Async XLA Ops:
  7.2 108.5 %all-gather.8.cloned.1.call-start = ((), (), s32[]{:S(2)}) async-start(), calls=%async_computation.3 | async-start | bytes 6488064 | tf_op jit(solution)/shard_map/all_gather | solution.py:1306
  11.1 135.0 %all-gather.10.cloned.1.call-start = ((), (), s32[]{:S(2)}) async-start(), calls=%async_computation.4 | async-start | bytes 4423680 | tf_op jit(solution)/shard_map/all_gather | solution.py:1310
  23.0 280.8 %all-gather.6.cloned.1.call-start = ((), (), s32[]{:S(2)}) async-start(), calls=%async_computation.1 | async-start | bytes 7864320 | tf_op jit(solution)/shard_map/all_gather | solution.py:1361
  32.7 26.5 %collective-permute-start.9 = (bf16[2,2,96,640]{3,2,1,0:T(8,128)(2,1)S(1)}, bf16[2,2,96,640]{3,2,1,0:T(8,128)(2,1)S(1)}, u32[]{:S(2)}, u32[]{:S(2)}) collective-permute-start(bf16[2,2,96,640]{3,2,1,0:T(8,128)(2,1)S(1)} %pad_maximum_fusion.1.refs_4_), channel_id=1, source_target_pairs={{0,8},{4,12},{8,0},{12,4},{16,24},{20,28},{24,16},{28,20},{1,9},{5... | collective-permute-start | bytes 1474568 | tf_op jit(solution)/shard_map/ppermute | solution.py:1155
  64.7 23.9 %collective-permute-start.8 = (bf16[2,2,96,640]{3,2,1,0:T(8,128)(2,1)S(1)}, bf16[2,2,96,640]{3,2,1,0:T(8,128)(2,1)}, u32[]{:S(2)}, u32[]{:S(2)}) collective-permute-start(bf16[2,2,96,640]{3,2,1,0:T(8,128)(2,1)S(1)} %pad_maximum_fusion.1.refs_4_), channel_id=1, source_target_pairs={{0,4},{4,0},{8,12},{12,8},{16,20},{20,16},{24,28},{28,24},{1,5},{5... | collective-permute-start | bytes 1474568 | tf_op jit(solution)/shard_map/ppermute | solution.py:1155
  64.7 26.0 %collective-permute-start.2 = (bf16[2,2,96,640]{3,2,1,0:T(8,128)(2,1)S(1)}, bf16[2,2,96,640]{3,2,1,0:T(8,128)(2,1)S(1)}, u32[]{:S(2)}, u32[]{:S(2)}) collective-permute-start(bf16[2,2,96,640]{3,2,1,0:T(8,128)(2,1)S(1)} %pad_maximum_fusion.refs_0_), channel_id=1, source_target_pairs={{0,4},{4,0},{8,12},{12,8},{16,20},{20,16},{24,28},{28,24},{1,5},{5... | collective-permute-start | bytes 1474568 | tf_op jit(solution)/shard_map/ppermute | solution.py:1155
  65.2 25.5 %collective-permute-start.10 = (bf16[2,2,96,640]{3,2,1,0:T(8,128)(2,1)S(1)}, bf16[2,2,96,640]{3,2,1,0:T(8,128)(2,1)S(1)}, u32[]{:S(2)}, u32[]{:S(2)}) collective-permute-start(bf16[2,2,96,640]{3,2,1,0:T(8,128)(2,1)S(1)} %collective-permute-done.9.refs_6_), channel_id=1, source_target_pairs={{0,4},{4,0},{8,12},{12,8},{16,20},{20,16},{24,28},{28,24},{1,5},{5... | collective-permute-start | bytes 1474568 | tf_op jit(solution)/shard_map/ppermute | solution.py:1155
  69.8 22.5 %collective-permute-start.4 = (bf16[2,2,96,640]{3,2,1,0:T(8,128)(2,1)}, bf16[2,2,96,640]{3,2,1,0:T(8,128)(2,1)}, u32[]{:S(2)}, u32[]{:S(2)}) collective-permute-start(bf16[2,2,96,640]{3,2,1,0:T(8,128)(2,1)} %collective-permute-done.3.refs_2_), channel_id=1, source_target_pairs={{0,4},{4,0},{8,12},{12,8},{16,20},{20,16},{24,28},{28,24},{1,5},{5... | collective-permute-start | bytes 1474568 | tf_op jit(solution)/shard_map/ppermute | solution.py:1155
  86.8 24.0 %collective-permute-start.20 = (bf16[2,2,96,768]{3,2,1,0:T(8,128)(2,1)S(1)}, bf16[2,2,96,768]{3,2,1,0:T(8,128)(2,1)S(1)}, u32[]{:S(2)}, u32[]{:S(2)}) collective-permute-start(bf16[2,2,96,768]{3,2,1,0:T(8,128)(2,1)S(1)} %constant_dynamic-update-slice_fusion.2.refs_4_.refs_8_), channel_id=1, source_target_pairs={{0,8},{4,12},{8,0},{12,4},{16,24},{20,28},{24,16},{28,20},{1,9},{5... | collective-permute-start | bytes 1769480 | tf_op jit(solution)/shard_map/ppermute | solution.py:1155
  88.6 22.3 %collective-permute-start.14 = (bf16[2,2,96,768]{3,2,1,0:T(8,128)(2,1)S(1)}, bf16[2,2,96,768]{3,2,1,0:T(8,128)(2,1)S(1)}, u32[]{:S(2)}, u32[]{:S(2)}) collective-permute-start(bf16[2,2,96,768]{3,2,1,0:T(8,128)(2,1)S(1)} %constant_dynamic-update-slice_fusion.refs_0_.refs_4_), channel_id=1, source_target_pairs={{0,16},{4,20},{8,24},{12,28},{16,0},{20,4},{24,8},{28,12},{1,17},{... | collective-permute-start | bytes 1769480 | tf_op jit(solution)/shard_map/ppermute | solution.py:1155
  141.2 244.5 %reduce-scatter.2.cloned.1.call-start = ((), (), s32[]{:S(2)}) async-start(), calls=%async_computation.2 | async-start | bytes 16809984 | tf_op jit(solution)/shard_map/reduce_scatter | solution.py:1389
  297.7 37.7 %collective-permute-start.37 = (bf16[1024,768]{1,0:T(8,128)(2,1)}, bf16[1024,768]{1,0:T(8,128)(2,1)S(1)}, u32[]{:S(2)}, u32[]{:S(2)}) collective-permute-start(bf16[1024,768]{1,0:T(8,128)(2,1)} %get-tuple-element.173.refs_0_), channel_id=1, source_target_pairs={{0,1},{1,2},{2,3},{4,5},{5,6},{6,7},{8,9},{9,10},{10,11},{12,13},{... | collective-permute-start | bytes 4718600 | tf_op jit(solution)/shard_map/ppermute | solution.py:1165
  302.5 37.1 %collective-permute-start.38 = (bf16[1024,768]{1,0:T(8,128)(2,1)}, bf16[1024,768]{1,0:T(8,128)(2,1)}, u32[]{:S(2)}, u32[]{:S(2)}) collective-permute-start(bf16[1024,768]{1,0:T(8,128)(2,1)} %get-tuple-element.173.refs_0_), channel_id=1, source_target_pairs={{1,0},{2,1},{3,2},{5,4},{6,5},{7,6},{9,8},{10,9},{11,10},{13,12},{... | collective-permute-start | bytes 4718600 | tf_op jit(solution)/shard_map/ppermute | solution.py:1165
  321.1 23.1 %collective-permute-start.48 = (bf16[4,2,96,640]{3,2,1,0:T(8,128)(2,1)}, bf16[4,2,96,640]{3,2,1,0:T(8,128)(2,1)S(1)}, u32[]{:S(2)}, u32[]{:S(2)}) collective-permute-start(bf16[4,2,96,640]{3,2,1,0:T(8,128)(2,1)} %get-tuple-element.186), channel_id=1, source_target_pairs={{0,4},{4,0},{8,12},{12,8},{16,20},{20,16},{24,28},{28,24},{1,5},{5... | collective-permute-start | bytes 2949128 | tf_op jit(solution)/shard_map/ppermute | solution.py:1155
  321.1 25.1 %collective-permute-start.44 = (bf16[4,2,96,640]{3,2,1,0:T(8,128)(2,1)}, bf16[4,2,96,640]{3,2,1,0:T(8,128)(2,1)S(1)}, u32[]{:S(2)}, u32[]{:S(2)}) collective-permute-start(bf16[4,2,96,640]{3,2,1,0:T(8,128)(2,1)} %get-tuple-element.182), channel_id=1, source_target_pairs={{0,4},{4,0},{8,12},{12,8},{16,20},{20,16},{24,28},{28,24},{1,5},{5... | collective-permute-start | bytes 2949128 | tf_op jit(solution)/shard_map/ppermute | solution.py:1155
  339.6 33.9 %collective-permute-start.39 = (bf16[1024,768]{1,0:T(8,128)(2,1)S(1)}, bf16[1024,768]{1,0:T(8,128)(2,1)}, u32[]{:S(2)}, u32[]{:S(2)}) collective-permute-start(bf16[1024,768]{1,0:T(8,128)(2,1)S(1)} %collective-permute-done.37.refs_1_), channel_id=1, source_target_pairs={{0,1},{1,2},{2,3},{4,5},{5,6},{6,7},{8,9},{9,10},{10,11},{12,13},{... | collective-permute-start | bytes 4718600 | tf_op jit(solution)/shard_map/ppermute | solution.py:1165
  342.9 36.1 %collective-permute-start.40 = (bf16[1024,768]{1,0:T(8,128)(2,1)}, bf16[1024,768]{1,0:T(8,128)(2,1)S(1)}, u32[]{:S(2)}, u32[]{:S(2)}) collective-permute-start(bf16[1024,768]{1,0:T(8,128)(2,1)} %collective-permute-done.38.refs_2_), channel_id=1, source_target_pairs={{1,0},{2,1},{3,2},{5,4},{6,5},{7,6},{9,8},{10,9},{11,10},{13,12},{... | collective-permute-start | bytes 4718600 | tf_op jit(solution)/shard_map/ppermute | solution.py:1165
  359.1 32.7 %collective-permute-start.46 = (bf16[1,2,96,640]{3,2,1,0:T(8,128)(2,1)S(1)}, bf16[1,2,96,640]{3,2,1,0:T(8,128)(2,1)S(1)}, u32[]{:S(2)}, u32[]{:S(2)}) collective-permute-start(bf16[1,2,96,640]{3,2,1,0:T(8,128)(2,1)S(1)} %get-tuple-element.275), channel_id=1, source_target_pairs={{0,16},{4,20},{8,24},{12,28},{16,0},{20,4},{24,8},{28,12},{1,17},{... | collective-permute-start | bytes 737288 | tf_op jit(solution)/shard_map/ppermute | solution.py:1155
  387.4 29.3 %collective-permute-start.43 = (bf16[224,768]{1,0:T(8,128)(2,1)S(1)}, bf16[224,768]{1,0:T(8,128)(2,1)S(1)}, u32[]{:S(2)}, u32[]{:S(2)}) collective-permute-start(bf16[224,768]{1,0:T(8,128)(2,1)S(1)} %get-tuple-element.181), channel_id=1, source_target_pairs={{0,1},{1,2},{2,3},{3,0},{4,5},{5,6},{6,7},{7,4},{8,9},{9,10},{10,1... | collective-permute-start | bytes 1032200 | tf_op jit(solution)/shard_map/ppermute | solution.py:1160
  389.1 27.6 %collective-permute-start.42 = (bf16[224,768]{1,0:T(8,128)(2,1)S(1)}, bf16[224,768]{1,0:T(8,128)(2,1)S(1)}, u32[]{:S(2)}, u32[]{:S(2)}) collective-permute-start(bf16[224,768]{1,0:T(8,128)(2,1)S(1)} %get-tuple-element.180), channel_id=1, source_target_pairs={{0,2},{1,3},{2,0},{3,1},{4,6},{5,7},{6,4},{7,5},{8,10},{9,11},{10,... | collective-permute-start | bytes 1032200 | tf_op jit(solution)/shard_map/ppermute | solution.py:1160
  391.8 24.9 %collective-permute-start.41 = (bf16[224,768]{1,0:T(8,128)(2,1)S(1)}, bf16[224,768]{1,0:T(8,128)(2,1)S(1)}, u32[]{:S(2)}, u32[]{:S(2)}) collective-permute-start(bf16[224,768]{1,0:T(8,128)(2,1)S(1)} %get-tuple-element.179), channel_id=1, source_target_pairs={{0,3},{1,0},{2,1},{3,2},{4,7},{5,4},{6,5},{7,6},{8,11},{9,8},{10,9... | collective-permute-start | bytes 1032200 | tf_op jit(solution)/shard_map/ppermute | solution.py:1160
  393.3 23.4 %collective-permute-start.47 = (bf16[96,640]{1,0:T(8,128)(2,1)S(1)}, bf16[96,640]{1,0:T(8,128)(2,1)S(1)}, u32[]{:S(2)}, u32[]{:S(2)}) collective-permute-start(bf16[96,640]{1,0:T(8,128)(2,1)S(1)} %fusion.3), channel_id=1, source_target_pairs={{0,3},{1,0},{2,1},{3,2},{4,7},{5,4},{6,5},{7,6},{8,11},{9,8},{10,9... | collective-permute-start | bytes 368648 | tf_op jit(solution)/shard_map/ppermute | solution.py:1160
  437.0 35.8 %collective-permute-start.55 = (bf16[1024,768]{1,0:T(8,128)(2,1)}, bf16[1024,768]{1,0:T(8,128)(2,1)S(1)}, u32[]{:S(2)}, u32[]{:S(2)}) collective-permute-start(bf16[1024,768]{1,0:T(8,128)(2,1)} %collective-permute-done.39.refs_3_.refs_5_), channel_id=1, source_target_pairs={{0,1},{1,2},{2,3},{4,5},{5,6},{6,7},{8,9},{9,10},{10,11},{12,13},{... | collective-permute-start | bytes 4718600 | tf_op jit(solution)/shard_map/ppermute | solution.py:1165
  441.0 35.8 %collective-permute-start.56 = (bf16[1024,768]{1,0:T(8,128)(2,1)}, bf16[1024,768]{1,0:T(8,128)(2,1)S(1)}, u32[]{:S(2)}, u32[]{:S(2)}) collective-permute-start(bf16[1024,768]{1,0:T(8,128)(2,1)} %copy-done.12), channel_id=1, source_target_pairs={{1,0},{2,1},{3,2},{5,4},{6,5},{7,6},{9,8},{10,9},{11,10},{13,12},{... | collective-permute-start | bytes 4718600 | tf_op jit(solution)/shard_map/ppermute | solution.py:1165
  (84 other events, 787.6 us)
Sparse Core Ops, SparseCore 0:
  11.5 87.7 all-gather.7
  101.7 35.8 all-gather.9
  141.4 130.2 all-gather.5
  275.1 110.6 reduce-scatter.1
